TPU v7x, 32 devices: a whole 2x2x4 slice. The times are simulated.
32 devices in a mesh: section: 2 (over core), dp: 4 (over y, x), mp: 4 (over z).
Axes of the slice: x: 2, y: 2, z: 4, core: 2. Of those that a mesh axis runs over, the one named last changes fastest.
Arguments:
- hidden_in: bfloat16 [2, 384, 8192], P('section', 'dp', 'mp'), may hold values from -6 to 6
- layer_gain: float32 [1, 2, 8192], P(None, 'section'), may hold values from 0.5 to 1.5
- gate_proj: bfloat16 [1, 2, 8192, 16384], P(None, 'section', 'dp', 'mp'), may hold values from -0.0625 to 0.0625
- up_proj: bfloat16 [1, 2, 8192, 16384], P(None, 'section', 'dp', 'mp'), may hold values from -0.0625 to 0.0625
- down_proj: bfloat16 [1, 2, 16384, 8192], P(None, 'section', 'mp', 'dp'), may hold values from -0.046875 to 0.046875
- final_gain: float32 [8192], P('mp'), may hold values from 0.5 to 1.5
- teacher_rows: bfloat16 [2, 4, 192, 8192], P('section', 'dp', None, 'mp'), may hold values from -6 to 6
- send_counts: int32 [2, 4, 4], P('section', 'dp'), may hold values from 0 to 48, as said below
- doc_ids: int32 [2, 4, 96], P('section', 'dp'), may hold values from 0 to 7, never falling along the last dimension, each value on 1 to 24 neighbouring positions
Outputs:
- d_hidden: float32 [2, 384, 8192], P('section', 'dp', 'mp')
- doc_loss: float32 [2, 4], P('section', 'dp')
Inputs may be any that keep to these rules, and one draw needn't show every extreme that they name: For every micro-batch m and data group p the counts send_counts[m, q, p] over the 4 teacher shards q sum to exactly 96; in every such column some count equals 48. `doc_ids`: within each micro-batch of each data group the ids never fall, all 8 documents occur, each with 1 to 24 tokens, and one has exactly 24.
All inputs are finite; a program needn't handle non-finite values.
Results may differ from a plain program's by a relative error of at most 0.02.
Values may be sent and summed in bfloat16 or wider, within the bound.
No kernel may reach another device: no remote copies, remote signals or barrier semaphores. Data moves between devices by JAX's collectives and lax.ppermute only.
A program may use at most 320 MiB of HBM per device.

v0:
```python
import jax
import jax.numpy as jnp
from jax import lax
from jax.sharding import PartitionSpec as P

D = 8192
DOCS = 8


EPSILON = 1e-05


def from_behind(value, axis, steps):
    count = lax.axis_size(axis)
    pairs = [(source, (source + steps) % count) for source in range(count)]
    return lax.ppermute(value, axis, pairs)


def widen_rows(carried, gain_row):
    full = lax.all_gather(carried, "mp", axis=1, tiled=True)
    wide_rows = full.astype(jnp.float32)
    scale = lax.rsqrt(jnp.mean(wide_rows * wide_rows, axis=-1, keepdims=True) + EPSILON)
    return (wide_rows * scale * gain_row[None, :]).astype(jnp.bfloat16)


def finish_layer(carried, partial_value):
    summed = lax.psum_scatter(
        partial_value.astype(jnp.bfloat16), "mp", scatter_dimension=1, tiled=True
    ).astype(jnp.float32)
    return (carried.astype(jnp.float32) + summed).astype(jnp.bfloat16)


def layer_held(carried, gain_row, gate_rows, up_rows, down_rows):
    normed = widen_rows(carried, gain_row)
    gate_full = jnp.dot(normed, gate_rows, preferred_element_type=jnp.float32)
    up_full = jnp.dot(normed, up_rows, preferred_element_type=jnp.float32)
    inner = (jax.nn.silu(gate_full) * up_full).astype(jnp.bfloat16)
    partial_value = jnp.dot(inner, down_rows, preferred_element_type=jnp.float32)
    return finish_layer(carried, partial_value)


def select_repeat(array, position):
    return lax.dynamic_index_in_dim(array, position, 0, keepdims=False)


def run_layer(layer_fn, carried, tick_num, phase_pos, count_phase, repeats, weights):
    relative = tick_num - phase_pos
    repeat_pos = jnp.clip(relative // count_phase, 0, repeats - 1)
    active = (relative >= 0) & (relative < count_phase * repeats)
    gains, gate_all, up_all, down_all = weights
    fresh = layer_fn(
        carried,
        select_repeat(gains, repeat_pos),
        select_repeat(gate_all, repeat_pos),
        select_repeat(up_all, repeat_pos),
        select_repeat(down_all, repeat_pos),
    )
    return (fresh, active, repeat_pos)


def body(
    hidden_in,
    layer_gain,
    gate_proj,
    up_proj,
    down_proj,
    final_gain,
    teacher_rows,
    send_counts,
    doc_ids,
):
    count_phase = lax.axis_size("section")
    count_data = lax.axis_size("dp")
    phase_pos = lax.axis_index("section")
    repeats = gate_proj.shape[0]
    gate_all, up_all, down_all = (
        lax.all_gather(gate_proj, "dp", axis=2, tiled=True),
        lax.all_gather(up_proj, "dp", axis=2, tiled=True),
        lax.all_gather(down_proj, "dp", axis=3, tiled=True),
    )
    weights = (layer_gain[:, 0], gate_all[:, 0], up_all[:, 0], down_all[:, 0])
    own_input = hidden_in[0]
    last_layer = count_phase * repeats - 1
    carried = own_input
    buffer = own_input
    for tick_num in range(count_phase * (repeats + 1)):
        if tick_num < count_phase + last_layer:
            if tick_num < count_phase:
                carried = jnp.where(phase_pos == 0, buffer, carried)
            fresh, active, repeat_pos = run_layer(
                layer_held, carried, tick_num, phase_pos, count_phase, repeats, weights
            )
            carried = jnp.where(active, fresh, carried)
            if tick_num >= last_layer:
                finish = active & (phase_pos == count_phase - 1) & (repeat_pos == repeats - 1)
                buffer = jnp.where(finish, fresh, buffer)
        carried, buffer = from_behind((carried, buffer), "section", 1)
    token_count = own_input.shape[0]
    teacher_local = teacher_rows[0, 0].reshape(count_data, -1, teacher_rows.shape[-1])
    counts_local = send_counts[0, 0].reshape(count_data, 1).astype(jnp.bfloat16)
    arrived, arrived_counts = (
        lax.all_to_all(teacher_local, "dp", split_axis=0, concat_axis=0, tiled=True),
        lax.all_to_all(counts_local, "dp", split_axis=0, concat_axis=0, tiled=True),
    )
    per_source = arrived_counts[:, 0].astype(jnp.int32)
    end_rows = jnp.cumsum(per_source)
    starts = end_rows - per_source
    positions = jnp.arange(token_count, dtype=jnp.int32)
    source_of = jnp.sum((end_rows[None, :] <= positions[:, None]).astype(jnp.int32), axis=1)
    matching = source_of[:, None] == jnp.arange(count_data, dtype=jnp.int32)[None, :]
    first_row = jnp.sum(jnp.where(matching, starts[None, :], 0), axis=1)
    capacity = teacher_local.shape[1]
    flat_index = source_of * capacity + positions - first_row
    targets = arrived.reshape(-1, arrived.shape[-1])[flat_index].astype(jnp.float32)
    member = (doc_ids[0, 0][:, None] == jnp.arange(DOCS, dtype=jnp.int32)[None, :]).astype(
        jnp.float32
    )
    doc_sizes = jnp.sum(member, axis=0)
    row_weight = jnp.sum(member * (1.0 / doc_sizes)[None, :], axis=1)
    wide_final = buffer.astype(jnp.float32)
    gain_row = final_gain[None, :]
    squares = lax.psum(jnp.sum(wide_final * wide_final, axis=-1), "mp")
    rscale = lax.rsqrt(squares / D + EPSILON)
    normal_rows = wide_final * rscale[:, None]
    student = normal_rows * gain_row
    residual = student - targets
    d_student = row_weight[:, None] * residual
    inner_sum, errors = lax.psum(
        (
            jnp.sum(normal_rows * gain_row * d_student, axis=-1),
            jnp.sum(residual * residual, axis=-1),
        ),
        "mp",
    )
    d_hidden = rscale[:, None] * (gain_row * d_student - normal_rows * inner_sum[:, None] / D)
    doc_loss = jnp.sum(row_weight * 0.5 * errors) / (DOCS * D)
    return (d_hidden[None], doc_loss.reshape(1, 1))


def solution(mesh):
    in_specs = (
        P("section", "dp", "mp"),
        P(None, "section", None),
        P(None, "section", "dp", "mp"),
        P(None, "section", "dp", "mp"),
        P(None, "section", "mp", "dp"),
        P("mp"),
        P("section", "dp", None, "mp"),
        P("section", "dp", None),
        P("section", "dp", None),
    )
    out_specs = (P("section", "dp", "mp"), P("section", "dp"))
    return jax.shard_map(body, mesh=mesh, in_specs=in_specs, out_specs=out_specs, check_vma=False)
```

profile of v0, /device:TPU:2, one launch (start us, length us, event | category | flops | bytes accessed | tf_op | source)
XLA Modules:
  0.0 2191.6 jit_solution(13684729433509529996)
XLA Ops:
  7.2 0.0 all-gather.18.cloned.1.call-start
  7.2 0.7 all-gather.18.cloned.1.call-update
  7.9 0.0 all-gather.8.cloned.1.call-start
  7.9 0.7 all-gather.8.cloned.1.call-update
  8.6 0.0 all-gather.10.cloned.1.call-start
  8.7 0.7 all-gather.10.cloned.1.call-update
  9.4 0.0 all-gather.12.cloned.1.call-start
  9.4 0.5 all-gather.12.cloned.1.call-update
  10.0 0.0 reduce-scatter.4.cloned.1.call-start
  10.0 37.9 %all-gather.18.cloned.1.call-done = bf16[1,96,8192]{2,1,0:T(8,128)(2,1)} async-done(((bf16[1,96,2048]{2,1,0:T(8,128)(2,1)}), bf16[1,96,8192]{2,1,0:T(8,128)(2,1)}) %all-gather.18.cloned.1.call-update) | async-done | bytes 1572880 | tf_op jit(solution)/shard_map/all_gather | solution.py:20
  47.9 1.8 fusion.57
  49.8 575.7 %all-gather.8.cloned.1.call-done = bf16[1,1,8192,4096]{3,2,1,0:T(8,128)(2,1)} async-done(((bf16[1,1,2048,4096]{3,2,1,0:T(8,128)(2,1)}), bf16[1,1,8192,4096]{3,2,1,0:T(8,128)(2,1)}) %all-gather.8.cloned.1.call-update) | async-done | bytes 67108880 | tf_op jit(solution)/shard_map/all_gather | solution.py:77
  625.5 36.6 %fusion.16 = f32[96,4096]{1,0:T(8,128)S(1)} fusion(bf16[1,1,8192,4096]{3,2,1,0:T(8,128)(2,1)} %all-gather.8.cloned.1.call-done, bf16[1,96,8192]{2,1,0:T(8,128)(2,1)} %all-gather.18.cloned.1.call-done, f32[8192]{0:T(1024)S(1)} %bitcast.92, f32[96]{0:T(128)S(1)} %add_rsqrt_fusion.3), kind=kOutput, calls=%fused_computation.17 | convolution fusion | flops 6445596672 | bytes 70287744 | tf_op jit(solution)/shard_map/dot_general | solution.py:35
  662.1 542.1 %all-gather.10.cloned.1.call-done = bf16[1,1,8192,4096]{3,2,1,0:T(8,128)(2,1)} async-done(((bf16[1,1,2048,4096]{3,2,1,0:T(8,128)(2,1)}), bf16[1,1,8192,4096]{3,2,1,0:T(8,128)(2,1)}) %all-gather.10.cloned.1.call-update) | async-done | bytes 67108880 | tf_op jit(solution)/shard_map/all_gather | solution.py:78
  1204.2 36.0 %fusion.46.clone.4 = bf16[96,4096]{1,0:T(8,128)(2,1)} fusion(bf16[1,1,8192,4096]{3,2,1,0:T(8,128)(2,1)} %all-gather.10.cloned.1.call-done, f32[96,4096]{1,0:T(8,128)S(1)} %fusion.16, bf16[1,96,8192]{2,1,0:T(8,128)(2,1)S(1)} %copy-done, f32[8192]{0:T(1024)S(1)} %bitcast.93, f32[96]{0:T(128)S(1)} %add_rsqrt_fusion.3), kind=kOutput, calls=%fused_computation.27.clone.clone.clone.1 | convolution fusion | flops 6447955968 | bytes 71074176 | tf_op jit(solution)/shard_map/dot_general | solution.py:36
  1240.2 542.5 %all-gather.12.cloned.1.call-done = bf16[1,1,4096,8192]{3,2,1,0:T(8,128)(2,1)} async-done(((bf16[1,1,4096,2048]{3,2,1,0:T(8,128)(2,1)}), bf16[1,1,4096,8192]{3,2,1,0:T(8,128)(2,1)}) %all-gather.12.cloned.1.call-update) | async-done | bytes 67108880 | tf_op jit(solution)/shard_map/all_gather | solution.py:79
  1782.7 25.5 %fusion.18 = bf16[96,8192]{1,0:T(8,128)(2,1)} fusion(bf16[1,1,4096,8192]{3,2,1,0:T(8,128)(2,1)} %all-gather.12.cloned.1.call-done, bf16[96,4096]{1,0:T(8,128)(2,1)} %fusion.46.clone.4), kind=kOutput, calls=%fused_computation.19 | convolution fusion | flops 6443237376 | bytes 69468160 | tf_op jit(solution)/shard_map/dot_general | solution.py:38
  1808.3 0.0 all-gather.14.cloned.1.call-start
  1808.3 0.1 collective-permute-start
  1808.4 35.3 %reduce-scatter.4.cloned.1.call-done = bf16[96,2048]{1,0:T(8,128)(2,1)} async-done(((bf16[96,8192]{1,0:T(8,128)(2,1)}), bf16[96,2048]{1,0:T(8,128)(2,1)}) %reduce-scatter.4.cloned.1.call-update) | async-done | bytes 393232 | tf_op jit(solution)/shard_map/reduce_scatter | solution.py:27
  1843.7 1.1 fusion.88
  1844.8 0.1 collective-permute-start.1
  1844.9 1.7 collective-permute-done.1
  1846.6 0.8 broadcast_select_fusion.1
  1847.4 0.0 all-gather.14.cloned.1.call-update
  1847.4 0.2 reduce-scatter.6.cloned.1.call-start
  1847.7 36.0 %all-gather.14.cloned.1.call-done = bf16[96,8192]{1,0:T(8,128)(2,1)} async-done(((bf16[96,2048]{1,0:T(8,128)(2,1)}), bf16[96,8192]{1,0:T(8,128)(2,1)}) %all-gather.14.cloned.1.call-update) | async-done | bytes 1572880 | tf_op jit(solution)/shard_map/all_gather | solution.py:20
  1883.7 1.8 fusion.51
  1885.5 23.8 %fusion.14 = f32[96,4096]{1,0:T(8,128)S(1)} fusion(bf16[1,1,8192,4096]{3,2,1,0:T(8,128)(2,1)} %all-gather.8.cloned.1.call-done, bf16[96,8192]{1,0:T(8,128)(2,1)} %all-gather.14.cloned.1.call-done, f32[96]{0:T(128)S(1)} %add_rsqrt_fusion.2, f32[8192]{0:T(1024)S(1)} %bitcast.94), kind=kOutput, calls=%fused_computation.15 | convolution fusion | flops 6445596672 | bytes 70287744 | tf_op jit(solution)/shard_map/dot_general | solution.py:35
  1909.4 24.6 %fusion.41.clone.4 = bf16[96,4096]{1,0:T(8,128)(2,1)} fusion(bf16[1,1,8192,4096]{3,2,1,0:T(8,128)(2,1)} %all-gather.10.cloned.1.call-done, f32[96,4096]{1,0:T(8,128)S(1)} %fusion.14, bf16[96,8192]{1,0:T(8,128)(2,1)S(1)} %copy-done.2, f32[96]{0:T(128)S(1)} %add_rsqrt_fusion.2, f32[8192]{0:T(1024)S(1)} %bitcast.95), kind=kOutput, calls=%fused_computation.26.clone.clone.clone.1 | convolution fusion | flops 6447955968 | bytes 71074176 | tf_op jit(solution)/shard_map/dot_general | solution.py:36
  1934.0 25.6 %fusion.21 = bf16[96,8192]{1,0:T(8,128)(2,1)} fusion(bf16[1,1,4096,8192]{3,2,1,0:T(8,128)(2,1)} %all-gather.12.cloned.1.call-done, bf16[96,4096]{1,0:T(8,128)(2,1)} %fusion.41.clone.4), kind=kOutput, calls=%fused_computation.20 | convolution fusion | flops 6443237376 | bytes 69468160 | tf_op jit(solution)/shard_map/dot_general | solution.py:38
  1959.6 0.0 all-gather.16.cloned.1.call-start
  1959.7 34.2 %reduce-scatter.6.cloned.1.call-done = bf16[96,2048]{1,0:T(8,128)(2,1)} async-done(((bf16[96,8192]{1,0:T(8,128)(2,1)}), bf16[96,2048]{1,0:T(8,128)(2,1)}) %reduce-scatter.6.cloned.1.call-update) | async-done | bytes 393232 | tf_op jit(solution)/shard_map/reduce_scatter | solution.py:27
  1993.9 2.0 broadcast_select_fusion.2
  1995.9 1.7 collective-permute-done.2
  1997.6 0.8 copy-done.8
  1998.4 0.3 reduce-scatter.8.cloned.1.call-start
  1998.6 35.9 %all-gather.16.cloned.1.call-done = bf16[96,8192]{1,0:T(8,128)(2,1)} async-done(((bf16[96,2048]{1,0:T(8,128)(2,1)}), bf16[96,8192]{1,0:T(8,128)(2,1)}) %all-gather.16.cloned.1.call-update) | async-done | bytes 1572880 | tf_op jit(solution)/shard_map/all_gather | solution.py:20
  2034.6 1.8 fusion.54
  2036.4 23.8 %fusion.12 = f32[96,4096]{1,0:T(8,128)S(1)} fusion(bf16[1,1,8192,4096]{3,2,1,0:T(8,128)(2,1)} %all-gather.8.cloned.1.call-done, bf16[96,8192]{1,0:T(8,128)(2,1)} %all-gather.16.cloned.1.call-done, f32[96]{0:T(128)S(1)} %add_rsqrt_fusion.1, f32[8192]{0:T(1024)S(1)} %bitcast.96), kind=kOutput, calls=%fused_computation.13 | convolution fusion | flops 6445596672 | bytes 70287744 | tf_op jit(solution)/shard_map/dot_general | solution.py:35
  2060.3 24.6 %fusion.36.clone.2 = bf16[96,4096]{1,0:T(8,128)(2,1)} fusion(bf16[1,1,8192,4096]{3,2,1,0:T(8,128)(2,1)} %all-gather.10.cloned.1.call-done, f32[96,4096]{1,0:T(8,128)S(1)} %fusion.12, bf16[96,8192]{1,0:T(8,128)(2,1)S(1)} %copy-done.1, f32[96]{0:T(128)S(1)} %add_rsqrt_fusion.1, f32[8192]{0:T(1024)S(1)} %bitcast.97), kind=kOutput, calls=%fused_computation.25.clone.clone.clone | convolution fusion | flops 6447955968 | bytes 71074176 | tf_op jit(solution)/shard_map/dot_general | solution.py:36
  2084.9 25.6 %fusion.24 = bf16[96,8192]{1,0:T(8,128)(2,1)} fusion(bf16[1,1,4096,8192]{3,2,1,0:T(8,128)(2,1)} %all-gather.12.cloned.1.call-done, bf16[96,4096]{1,0:T(8,128)(2,1)} %fusion.36.clone.2), kind=kOutput, calls=%fused_computation.21 | convolution fusion | flops 6443237376 | bytes 69468160 | tf_op jit(solution)/shard_map/dot_general | solution.py:38
  2110.6 0.7 copy.13
  2111.2 4.2 all-to-all-start.1
  2115.5 0.1 convert_reduce_fusion
  2115.6 0.1 select_reduce_fusion
  2115.7 1.5 collective-permute-done.3
  2117.2 27.7 %reduce-scatter.8.cloned.1.call-done = bf16[96,2048]{1,0:T(8,128)(2,1)} async-done(((bf16[96,8192]{1,0:T(8,128)(2,1)}), bf16[96,2048]{1,0:T(8,128)(2,1)}) %reduce-scatter.8.cloned.1.call-update) | async-done | bytes 393232 | tf_op jit(solution)/shard_map/reduce_scatter | solution.py:27
  2144.8 1.1 fusion.98
  2146.0 0.1 collective-permute-start.4
  2146.1 4.2 all-to-all-start
  2150.3 0.2 convert_reduce_fusion.1
  2150.5 0.2 reduce-window.7
  2150.6 0.1 convert_reduce_fusion.2
  2150.7 0.1 collective-permute-start.5
  2150.8 0.1 select_reduce_fusion.1
  2150.9 10.3 all-to-all-done
  2161.3 0.8 gather_fusion
  2162.1 0.2 fusion.84
  2162.3 9.8 psum.21
  2172.1 0.4 multiply_reduce_fusion
  2172.5 9.0 all-reduce
  2181.5 0.6 multiply_reduce_fusion.1
  2182.7 1.2 fusion.83
  (46 shorter events, 0.2 us)
Async XLA Ops:
  7.2 40.8 %all-gather.18.cloned.1.call-start = ((), (), s32[]{:S(2)}) async-start(), calls=%async_computation.13 | async-start | bytes 1966080 | tf_op jit(solution)/shard_map/all_gather | solution.py:20
  7.9 617.6 %all-gather.8.cloned.1.call-start = ((), (), s32[]{:S(2)}) async-start(), calls=%async_computation.5 | async-start | bytes 83886080 | tf_op jit(solution)/shard_map/all_gather | solution.py:77
  8.6 1195.5 %all-gather.10.cloned.1.call-start = ((), (), s32[]{:S(2)}) async-start(), calls=%async_computation.6 | async-start | bytes 83886080 | tf_op jit(solution)/shard_map/all_gather | solution.py:78
  9.4 616.1 %copy-start.3 = (f32[1,1,8192]{2,1,0:T(1,128)S(1)}, f32[1,1,8192]{2,1,0:T(1,128)}, u32[]{:S(2)}) copy-start(f32[1,1,8192]{2,1,0:T(1,128)} %param.10) | copy-start | bytes 98308
  9.4 1773.3 %all-gather.12.cloned.1.call-start = ((), (), s32[]{:S(2)}) async-start(), calls=%async_computation.7 | async-start | bytes 83886080 | tf_op jit(solution)/shard_map/all_gather | solution.py:79
  10.0 1833.7 %reduce-scatter.4.cloned.1.call-start = ((), (), s32[]{:S(2)}) async-start(), calls=%async_computation.8 | async-start | bytes 1966080 | tf_op jit(solution)/shard_map/reduce_scatter | solution.py:27
  625.5 578.7 %copy-start = (bf16[1,96,8192]{2,1,0:T(8,128)(2,1)S(1)}, bf16[1,96,8192]{2,1,0:T(8,128)(2,1)}, u32[]{:S(2)}) copy-start(bf16[1,96,8192]{2,1,0:T(8,128)(2,1)} %all-gather.18.cloned.1.call-done) | copy-start | bytes 4718596
  1240.2 568.1 %copy-start.7 = (bf16[1,96,2048]{2,1,0:T(8,128)(2,1)S(1)}, bf16[1,96,2048]{2,1,0:T(8,128)(2,1)}, u32[]{:S(2)}) copy-start(bf16[1,96,2048]{2,1,0:T(8,128)(2,1)} %param.9) | copy-start | bytes 1179652
  1808.3 75.4 %all-gather.14.cloned.1.call-start = ((), (), s32[]{:S(2)}) async-start(), calls=%async_computation.9 | async-start | bytes 1966080 | tf_op jit(solution)/shard_map/all_gather | solution.py:20
  1808.3 36.6 %collective-permute-start = (bf16[96,2048]{1,0:T(8,128)(2,1)S(1)}, bf16[96,2048]{1,0:T(8,128)(2,1)S(1)}, u32[]{:S(2)}, u32[]{:S(2)}) collective-permute-start(bf16[96,2048]{1,0:T(8,128)(2,1)S(1)} %bitcast.98), channel_id=1, source_target_pairs={{0,16},{16,0},{1,17},{17,1},{2,18},{18,2},{3,19},{19,3},{4,20},{20... | collective-permute-start | bytes 1179656 | tf_op jit(solution)/shard_map/ppermute | solution.py:16
  1844.8 1.8 collective-permute-start.1
  1844.9 40.6 %copy-start.5 = (bf16[96,2048]{1,0:T(8,128)(2,1)}, bf16[96,2048]{1,0:T(8,128)(2,1)S(1)}, u32[]{:S(2)}) copy-start(bf16[96,2048]{1,0:T(8,128)(2,1)S(1)} %collective-permute-done) | copy-start | bytes 1179652
  1847.4 146.5 %reduce-scatter.6.cloned.1.call-start = ((), (), s32[]{:S(2)}) async-start(), calls=%async_computation.10 | async-start | bytes 1966080 | tf_op jit(solution)/shard_map/reduce_scatter | solution.py:27
  1885.5 23.9 %copy-start.2 = (bf16[96,8192]{1,0:T(8,128)(2,1)S(1)}, bf16[96,8192]{1,0:T(8,128)(2,1)}, u32[]{:S(2)}) copy-start(bf16[96,8192]{1,0:T(8,128)(2,1)} %all-gather.14.cloned.1.call-done) | copy-start | bytes 4718596
  1934.0 59.9 %copy-start.4 = (bf16[96,2048]{1,0:T(8,128)(2,1)S(1)}, bf16[96,2048]{1,0:T(8,128)(2,1)}, u32[]{:S(2)}) copy-start(bf16[96,2048]{1,0:T(8,128)(2,1)} %broadcast_select_fusion.1) | copy-start | bytes 1179652
  1934.0 59.9 %copy-start.6 = (bf16[96,2048]{1,0:T(8,128)(2,1)S(1)}, bf16[96,2048]{1,0:T(8,128)(2,1)}, u32[]{:S(2)}) copy-start(bf16[96,2048]{1,0:T(8,128)(2,1)} %copy-done.5) | copy-start | bytes 1179652
  1959.6 75.0 %all-gather.16.cloned.1.call-start = ((), (), s32[]{:S(2)}) async-start(), calls=%async_computation.11 | async-start | bytes 1966080 | tf_op jit(solution)/shard_map/all_gather | solution.py:20
  1995.9 1.7 collective-permute-start.2
  1997.6 0.8 copy-start.8
  1998.4 146.5 %reduce-scatter.8.cloned.1.call-start = ((), (), s32[]{:S(2)}) async-start(), calls=%async_computation.12 | async-start | bytes 1966080 | tf_op jit(solution)/shard_map/reduce_scatter | solution.py:27
  2036.4 23.9 %copy-start.1 = (bf16[96,8192]{1,0:T(8,128)(2,1)S(1)}, bf16[96,8192]{1,0:T(8,128)(2,1)}, u32[]{:S(2)}) copy-start(bf16[96,8192]{1,0:T(8,128)(2,1)} %all-gather.16.cloned.1.call-done) | copy-start | bytes 4718596
  2084.9 25.6 %copy-start.12 = (s32[1,1,4]{2,1,0:T(1,128)S(1)}, s32[1,1,4]{2,1,0:T(1,128)}, u32[]{:S(2)}) copy-start(s32[1,1,4]{2,1,0:T(1,128)} %param.16) | copy-start | bytes 52
  2084.9 30.6 %copy-start.10 = (bf16[96,2048]{1,0:T(8,128)(2,1)S(1)}, bf16[96,2048]{1,0:T(8,128)(2,1)}, u32[]{:S(2)}) copy-start(bf16[96,2048]{1,0:T(8,128)(2,1)} %get-tuple-element.7) | copy-start | bytes 1179652
  2084.9 30.6 %copy-start.13 = (s32[1,1,96]{2,1,0:T(1,128)S(1)}, s32[1,1,96]{2,1,0:T(1,128)}, u32[]{:S(2)}) copy-start(s32[1,1,96]{2,1,0:T(1,128)} %param.17) | copy-start | bytes 1156
  2084.9 59.9 %copy-start.9 = (bf16[96,2048]{1,0:T(8,128)(2,1)S(1)}, bf16[96,2048]{1,0:T(8,128)(2,1)}, u32[]{:S(2)}) copy-start(bf16[96,2048]{1,0:T(8,128)(2,1)} %copy-done.8) | copy-start | bytes 1179652
  2111.2 34.8 %all-to-all-start.1 = ((bf16[4,1,1]{2,1,0:T(2,128)(2,1)}), bf16[4,1,1]{2,1,0:T(2,128)(2,1)S(1)}, u32[]{:S(2)}, u32[]{:S(2)}) async-start(bf16[4,1,1]{2,1,0:T(2,128)(2,1)} %copy.13), calls=%async_computation.4 | async-start | bytes 4096 | tf_op jit(solution)/shard_map/all_to_all | solution.py:103
  2115.4 1.7 collective-permute-start.3
  2146.0 26.1 %copy-start.11 = (f32[2048]{0:T(1024)S(1)}, f32[2048]{0:T(1024)}, u32[]{:S(2)}) copy-start(f32[2048]{0:T(1024)} %param.14) | copy-start | bytes 24580
  2146.0 4.7 collective-permute-start.4
  2146.1 15.2 all-to-all-start
  2150.7 11.4 collective-permute-start.5
Sparse Core Ops, SparseCore 0:
  9.6 38.3 all-gather.17
  49.8 575.6 all-gather.7
  627.3 576.7 all-gather.9
  1205.9 576.7 all-gather.11
  1808.4 35.2 reduce-scatter.3
  1847.5 36.0 all-gather.13
  1959.7 34.1 reduce-scatter.5
  1998.5 36.0 all-gather.15
  2110.7 34.1 reduce-scatter.7
where the time goes:
time: 2190 us
  waiting for transfers between devices  1890 us (86%)
  matrix products  246 us (11%)
    all_gather x1, waiting for transfers between devices, body(): lax.all_gather(gate_proj, 'dp', axis=2, tiled=True)  576 us
    all_gather x1, waiting for transfers between devices, body(): lax.all_gather(down_proj, 'dp', axis=3, tiled=True)  543 us
    all_gather x1, waiting for transfers between devices, body(): lax.all_gather(up_proj, 'dp', axis=2, tiled=True)  542 us
    all_gather x3, waiting for transfers between devices, widen_rows(): full = lax.all_gather(carried, 'mp', axis=1, tiled=True)  110 us
    reduce_scatter x3, waiting for transfers between devices, finish_layer(): lax.psum_scatter(partial_value.astype(jnp.bfloat16), 'mp', scatter_dimens...  97.2 us
    dot_general x3, matrix products, layer_held(): up_full = jnp.dot(normed, up_rows, preferred_element_type=jnp.float32)  85.3 us
    dot_general x3, matrix products, layer_held(): gate_full = jnp.dot(normed, gate_rows, preferred_element_type=jnp.float32)  84.3 us
    dot_general x3, matrix products, layer_held(): jnp.dot(inner, down_rows, preferred_element_type=jnp.float32)  76.7 us
  transfers between devices with their start and end apart: 17, of which 13 were waited for; matrix products, arithmetic and copies ran while one was open for 4% of the time, Pallas kernels for 0%

commit v1 on v0

v1 whole, which is shorter than its diff:
```python
import functools

import jax
import jax.numpy as jnp
from jax import lax
from jax.experimental import pallas as pl
from jax.experimental.pallas import tpu as pltpu
from jax.sharding import PartitionSpec as P

D = 8192
DOCS = 8
EPSILON = 1e-05
AXES = ("section", "dp", "mp")
TILE = 512
HALVES = 2
VMEM_LIMIT = 40 * 1024 * 1024


def swap_section(value):
    return lax.ppermute(value, "section", [(0, 1), (1, 0)])


def transpose_mesh(value):
    pairs = [(d * 4 + m, m * 4 + d) for d in range(4) for m in range(4)]
    return lax.ppermute(value, ("dp", "mp"), pairs)


def swap_dp(value, e):
    return lax.ppermute(value, "dp", [(d, d ^ e) for d in range(4)])


def swap_mp(value, k):
    return lax.ppermute(value, "mp", [(m, m ^ k) for m in range(4)])


def exchange(value, axis):
    return lax.all_to_all(value, axis, split_axis=0, concat_axis=0, tiled=True)


def either(is_own, start_own, start_other):
    pl.when(is_own)(start_own)
    pl.when(jnp.logical_not(is_own))(start_other)


def gate_up_kernel(number, first, swapped, x0, x1, x2, x3, gain_ref, gate0, up0, gate1, up1, keep_ref, send_ref, rows_ref, held, sems):
    step = pl.program_id(0)
    steps = pl.num_programs(0)
    is_own = lax.axis_index("section") == number
    own_place = lax.axis_index("dp") ^ lax.axis_index("mp")
    count = x0.shape[0]

    def fetch(j, tile):
        slot = 2 * lax.rem(tile, 2) + j
        columns = pl.ds(pl.multiple_of(first + tile * TILE, TILE), TILE)

        def copy(source):
            return lambda: pltpu.make_async_copy(source.at[:, columns], held.at[slot], sems.at[slot]).start()

        either(is_own, copy((gate0, up0)[j]), copy((gate1, up1)[j]))

    @pl.when(step == 0)
    def _():
        fetch(0, 0)
        fetch(1, 0)
        for k, ref in enumerate((x0, x1, x2, x3)):
            place = own_place ^ k
            if swapped:
                place = 2 * (place % 2) + place // 2
            piece = ref[...].astype(jnp.float32) * gain_ref[...]
            rows_ref[pl.ds(pl.multiple_of(place * count, count), count), :] = piece.astype(jnp.bfloat16)

    for j in range(2):

        @pl.when(step + 1 < steps)
        def _():
            fetch(j, step + 1)

        slot = 2 * lax.rem(step, 2) + j
        pltpu.make_async_copy(gate0.at[:, pl.ds(0, TILE)], held.at[slot], sems.at[slot]).wait()
        product = jnp.dot(rows_ref[...], held[slot], preferred_element_type=jnp.float32)
        keep_ref[j] = product[: 2 * count]
        send_ref[j] = product[2 * count :].astype(jnp.bfloat16)


def gate_up(number, first, width, swapped, rows, gain_row, own, received):
    groups = 4
    count, depth = rows[0].shape
    whole = lambda shape: pl.BlockSpec(shape, lambda t: (0,) * len(shape))
    return pl.pallas_call(
        functools.partial(gate_up_kernel, number, first, swapped),
        grid=(width // TILE,),
        in_specs=[whole((count, depth))] * 4 + [whole((1, depth))] + [pl.BlockSpec(memory_space=pl.ANY)] * 4,
        out_specs=[pl.BlockSpec((2, 2 * count, TILE), lambda t: (0, 0, t))] * 2,
        out_shape=[
            jax.ShapeDtypeStruct((2, 2 * count, width), jnp.float32),
            jax.ShapeDtypeStruct((2, 2 * count, width), jnp.bfloat16),
        ],
        scratch_shapes=[
            pltpu.VMEM((groups * count, depth), jnp.bfloat16),
            pltpu.VMEM((4, depth, TILE), jnp.bfloat16),
            pltpu.SemaphoreType.DMA((4,)),
        ],
        compiler_params=pltpu.CompilerParams(vmem_limit_bytes=VMEM_LIMIT),
        cost_estimate=pl.CostEstimate(
            flops=4 * groups * count * depth * width, bytes_accessed=4 * depth * width, transcendentals=0
        ),
        name="gate_up",
    )(*rows, gain_row, *own, *received)


def down_kernel(number, x0, x1, x2, x3a, x3b, own, received, out_ref, rows_ref, held, sems):
    step = pl.program_id(0)
    steps = pl.num_programs(0)
    is_own = lax.axis_index("section") == number
    data_pos = lax.axis_index("dp")
    groups = 4
    count, depth = x0.shape

    def fetch(tile):
        slot = lax.rem(tile, 2)
        columns = pl.ds(pl.multiple_of(tile * TILE, TILE), TILE)

        def copy(source):
            return lambda: pltpu.make_async_copy(source.at[:, columns], held.at[slot], sems.at[slot]).start()

        either(is_own, copy(own), copy(received))

    @pl.when(step == 0)
    def _():
        fetch(0)
        for e, piece in enumerate((x0, x1, x2)):
            rows_ref[pl.ds(pl.multiple_of((data_pos ^ e) * count, count), count), :] = piece[...]
        corner = pl.ds(pl.multiple_of((data_pos ^ 3) * count, count), count)
        rows_ref[corner, : depth // 2] = x3a[...]
        rows_ref[corner, depth // 2 :] = x3b[...]

    @pl.when(step + 1 < steps)
    def _():
        fetch(step + 1)

    slot = lax.rem(step, 2)
    pltpu.make_async_copy(own.at[:, pl.ds(0, TILE)], held.at[slot], sems.at[slot]).wait()
    product = jnp.dot(rows_ref[...], held[slot], preferred_element_type=jnp.float32)
    for g in range(groups):
        out_ref[g] = product[g * count : (g + 1) * count].astype(jnp.bfloat16)


def down_terms(number, pieces, own, received):
    groups = 4
    count, depth = pieces[0].shape
    features = own.shape[1]
    return pl.pallas_call(
        functools.partial(down_kernel, number),
        grid=(features // TILE,),
        in_specs=[pl.BlockSpec(piece.shape, lambda t: (0, 0)) for piece in pieces]
        + [pl.BlockSpec(memory_space=pl.ANY)] * 2,
        out_specs=pl.BlockSpec((groups, count, TILE), lambda t: (0, 0, t)),
        out_shape=jax.ShapeDtypeStruct((groups, count, features), jnp.bfloat16),
        scratch_shapes=[
            pltpu.VMEM((groups * count, depth), jnp.bfloat16),
            pltpu.VMEM((2, depth, TILE), jnp.bfloat16),
            pltpu.SemaphoreType.DMA((2,)),
        ],
        compiler_params=pltpu.CompilerParams(vmem_limit_bytes=VMEM_LIMIT),
        cost_estimate=pl.CostEstimate(
            flops=2 * groups * count * depth * features, bytes_accessed=2 * depth * features, transcendentals=0
        ),
        name="down",
    )(*pieces, own, received)


def sum_squares(rows):
    squares = jnp.stack([jnp.sum(jnp.square(piece.astype(jnp.float32)), axis=-1) for piece in rows])
    own_place = lax.axis_index("dp") ^ lax.axis_index("mp")
    keep, send = [jnp.stack([squares[i ^ own_place] for i in pair]) for pair in ((0, 2), (1, 3))]
    keep = keep + swap_dp(send, 1)
    return keep[0] + swap_dp(keep[1], 2)


def stream(number, first, width, steps, rows, gain_row, own, received):
    keep, send = gate_up(number, first, width, steps[0] == 1, rows, gain_row, own, received)
    count = rows[0].shape[0]
    got = swap_dp(send, steps[0])
    onward = (keep[:, count:] + got[:, count:].astype(jnp.float32)).astype(jnp.bfloat16)
    last = swap_dp(onward, steps[1])
    return keep[:, :count] + got[:, :count].astype(jnp.float32) + last.astype(jnp.float32)


def enter(own):
    return [own] + [swap_mp(own, k) for k in (1, 2, 3)]


def layer(number, own, rows, gain_row, weights, received):
    half = weights[0].shape[1] // 2
    scale = lax.rsqrt(sum_squares(rows) / D + EPSILON)[:, None]
    args = (rows, gain_row, weights[:2], received[:2])
    inner = []
    for total in (stream(number, 0, half, (1, 2), *args), stream(number, half, half, (2, 1), *args)):
        inner.append((jax.nn.silu(total[0] * scale) * (total[1] * scale)).astype(jnp.bfloat16))
    inner = jnp.concatenate(inner, axis=1)
    along_x = swap_dp(inner, 1)
    along_y = swap_dp(inner, 2)
    corner = (swap_dp(along_y[:, :half], 1), swap_dp(along_x[:, half:], 2))
    terms = down_terms(number, (inner, along_x, along_y) + corner, weights[2], received[2])
    terms = exchange(terms, "mp")
    return (own.astype(jnp.float32) + jnp.sum(terms.astype(jnp.float32), axis=0)).astype(jnp.bfloat16)


def fast_final(hidden_in, layer_gain, gate, up, down, targets):
    tokens, features = hidden_in.shape[1:]
    count = tokens // HALVES
    is_first = lax.axis_index("section") == 0
    gain = lax.dynamic_slice_in_dim(layer_gain[0, 0], lax.axis_index("dp") * features, features, 0)
    other_gain = swap_section(gain)
    owns = [transpose_mesh(hidden_in[0, i * count : (i + 1) * count]) for i in range(HALVES)]
    other_gate, other_up = swap_section(gate), swap_section(up)
    rows = [enter(owns[0])]
    rows[0], targets, later_down = lax.optimization_barrier((rows[0], targets, down))
    received = (other_gate, other_up, swap_section(later_down))
    rows += [enter(own) for own in owns[1:]]
    for number in range(2):
        gain_row = jnp.where(is_first == (number == 0), gain, other_gain)[None, :]
        if number:
            rows = [enter(own) for own in owns]
        owns = [layer(number, own, piece, gain_row, (gate, up, down), received) for own, piece in zip(owns, rows)]
    return jnp.concatenate([transpose_mesh(own) for own in owns], axis=0), targets


def fast_targets(teacher, counts, token_count):
    capacity = teacher.shape[0] // 4
    features = teacher.shape[1]
    arrived = lax.all_to_all(
        teacher.reshape(4, capacity, features), "dp", split_axis=0, concat_axis=0, tiled=True
    )
    all_counts = lax.all_to_all(
        counts.reshape(4, 1).astype(jnp.bfloat16), "dp", split_axis=0, concat_axis=0, tiled=True
    )
    per_source = all_counts[:, 0].astype(jnp.int32)
    end_rows = jnp.cumsum(per_source)
    starts = end_rows - per_source
    positions = jnp.arange(token_count, dtype=jnp.int32)
    source_of = jnp.sum((end_rows[None, :] <= positions[:, None]).astype(jnp.int32), axis=1)
    matching = source_of[:, None] == jnp.arange(4, dtype=jnp.int32)[None, :]
    first_row = jnp.sum(jnp.where(matching, starts[None, :], 0), axis=1)
    flat_index = source_of * capacity + positions - first_row
    return arrived.reshape(-1, features)[flat_index].astype(jnp.float32)


def weights_of_rows(doc_row):
    member = (doc_row[:, None] == jnp.arange(DOCS, dtype=jnp.int32)[None, :]).astype(jnp.float32)
    doc_sizes = jnp.sum(member, axis=0)
    return jnp.sum(member * (1.0 / doc_sizes)[None, :], axis=1)


def distil(final, targets, row_weight, final_gain, sum_features):
    wide = final.astype(jnp.float32)
    gain_row = final_gain[None, :]
    squares = sum_features(jnp.sum(wide * wide, axis=-1))
    rscale = lax.rsqrt(squares / D + EPSILON)
    normal_rows = wide * rscale[:, None]
    residual = normal_rows * gain_row - targets
    d_student = row_weight[:, None] * residual
    sums = sum_features(
        jnp.stack(
            [
                jnp.sum(normal_rows * gain_row * d_student, axis=-1),
                jnp.sum(residual * residual, axis=-1),
            ]
        )
    )
    d_hidden = rscale[:, None] * (gain_row * d_student - normal_rows * sums[0][:, None] / D)
    doc_loss = jnp.sum(row_weight * 0.5 * sums[1]) / (DOCS * D)
    return d_hidden[None], doc_loss.reshape(1, 1)


def distil_once(final, targets, row_weight, final_gain):
    wide = final.astype(jnp.float32)
    features = wide.shape[1]
    gained = wide * final_gain[None, :]
    squares = jnp.sum(wide * wide, axis=-1)
    rough = gained * lax.rsqrt(squares / features + EPSILON)[:, None] - targets
    local = jnp.stack(
        [squares, jnp.sum(rough * rough, axis=-1), jnp.sum(gained * rough, axis=-1), jnp.sum(gained * gained, axis=-1)]
    )
    squares, rough_squares, crossed, gained_squares = jnp.moveaxis(lax.all_gather(local, "mp"), 1, 0)
    rscale = lax.rsqrt(jnp.sum(squares, axis=0) / D + EPSILON)
    shift = rscale[None, :] - lax.rsqrt(squares / features + EPSILON)
    errors = jnp.sum(rough_squares + shift * (2.0 * crossed + shift * gained_squares), axis=0)
    inner_sum = row_weight * rscale * jnp.sum(crossed + shift * gained_squares, axis=0)
    gain_row = final_gain[None, :]
    normal_rows = wide * rscale[:, None]
    d_student = row_weight[:, None] * (normal_rows * gain_row - targets)
    d_hidden = rscale[:, None] * (gain_row * d_student - normal_rows * inner_sum[:, None] / D)
    doc_loss = jnp.sum(row_weight * 0.5 * errors) / (DOCS * D)
    return d_hidden[None], doc_loss.reshape(1, 1)


def fast_body(
    hidden_in, layer_gain, gate_proj, up_proj, down_proj, final_gain, teacher_rows, send_counts, doc_ids
):
    targets = fast_targets(teacher_rows[0, 0], send_counts[0, 0], hidden_in.shape[1])
    final, targets = fast_final(
        hidden_in, layer_gain, gate_proj[0, 0], up_proj[0, 0], down_proj[0, 0], targets
    )
    return distil_once(final, targets, weights_of_rows(doc_ids[0, 0]), final_gain)


def wide_layer(rows, gain_row, gate, up, down):
    wide = rows.astype(jnp.float32)
    squares = lax.psum(jnp.sum(wide * wide, axis=-1, keepdims=True), "dp")
    scale = lax.rsqrt(squares / D + EPSILON)
    normed = (wide * scale * gain_row[None, :]).astype(jnp.bfloat16)
    both = jnp.stack(
        [jnp.dot(normed, weight, preferred_element_type=jnp.float32) for weight in (gate, up)]
    )
    total = lax.psum_scatter(both, "dp", scatter_dimension=1, tiled=True)
    inner = (jax.nn.silu(total[0]) * total[1]).astype(jnp.bfloat16)
    inner = lax.all_gather(inner, "dp", axis=0, tiled=True)
    term = jnp.dot(inner, down, preferred_element_type=jnp.float32)
    return (wide + lax.psum(term, "mp")).astype(jnp.bfloat16)


def wide_body(
    hidden_in, layer_gain, gate_proj, up_proj, down_proj, final_gain, teacher_rows, send_counts, doc_ids
):
    phases = lax.axis_size("section")
    count_data = lax.axis_size("dp")
    phase_pos = lax.axis_index("section")
    data_pos = lax.axis_index("dp")
    model_pos = lax.axis_index("mp")
    tokens, narrow = hidden_in.shape[1:]
    rows = lax.all_gather(hidden_in[0], "section", axis=0)
    rows = lax.all_gather(rows, "mp", axis=2, tiled=True)
    rows = lax.all_to_all(rows, "dp", split_axis=2, concat_axis=1, tiled=True)
    features = rows.shape[2]
    rows = rows.reshape(-1, features)
    ring = [(s, (s + 1) % phases) for s in range(phases)]
    for repeat in range(gate_proj.shape[0]):
        gain_row = lax.dynamic_slice_in_dim(layer_gain[repeat, 0], data_pos * features, features, 0)
        for phase in range(phases):
            fresh = wide_layer(
                rows, gain_row, gate_proj[repeat, 0], up_proj[repeat, 0], down_proj[repeat, 0]
            )
            rows = lax.ppermute(jnp.where(phase_pos == phase, fresh, rows), "section", ring)
    rows = lax.all_gather(rows, "section", axis=0)[0]
    rows = lax.dynamic_index_in_dim(
        rows.reshape(phases, count_data * tokens, features), phase_pos, 0, keepdims=False
    )
    rows = lax.all_to_all(rows, "dp", split_axis=0, concat_axis=1, tiled=True)
    final = lax.dynamic_slice_in_dim(rows, model_pos * narrow, narrow, 1)
    teacher = teacher_rows[0, 0].reshape(count_data, -1, narrow)
    capacity = teacher.shape[1]
    arrived = lax.all_to_all(teacher, "dp", split_axis=0, concat_axis=0, tiled=True)
    counts = lax.all_gather(send_counts[0, 0], "dp", axis=0)
    per_source = lax.dynamic_index_in_dim(counts, data_pos, 1, keepdims=False)
    end_rows = jnp.cumsum(per_source)
    starts = end_rows - per_source
    positions = jnp.arange(tokens, dtype=jnp.int32)
    source_of = jnp.sum((end_rows[None, :] <= positions[:, None]).astype(jnp.int32), axis=1)
    flat_index = source_of * capacity + positions - starts[source_of]
    targets = arrived.reshape(-1, narrow)[flat_index].astype(jnp.float32)
    return distil(
        final,
        targets,
        weights_of_rows(doc_ids[0, 0]),
        final_gain,
        lambda value: lax.psum(value, "mp"),
    )


def solution(mesh):
    in_specs = (
        P("section", "dp", "mp"),
        P(None, "section", None),
        P(None, "section", "dp", "mp"),
        P(None, "section", "dp", "mp"),
        P(None, "section", "mp", "dp"),
        P("mp"),
        P("section", "dp", None, "mp"),
        P("section", "dp", None),
        P("section", "dp", None),
    )
    out_specs = (P("section", "dp", "mp"), P("section", "dp"))
    sizes = tuple(mesh.shape[axis] for axis in AXES)
    body = fast_body if sizes == (2, 4, 4) else wide_body
    return jax.shard_map(body, mesh=mesh, in_specs=in_specs, out_specs=out_specs, check_vma=False)
```

time: 2190 us -> 420 us (0.19)
  waiting for transfers between devices: 1890 us -> 189 us
  matrix products: 246 us -> 0 us
  starting transfers between devices: 9.5 us -> 107 us
  Pallas kernels: 0 us -> 94.8 us
    all_gather x6 -> x0, waiting for transfers between devices: 1770 us -> none  [the longest x1 576 us: body(): lax.all_gather(gate_proj, 'dp', axis=2, tiled=True)]
    dot_general x9 -> x0, matrix products: 246 us -> none  [the longest x3 85.3 us: layer_held(): up_full = jnp.dot(normed, up_rows, preferred_element_type=jnp.float32)]
    ppermute x6 -> x60, waiting for transfers between devices: 4.91 us -> 152 us  [the longest x40 93.5 us: swap_dp(): return lax.ppermute(value, 'dp', [(d, d ^ e) for d in range(4)])]
    reduce_scatter x3 -> x0, waiting for transfers between devices: 97.2 us -> none  [finish_layer(): lax.psum_scatter(partial_value.astype(jnp.bfloat16), 'mp', scatter_dimens...]
    pallas_call x0 -> x12, Pallas kernels: none -> 94.8 us  [the longest x8 59.7 us: gate_up(): pl.pallas_call(functools.partial(gate_up_kernel, number, first, swapped),...]
    ppermute x6 -> x60, starting transfers between devices: 0.32 us -> 69.8 us  [the longest x40 41.3 us: swap_dp(): return lax.ppermute(value, 'dp', [(d, d ^ e) for d in range(4)])]
    all_to_all x2 -> x6, starting transfers between devices: 8.42 us -> 36.9 us  [the longest x4 26.4 us: exchange(): return lax.all_to_all(value, axis, split_axis=0, concat_axis=0, tiled=True)]
    all_to_all x2 -> x6, waiting for transfers between devices: 10.3 us -> 36.9 us  [the longest x4 36.9 us: exchange(): return lax.all_to_all(value, axis, split_axis=0, concat_axis=0, tiled=True)]
  transfers between devices with their start and end apart: 17 -> 66, of which waited for: 13 -> 37; matrix products, arithmetic and copies ran while one was open for 4% -> 3% of each run, Pallas kernels for 0% -> 18%
where the time goes in v1:
time: 420 us; the launch traced here: 419 us
  waiting for transfers between devices  189 us (45%)
  starting transfers between devices  107 us (25%)
  Pallas kernels  94.8 us (23%)
  blocking collectives  11.9 us (3%)
  other arithmetic  10.6 us (3%)
    ppermute x40, waiting for transfers between devices, swap_dp(): return lax.ppermute(value, 'dp', [(d, d ^ e) for d in range(4)])  93.5 us
    pallas_call x8, Pallas kernels, gate_up(): pl.pallas_call(functools.partial(gate_up_kernel, number, first, swapped),...  59.7 us
    ppermute x40, starting transfers between devices, swap_dp(): return lax.ppermute(value, 'dp', [(d, d ^ e) for d in range(4)])  41.3 us
    all_to_all x4, waiting for transfers between devices, exchange(): return lax.all_to_all(value, axis, split_axis=0, concat_axis=0, tiled=True)  36.9 us
    pallas_call x4, Pallas kernels, down_terms(): pl.pallas_call(functools.partial(down_kernel, number), grid=(features //...  35 us
    ppermute x4, waiting for transfers between devices, transpose_mesh(): return lax.ppermute(value, ('dp', 'mp'), pairs)  31.6 us
    all_to_all x4, starting transfers between devices, exchange(): return lax.all_to_all(value, axis, split_axis=0, concat_axis=0, tiled=True)  26.4 us
    ppermute x12, waiting for transfers between devices, swap_mp(): return lax.ppermute(value, 'mp', [(m, m ^ k) for m in range(4)])  26.2 us
  transfers between devices with their start and end apart: 66, of which 37 were waited for; matrix products, arithmetic and copies ran while one was open for 3% of the time, Pallas kernels for 18%

profile of v1, /device:TPU:2, one launch (start us, length us, event | category | flops | bytes accessed | tf_op | source)
XLA Modules:
  0.0 419.0 jit_solution(10610763443389964468)
XLA Ops:
  2.6 4.2 %all-to-all-start.1 = ((bf16[4,1,1]{2,1,0:T(2,128)(2,1)}), bf16[4,1,1]{2,1,0:T(2,128)(2,1)S(1)}, u32[]{:S(2)}, u32[]{:S(2)}) async-start(bf16[4,1,1]{2,1,0:T(2,128)(2,1)} %copy.22), calls=%async_computation.1 | async-start | bytes 4096 | tf_op jit(solution)/shard_map/all_to_all | solution.py:235
  7.9 2.9 collective-permute-start
  10.8 6.2 %all-to-all-start = ((bf16[4,48,2048]{2,1,0:T(8,128)(2,1)}), bf16[4,48,2048]{2,1,0:T(8,128)(2,1)S(1)}, u32[]{:S(2)}, u32[]{:S(2)}) async-start(bf16[4,48,2048]{2,1,0:T(8,128)(2,1)} %bitcast.256), calls=%async_computation | async-start | bytes 1572864 | tf_op jit(solution)/shard_map/all_to_all | solution.py:232
  17.6 8.4 %collective-permute-done.x0 = bf16[48,2048]{1,0:T(8,128)(2,1)S(1)} collective-permute-done((bf16[48,2048]{1,0:T(8,128)(2,1)S(1)}, bf16[48,2048]{1,0:T(8,128)(2,1)S(1)}, u32[]{:S(2)}, u32[]{:S(2)}) %collective-permute-start) | collective-permute-done | bytes 196640 | tf_op jit(solution)/shard_map/ppermute | solution.py:25
  25.9 2.0 collective-permute-start.2
  28.0 2.3 collective-permute-start.3
  32.1 2.5 collective-permute-done.1.x1
  34.7 7.8 %collective-permute-done.2.x2 = bf16[48,2048]{1,0:T(8,128)(2,1)S(1)} collective-permute-done((bf16[48,2048]{1,0:T(8,128)(2,1)S(1)}, bf16[48,2048]{1,0:T(8,128)(2,1)S(1)}, u32[]{:S(2)}, u32[]{:S(2)}) %collective-permute-start.2) | collective-permute-done | bytes 196640 | tf_op jit(solution)/shard_map/ppermute | solution.py:33
  42.5 4.0 collective-permute-start.32
  46.5 14.5 %collective-permute-done.32.x0 = bf16[48,2048]{1,0:T(8,128)(2,1)S(1)} collective-permute-done((bf16[48,2048]{1,0:T(8,128)(2,1)S(1)}, bf16[48,2048]{1,0:T(8,128)(2,1)S(1)}, u32[]{:S(2)}, u32[]{:S(2)}) %collective-permute-start.32) | collective-permute-done | bytes 196640 | tf_op jit(solution)/shard_map/ppermute | solution.py:25
  61.3 9.2 %collective-permute-done.33.x1 = bf16[48,2048]{1,0:T(8,128)(2,1)S(1)} collective-permute-done((bf16[48,2048]{1,0:T(8,128)(2,1)S(1)}, bf16[48,2048]{1,0:T(8,128)(2,1)S(1)}, u32[]{:S(2)}, u32[]{:S(2)}) %collective-permute-start.33) | collective-permute-done | bytes 196640 | tf_op jit(solution)/shard_map/ppermute | solution.py:33
  71.6 6.6 %collective-permute-done.34.x2 = bf16[48,2048]{1,0:T(8,128)(2,1)S(1)} collective-permute-done((bf16[48,2048]{1,0:T(8,128)(2,1)S(1)}, bf16[48,2048]{1,0:T(8,128)(2,1)S(1)}, u32[]{:S(2)}, u32[]{:S(2)}) %collective-permute-start.34) | collective-permute-done | bytes 196640 | tf_op jit(solution)/shard_map/ppermute | solution.py:33
  79.4 2.8 collective-permute-done.38
  83.6 2.7 collective-permute-done.9
  86.5 3.5 collective-permute-done.10
  90.0 7.5 %gate_up.9 = (f32[2,96,2048]{2,1,0:T(8,128)S(1)}, bf16[2,96,2048]{2,1,0:T(8,128)(2,1)S(1)}) custom-call(bf16[48,2048]{1,0:T(8,128)(2,1)S(1)} %collective-permute-done.x0, bf16[48,2048]{1,0:T(8,128)(2,1)S(1)} %collective-permute-done.1.x1, bf16[48,2048]{1,0:T(8,128)(2,1)S(1)} %collective-permute-done.2.x2, bf16[48,2048]{1,0:T(8,128)(2,1)S(1)} %collective-permute-done.3.x3, ...), custom_call_target="tpu_custom_call" | custom-call | flops 3221225472 | bytes 16777216 | tf_op jit(solution)/shard_map/gate_up/pallas_call | solution.py:89
  97.6 7.5 %gate_up.8 = (f32[2,96,2048]{2,1,0:T(8,128)S(1)}, bf16[2,96,2048]{2,1,0:T(8,128)(2,1)S(1)}) custom-call(bf16[48,2048]{1,0:T(8,128)(2,1)S(1)} %collective-permute-done.x0, bf16[48,2048]{1,0:T(8,128)(2,1)S(1)} %collective-permute-done.1.x1, bf16[48,2048]{1,0:T(8,128)(2,1)S(1)} %collective-permute-done.2.x2, bf16[48,2048]{1,0:T(8,128)(2,1)S(1)} %collective-permute-done.3.x3, ...), custom_call_target="tpu_custom_call" | custom-call | flops 3221225472 | bytes 16777216 | tf_op jit(solution)/shard_map/gate_up/pallas_call | solution.py:89
  105.9 7.4 %gate_up.13 = (f32[2,96,2048]{2,1,0:T(8,128)S(1)}, bf16[2,96,2048]{2,1,0:T(8,128)(2,1)S(1)}) custom-call(bf16[48,2048]{1,0:T(8,128)(2,1)S(1)} %collective-permute-done.32.x0, bf16[48,2048]{1,0:T(8,128)(2,1)S(1)} %collective-permute-done.33.x1, bf16[48,2048]{1,0:T(8,128)(2,1)S(1)} %collective-permute-done.34.x2, ...), custom_call_target="tpu_custom_call" | custom-call | flops 3221225472 | bytes 16777216 | tf_op jit(solution)/shard_map/gate_up/pallas_call | solution.py:89
  114.7 7.5 %gate_up.12 = (f32[2,96,2048]{2,1,0:T(8,128)S(1)}, bf16[2,96,2048]{2,1,0:T(8,128)(2,1)S(1)}) custom-call(bf16[48,2048]{1,0:T(8,128)(2,1)S(1)} %collective-permute-done.32.x0, bf16[48,2048]{1,0:T(8,128)(2,1)S(1)} %collective-permute-done.33.x1, bf16[48,2048]{1,0:T(8,128)(2,1)S(1)} %collective-permute-done.34.x2, ...), custom_call_target="tpu_custom_call" | custom-call | flops 3221225472 | bytes 16777216 | tf_op jit(solution)/shard_map/gate_up/pallas_call | solution.py:89
  122.1 2.0 collective-permute-start.36
  125.3 8.6 %collective-permute-done.40 = bf16[2,96,2048]{2,1,0:T(8,128)(2,1)S(1)} collective-permute-done((bf16[2,96,2048]{2,1,0:T(8,128)(2,1)S(1)}, bf16[2,96,2048]{2,1,0:T(8,128)(2,1)S(1)}, u32[]{:S(2)}, u32[]{:S(2)}) %collective-permute-start.40) | collective-permute-done | bytes 786464 | tf_op jit(solution)/shard_map/ppermute | solution.py:29
  135.3 7.4 %collective-permute-done.36 = bf16[2,96,2048]{2,1,0:T(8,128)(2,1)S(1)} collective-permute-done((bf16[2,96,2048]{2,1,0:T(8,128)(2,1)S(1)}, bf16[2,96,2048]{2,1,0:T(8,128)(2,1)S(1)}, u32[]{:S(2)}, u32[]{:S(2)}) %collective-permute-start.36) | collective-permute-done | bytes 786464 | tf_op jit(solution)/shard_map/ppermute | solution.py:29
  143.6 7.5 %collective-permute-done.12 = bf16[2,48,2048]{2,1,0:T(8,128)(2,1)S(1)} collective-permute-done((bf16[2,48,2048]{2,1,0:T(8,128)(2,1)S(1)}, bf16[2,48,2048]{2,1,0:T(8,128)(2,1)S(1)}, u32[]{:S(2)}, u32[]{:S(2)}) %collective-permute-start.12) | collective-permute-done | bytes 393248 | tf_op jit(solution)/shard_map/ppermute | solution.py:29
  153.8 5.7 %collective-permute-done.41 = bf16[2,48,2048]{2,1,0:T(8,128)(2,1)S(1)} collective-permute-done((bf16[2,48,2048]{2,1,0:T(8,128)(2,1)S(1)}, bf16[2,48,2048]{2,1,0:T(8,128)(2,1)S(1)}, u32[]{:S(2)}, u32[]{:S(2)}) %collective-permute-start.41) | collective-permute-done | bytes 393248 | tf_op jit(solution)/shard_map/ppermute | solution.py:29
  159.8 2.0 collective-permute-start.15
  161.9 4.0 collective-permute-done.13.x1
  168.0 3.6 collective-permute-done.16.x3b
  171.6 8.7 %down.4 = bf16[4,48,2048]{2,1,0:T(8,128)(2,1)} custom-call(bf16[48,4096]{1,0:T(8,128)(2,1)S(1)} %pad_maximum_fusion.x0, bf16[48,4096]{1,0:T(8,128)(2,1)S(1)} %collective-permute-done.13.x1, bf16[48,4096]{1,0:T(8,128)(2,1)S(1)} %collective-permute-done.14.x2, bf16[48,2048]{1,0:T(8,128)(2,1)S(1)} %collective-permute-done.15.x3a, ...), custom_call_target="tpu_custom_call" | custom-call | flops 3221225472 | bytes 16777216 | tf_op jit(solution)/shard_map/down/pallas_call | solution.py:152
  180.4 4.0 all-to-all-start.2
  186.5 7.9 %collective-permute-done.43.x2 = bf16[48,4096]{1,0:T(8,128)(2,1)S(1)} collective-permute-done((bf16[48,4096]{1,0:T(8,128)(2,1)S(1)}, bf16[48,4096]{1,0:T(8,128)(2,1)S(1)}, u32[]{:S(2)}, u32[]{:S(2)}) %collective-permute-start.43) | collective-permute-done | bytes 393248 | tf_op jit(solution)/shard_map/ppermute | solution.py:29
  196.5 3.6 collective-permute-done.44.x3a
  201.1 8.8 %down.6 = bf16[4,48,2048]{2,1,0:T(8,128)(2,1)} custom-call(bf16[48,4096]{1,0:T(8,128)(2,1)S(1)} %pad_maximum_fusion.2.x0, bf16[48,4096]{1,0:T(8,128)(2,1)S(1)} %collective-permute-done.42.x1, bf16[48,4096]{1,0:T(8,128)(2,1)S(1)} %collective-permute-done.43.x2, bf16[48,2048]{1,0:T(8,128)(2,1)S(1)} %collective-permute-done.44.x3a, ...), custom_call_target="tpu_custom_call" | custom-call | flops 3221225472 | bytes 16777216 | tf_op jit(solution)/shard_map/down/pallas_call | solution.py:152
  209.9 4.8 %all-to-all-start.4 = ((bf16[4,48,2048]{2,1,0:T(8,128)(2,1)}), bf16[4,48,2048]{2,1,0:T(8,128)(2,1)S(1)}, u32[]{:S(2)}, u32[]{:S(2)}) async-start(bf16[4,48,2048]{2,1,0:T(8,128)(2,1)} %down.6), calls=%async_computation.4 | async-start | bytes 1572864 | tf_op jit(solution)/shard_map/all_to_all | solution.py:37
  215.0 2.1 collective-permute-start.18
  217.1 2.4 collective-permute-start.19
  219.5 25.2 %all-to-all-done.4 = bf16[4,48,2048]{2,1,0:T(8,128)(2,1)S(1)} async-done(((bf16[4,48,2048]{2,1,0:T(8,128)(2,1)}), bf16[4,48,2048]{2,1,0:T(8,128)(2,1)S(1)}, u32[]{:S(2)}, u32[]{:S(2)}) %all-to-all-start.4) | async-done | bytes 786464 | tf_op jit(solution)/shard_map/all_to_all | solution.py:37
  246.1 3.4 collective-permute-start.48
  249.5 7.5 %gate_up.11 = (f32[2,96,2048]{2,1,0:T(8,128)S(1)}, bf16[2,96,2048]{2,1,0:T(8,128)(2,1)S(1)}) custom-call(bf16[48,2048]{1,0:T(8,128)(2,1)S(1)} %get-tuple-element.52.x0, bf16[48,2048]{1,0:T(8,128)(2,1)S(1)} %collective-permute-done.18.x1, bf16[48,2048]{1,0:T(8,128)(2,1)S(1)} %collective-permute-done.19.x2, bf16[48,2048]{1,0:T(8,128)(2,1)S(1)} %collective-permute-done.20.x3, ...), custom_call_target="tpu_custom_call" | custom-call | flops 3221225472 | bytes 16777216 | tf_op jit(solution)/shard_map/gate_up/pallas_call | solution.py:89
  257.5 2.1 collective-permute-start.23
  259.7 7.5 %gate_up.10 = (f32[2,96,2048]{2,1,0:T(8,128)S(1)}, bf16[2,96,2048]{2,1,0:T(8,128)(2,1)S(1)}) custom-call(bf16[48,2048]{1,0:T(8,128)(2,1)S(1)} %get-tuple-element.52.x0, bf16[48,2048]{1,0:T(8,128)(2,1)S(1)} %collective-permute-done.18.x1, bf16[48,2048]{1,0:T(8,128)(2,1)S(1)} %collective-permute-done.19.x2, bf16[48,2048]{1,0:T(8,128)(2,1)S(1)} %collective-permute-done.20.x3, ...), custom_call_target="tpu_custom_call" | custom-call | flops 3221225472 | bytes 16777216 | tf_op jit(solution)/shard_map/gate_up/pallas_call | solution.py:89
  267.2 7.5 %gate_up.15 = (f32[2,96,2048]{2,1,0:T(8,128)S(1)}, bf16[2,96,2048]{2,1,0:T(8,128)(2,1)S(1)}) custom-call(bf16[48,2048]{1,0:T(8,128)(2,1)S(1)} %get-tuple-element.54.x0, bf16[48,2048]{1,0:T(8,128)(2,1)S(1)} %collective-permute-done.46.x1, bf16[48,2048]{1,0:T(8,128)(2,1)S(1)} %collective-permute-done.47.x2, bf16[48,2048]{1,0:T(8,128)(2,1)S(1)} %collective-permute-done.48.x3, ...), custom_call_target="tpu_custom_call" | custom-call | flops 3221225472 | bytes 16777216 | tf_op jit(solution)/shard_map/gate_up/pallas_call | solution.py:89
  274.7 2.0 collective-permute-start.53
  277.4 7.5 %gate_up.14 = (f32[2,96,2048]{2,1,0:T(8,128)S(1)}, bf16[2,96,2048]{2,1,0:T(8,128)(2,1)S(1)}) custom-call(bf16[48,2048]{1,0:T(8,128)(2,1)S(1)} %get-tuple-element.54.x0, bf16[48,2048]{1,0:T(8,128)(2,1)S(1)} %collective-permute-done.46.x1, bf16[48,2048]{1,0:T(8,128)(2,1)S(1)} %collective-permute-done.47.x2, bf16[48,2048]{1,0:T(8,128)(2,1)S(1)} %collective-permute-done.48.x3, ...), custom_call_target="tpu_custom_call" | custom-call | flops 3221225472 | bytes 16777216 | tf_op jit(solution)/shard_map/gate_up/pallas_call | solution.py:89
  284.8 2.0 collective-permute-start.49
  287.8 7.6 %collective-permute-done.24 = f32[48]{0:T(128)S(1)} collective-permute-done((f32[48]{0:T(128)S(1)}, f32[48]{0:T(128)S(1)}, u32[]{:S(2)}, u32[]{:S(2)}) %collective-permute-start.24) | collective-permute-done | bytes 224 | tf_op jit(solution)/shard_map/ppermute | solution.py:29
  295.3 1.9 collective-permute-start.52
  299.0 2.0 collective-permute-start.26
  301.3 2.0 collective-permute-start.54
  303.3 2.1 collective-permute-done.49
  307.2 3.7 collective-permute-done.26
  315.4 4.1 collective-permute-done.28.x2
  322.0 3.3 collective-permute-done.29.x3a
  325.5 8.7 %down.5 = bf16[4,48,2048]{2,1,0:T(8,128)(2,1)} custom-call(bf16[48,4096]{1,0:T(8,128)(2,1)S(1)} %pad_maximum_fusion.1.x0, bf16[48,4096]{1,0:T(8,128)(2,1)S(1)} %collective-permute-done.27.x1, bf16[48,4096]{1,0:T(8,128)(2,1)S(1)} %collective-permute-done.28.x2, bf16[48,2048]{1,0:T(8,128)(2,1)S(1)} %collective-permute-done.29.x3a, ...), custom_call_target="tpu_custom_call" | custom-call | flops 3221225472 | bytes 16777216 | tf_op jit(solution)/shard_map/down/pallas_call | solution.py:152
  334.2 12.5 %all-to-all-start.3 = ((bf16[4,48,2048]{2,1,0:T(8,128)(2,1)}), bf16[4,48,2048]{2,1,0:T(8,128)(2,1)S(1)}, u32[]{:S(2)}, u32[]{:S(2)}) async-start(bf16[4,48,2048]{2,1,0:T(8,128)(2,1)} %down.5), calls=%async_computation.3 | async-start | bytes 1572864 | tf_op jit(solution)/shard_map/all_to_all | solution.py:37
  348.9 5.8 %collective-permute-done.56.x2 = bf16[48,4096]{1,0:T(8,128)(2,1)S(1)} collective-permute-done((bf16[48,4096]{1,0:T(8,128)(2,1)S(1)}, bf16[48,4096]{1,0:T(8,128)(2,1)S(1)}, u32[]{:S(2)}, u32[]{:S(2)}) %collective-permute-start.56) | collective-permute-done | bytes 393248 | tf_op jit(solution)/shard_map/ppermute | solution.py:29
  356.8 3.6 collective-permute-done.57.x3a
  361.3 8.8 %down.7 = bf16[4,48,2048]{2,1,0:T(8,128)(2,1)} custom-call(bf16[48,4096]{1,0:T(8,128)(2,1)S(1)} %pad_maximum_fusion.3.x0, bf16[48,4096]{1,0:T(8,128)(2,1)S(1)} %collective-permute-done.55.x1, bf16[48,4096]{1,0:T(8,128)(2,1)S(1)} %collective-permute-done.56.x2, bf16[48,2048]{1,0:T(8,128)(2,1)S(1)} %collective-permute-done.57.x3a, ...), custom_call_target="tpu_custom_call" | custom-call | flops 3221225472 | bytes 16777216 | tf_op jit(solution)/shard_map/down/pallas_call | solution.py:152
  370.1 5.1 %all-to-all-start.5 = ((bf16[4,48,2048]{2,1,0:T(8,128)(2,1)}), bf16[4,48,2048]{2,1,0:T(8,128)(2,1)S(1)}, u32[]{:S(2)}, u32[]{:S(2)}) async-start(bf16[4,48,2048]{2,1,0:T(8,128)(2,1)} %down.7), calls=%async_computation.5 | async-start | bytes 1572864 | tf_op jit(solution)/shard_map/all_to_all | solution.py:37
  375.5 4.7 %collective-permute-start.31 = (bf16[48,2048]{1,0:T(8,128)(2,1)S(1)}, bf16[48,2048]{1,0:T(8,128)(2,1)S(1)}, u32[]{:S(2)}, u32[]{:S(2)}) collective-permute-start(bf16[48,2048]{1,0:T(8,128)(2,1)S(1)} %fusion.17), channel_id=1, source_target_pairs={{0,0},{1,4},{2,8},{3,12},{4,1},{5,5},{6,9},{7,13},{8,2},{9,6},{10,... | collective-permute-start | bytes 589832 | tf_op jit(solution)/shard_map/ppermute | solution.py:25
  380.2 11.7 %all-to-all-done.5 = bf16[4,48,2048]{2,1,0:T(8,128)(2,1)S(1)} async-done(((bf16[4,48,2048]{2,1,0:T(8,128)(2,1)}), bf16[4,48,2048]{2,1,0:T(8,128)(2,1)S(1)}, u32[]{:S(2)}, u32[]{:S(2)}) %all-to-all-start.5) | async-done | bytes 786464 | tf_op jit(solution)/shard_map/all_to_all | solution.py:37
  392.1 1.9 collective-permute-start.59
  394.1 6.6 %collective-permute-done.31 = bf16[48,2048]{1,0:T(8,128)(2,1)S(1)} collective-permute-done((bf16[48,2048]{1,0:T(8,128)(2,1)S(1)}, bf16[48,2048]{1,0:T(8,128)(2,1)S(1)}, u32[]{:S(2)}, u32[]{:S(2)}) %collective-permute-start.31) | collective-permute-done | bytes 196640 | tf_op jit(solution)/shard_map/ppermute | solution.py:25
  400.7 2.1 collective-permute-done.59
  403.5 11.9 %all-gather.1 = f32[4,4,96]{2,1,0:T(4,128)S(1)} all-gather(f32[1,4,96]{2,1,0:T(4,128)S(1)} %maximum_bitcast_fusion), channel_id=2, replica_groups=mesh['section'=2,'dp'=4,'mp'=4] {'mp'}, dimensions={0}, use_global_device_ids=true | all-gather | bytes 7680 | tf_op jit(solution)/shard_map/all_gather | solution.py:285
  (194 shorter events, 48.3 us)
Async XLA Ops:
  0.6 89.3 %collective-permute-start.5 = (bf16[2048,4096]{1,0:T(8,128)(2,1)}, bf16[2048,4096]{1,0:T(8,128)(2,1)}, u32[]{:S(2)}, u32[]{:S(2)}) collective-permute-start(bf16[2048,4096]{1,0:T(8,128)(2,1)} %bitcast.232), channel_id=1, source_target_pairs={{0,16},{16,0},{1,17},{17,1},{2,18},{18,2},{3,19},{19,3},{4,20},{20... | collective-permute-start | bytes 50331656 | tf_op jit(solution)/shard_map/ppermute | solution.py:20
  0.7 89.2 %collective-permute-start.6 = (bf16[2048,4096]{1,0:T(8,128)(2,1)}, bf16[2048,4096]{1,0:T(8,128)(2,1)}, u32[]{:S(2)}, u32[]{:S(2)}) collective-permute-start(bf16[2048,4096]{1,0:T(8,128)(2,1)} %bitcast.241), channel_id=1, source_target_pairs={{0,16},{16,0},{1,17},{17,1},{2,18},{18,2},{3,19},{19,3},{4,20},{20... | collective-permute-start | bytes 50331656 | tf_op jit(solution)/shard_map/ppermute | solution.py:20
  2.6 8.2 %all-to-all-start.1 = ((bf16[4,1,1]{2,1,0:T(2,128)(2,1)}), bf16[4,1,1]{2,1,0:T(2,128)(2,1)S(1)}, u32[]{:S(2)}, u32[]{:S(2)}) async-start(bf16[4,1,1]{2,1,0:T(2,128)(2,1)} %copy.22), calls=%async_computation.1 | async-start | bytes 4096 | tf_op jit(solution)/shard_map/all_to_all | solution.py:235
  7.9 18.1 %collective-permute-start = (bf16[48,2048]{1,0:T(8,128)(2,1)S(1)}, bf16[48,2048]{1,0:T(8,128)(2,1)S(1)}, u32[]{:S(2)}, u32[]{:S(2)}) collective-permute-start(bf16[48,2048]{1,0:T(8,128)(2,1)S(1)} %get-tuple-element.56), channel_id=1, source_target_pairs={{0,0},{1,4},{2,8},{3,12},{4,1},{5,5},{6,9},{7,13},{8,2},{9,6},{10,... | collective-permute-start | bytes 589832 | tf_op jit(solution)/shard_map/ppermute | solution.py:25
  10.8 19.5 %all-to-all-start = ((bf16[4,48,2048]{2,1,0:T(8,128)(2,1)}), bf16[4,48,2048]{2,1,0:T(8,128)(2,1)S(1)}, u32[]{:S(2)}, u32[]{:S(2)}) async-start(bf16[4,48,2048]{2,1,0:T(8,128)(2,1)} %bitcast.256), calls=%async_computation | async-start | bytes 1572864 | tf_op jit(solution)/shard_map/all_to_all | solution.py:232
  25.9 8.7 %collective-permute-start.1 = (bf16[48,2048]{1,0:T(8,128)(2,1)S(1)}, bf16[48,2048]{1,0:T(8,128)(2,1)S(1)}, u32[]{:S(2)}, u32[]{:S(2)}) collective-permute-start(bf16[48,2048]{1,0:T(8,128)(2,1)S(1)} %collective-permute-done.x0), channel_id=1, source_target_pairs={{0,1},{1,0},{2,3},{3,2},{4,5},{5,4},{6,7},{7,6},{8,9},{9,8},{10,11... | collective-permute-start | bytes 589832 | tf_op jit(solution)/shard_map/ppermute | solution.py:33
  25.9 16.6 %collective-permute-start.2 = (bf16[48,2048]{1,0:T(8,128)(2,1)S(1)}, bf16[48,2048]{1,0:T(8,128)(2,1)S(1)}, u32[]{:S(2)}, u32[]{:S(2)}) collective-permute-start(bf16[48,2048]{1,0:T(8,128)(2,1)S(1)} %collective-permute-done.x0), channel_id=1, source_target_pairs={{0,2},{1,3},{2,0},{3,1},{4,6},{5,7},{6,4},{7,5},{8,10},{9,11},{10,... | collective-permute-start | bytes 589832 | tf_op jit(solution)/shard_map/ppermute | solution.py:33
  28.0 14.5 %collective-permute-start.3 = (bf16[48,2048]{1,0:T(8,128)(2,1)S(1)}, bf16[48,2048]{1,0:T(8,128)(2,1)S(1)}, u32[]{:S(2)}, u32[]{:S(2)}) collective-permute-start(bf16[48,2048]{1,0:T(8,128)(2,1)S(1)} %collective-permute-done.x0), channel_id=1, source_target_pairs={{0,3},{1,2},{2,1},{3,0},{4,7},{5,6},{6,5},{7,4},{8,11},{9,10},{10,... | collective-permute-start | bytes 589832 | tf_op jit(solution)/shard_map/ppermute | solution.py:33
  42.5 125.5 %collective-permute-start.17 = (bf16[4096,2048]{1,0:T(8,128)(2,1)}, bf16[4096,2048]{1,0:T(8,128)(2,1)}, u32[]{:S(2)}, u32[]{:S(2)}) collective-permute-start(bf16[4096,2048]{1,0:T(8,128)(2,1)} %bitcast.250), channel_id=1, source_target_pairs={{0,16},{16,0},{1,17},{17,1},{2,18},{18,2},{3,19},{19,3},{4,20},{20... | collective-permute-start | bytes 50331656 | tf_op jit(solution)/shard_map/ppermute | solution.py:20
  42.5 18.5 %collective-permute-start.32 = (bf16[48,2048]{1,0:T(8,128)(2,1)S(1)}, bf16[48,2048]{1,0:T(8,128)(2,1)S(1)}, u32[]{:S(2)}, u32[]{:S(2)}) collective-permute-start(bf16[48,2048]{1,0:T(8,128)(2,1)S(1)} %get-tuple-element.55), channel_id=1, source_target_pairs={{0,0},{1,4},{2,8},{3,12},{4,1},{5,5},{6,9},{7,13},{8,2},{9,6},{10,... | collective-permute-start | bytes 589832 | tf_op jit(solution)/shard_map/ppermute | solution.py:25
  61.0 9.5 %collective-permute-start.33 = (bf16[48,2048]{1,0:T(8,128)(2,1)S(1)}, bf16[48,2048]{1,0:T(8,128)(2,1)S(1)}, u32[]{:S(2)}, u32[]{:S(2)}) collective-permute-start(bf16[48,2048]{1,0:T(8,128)(2,1)S(1)} %collective-permute-done.32.x0), channel_id=1, source_target_pairs={{0,1},{1,0},{2,3},{3,2},{4,5},{5,4},{6,7},{7,6},{8,9},{9,8},{10,11... | collective-permute-start | bytes 589832 | tf_op jit(solution)/shard_map/ppermute | solution.py:33
  61.1 17.2 %collective-permute-start.34 = (bf16[48,2048]{1,0:T(8,128)(2,1)S(1)}, bf16[48,2048]{1,0:T(8,128)(2,1)S(1)}, u32[]{:S(2)}, u32[]{:S(2)}) collective-permute-start(bf16[48,2048]{1,0:T(8,128)(2,1)S(1)} %collective-permute-done.32.x0), channel_id=1, source_target_pairs={{0,2},{1,3},{2,0},{3,1},{4,6},{5,7},{6,4},{7,5},{8,10},{9,11},{10,... | collective-permute-start | bytes 589832 | tf_op jit(solution)/shard_map/ppermute | solution.py:33
  70.5 7.9 %collective-permute-start.35 = (bf16[48,2048]{1,0:T(8,128)(2,1)S(1)}, bf16[48,2048]{1,0:T(8,128)(2,1)S(1)}, u32[]{:S(2)}, u32[]{:S(2)}) collective-permute-start(bf16[48,2048]{1,0:T(8,128)(2,1)S(1)} %collective-permute-done.32.x0), channel_id=1, source_target_pairs={{0,3},{1,2},{2,1},{3,0},{4,7},{5,6},{6,5},{7,4},{8,11},{9,10},{10,... | collective-permute-start | bytes 589832 | tf_op jit(solution)/shard_map/ppermute | solution.py:33
  78.6 3.6 collective-permute-start.38
  82.7 3.6 collective-permute-start.9
  82.8 3.6 collective-permute-start.39
  86.3 3.6 collective-permute-start.10
  97.5 26.7 %collective-permute-start.11 = (bf16[2,96,2048]{2,1,0:T(8,128)(2,1)S(1)}, bf16[2,96,2048]{2,1,0:T(8,128)(2,1)S(1)}, u32[]{:S(2)}, u32[]{:S(2)}) collective-permute-start(bf16[2,96,2048]{2,1,0:T(8,128)(2,1)S(1)} %get-tuple-element.31), channel_id=1, source_target_pairs={{0,8},{4,12},{8,0},{12,4},{1,9},{5,13},{9,1},{13,5},{2,10},{6,14},... | collective-permute-start | bytes 2359304 | tf_op jit(solution)/shard_map/ppermute | solution.py:29
  105.1 19.3 %collective-permute-start.7 = (bf16[2,96,2048]{2,1,0:T(8,128)(2,1)S(1)}, bf16[2,96,2048]{2,1,0:T(8,128)(2,1)S(1)}, u32[]{:S(2)}, u32[]{:S(2)}) collective-permute-start(bf16[2,96,2048]{2,1,0:T(8,128)(2,1)S(1)} %get-tuple-element.29), channel_id=1, source_target_pairs={{0,4},{4,0},{8,12},{12,8},{1,5},{5,1},{9,13},{13,9},{2,6},{6,2},{1... | collective-permute-start | bytes 2359304 | tf_op jit(solution)/shard_map/ppermute | solution.py:29
  113.4 20.5 %collective-permute-start.40 = (bf16[2,96,2048]{2,1,0:T(8,128)(2,1)S(1)}, bf16[2,96,2048]{2,1,0:T(8,128)(2,1)S(1)}, u32[]{:S(2)}, u32[]{:S(2)}) collective-permute-start(bf16[2,96,2048]{2,1,0:T(8,128)(2,1)S(1)} %get-tuple-element.40), channel_id=1, source_target_pairs={{0,8},{4,12},{8,0},{12,4},{1,9},{5,13},{9,1},{13,5},{2,10},{6,14},... | collective-permute-start | bytes 2359304 | tf_op jit(solution)/shard_map/ppermute | solution.py:29
  122.1 20.5 %collective-permute-start.36 = (bf16[2,96,2048]{2,1,0:T(8,128)(2,1)S(1)}, bf16[2,96,2048]{2,1,0:T(8,128)(2,1)S(1)}, u32[]{:S(2)}, u32[]{:S(2)}) collective-permute-start(bf16[2,96,2048]{2,1,0:T(8,128)(2,1)S(1)} %get-tuple-element.38), channel_id=1, source_target_pairs={{0,4},{4,0},{8,12},{12,8},{1,5},{5,1},{9,13},{13,9},{2,6},{6,2},{1... | collective-permute-start | bytes 2359304 | tf_op jit(solution)/shard_map/ppermute | solution.py:29
  124.3 26.8 %collective-permute-start.12 = (bf16[2,48,2048]{2,1,0:T(8,128)(2,1)S(1)}, bf16[2,48,2048]{2,1,0:T(8,128)(2,1)S(1)}, u32[]{:S(2)}, u32[]{:S(2)}) collective-permute-start(bf16[2,48,2048]{2,1,0:T(8,128)(2,1)S(1)} %add_convert_fusion.6), channel_id=1, source_target_pairs={{0,4},{4,0},{8,12},{12,8},{1,5},{5,1},{9,13},{13,9},{2,6},{6,2},{1... | collective-permute-start | bytes 1179656 | tf_op jit(solution)/shard_map/ppermute | solution.py:29
  124.5 26.8 %collective-permute-start.8 = (bf16[2,48,2048]{2,1,0:T(8,128)(2,1)S(1)}, bf16[2,48,2048]{2,1,0:T(8,128)(2,1)S(1)}, u32[]{:S(2)}, u32[]{:S(2)}) collective-permute-start(bf16[2,48,2048]{2,1,0:T(8,128)(2,1)S(1)} %add_convert_fusion.7), channel_id=1, source_target_pairs={{0,8},{4,12},{8,0},{12,4},{1,9},{5,13},{9,1},{13,5},{2,10},{6,14},... | collective-permute-start | bytes 1179656 | tf_op jit(solution)/shard_map/ppermute | solution.py:29
  134.0 25.5 %collective-permute-start.41 = (bf16[2,48,2048]{2,1,0:T(8,128)(2,1)S(1)}, bf16[2,48,2048]{2,1,0:T(8,128)(2,1)S(1)}, u32[]{:S(2)}, u32[]{:S(2)}) collective-permute-start(bf16[2,48,2048]{2,1,0:T(8,128)(2,1)S(1)} %add_convert_fusion.2), channel_id=1, source_target_pairs={{0,4},{4,0},{8,12},{12,8},{1,5},{5,1},{9,13},{13,9},{2,6},{6,2},{1... | collective-permute-start | bytes 1179656 | tf_op jit(solution)/shard_map/ppermute | solution.py:29
  142.8 16.9 %collective-permute-start.37 = (bf16[2,48,2048]{2,1,0:T(8,128)(2,1)S(1)}, bf16[2,48,2048]{2,1,0:T(8,128)(2,1)S(1)}, u32[]{:S(2)}, u32[]{:S(2)}) collective-permute-start(bf16[2,48,2048]{2,1,0:T(8,128)(2,1)S(1)} %add_convert_fusion.3), channel_id=1, source_target_pairs={{0,8},{4,12},{8,0},{12,4},{1,9},{5,13},{9,1},{13,5},{2,10},{6,14},... | collective-permute-start | bytes 1179656 | tf_op jit(solution)/shard_map/ppermute | solution.py:29
  151.7 8.1 %collective-permute-start.14 = (bf16[48,4096]{1,0:T(8,128)(2,1)S(1)}, bf16[48,4096]{1,0:T(8,128)(2,1)S(1)}, u32[]{:S(2)}, u32[]{:S(2)}) collective-permute-start(bf16[48,4096]{1,0:T(8,128)(2,1)S(1)} %pad_maximum_fusion.x0), channel_id=1, source_target_pairs={{0,8},{4,12},{8,0},{12,4},{1,9},{5,13},{9,1},{13,5},{2,10},{6,14},... | collective-permute-start | bytes 1179656 | tf_op jit(solution)/shard_map/ppermute | solution.py:29
  152.6 13.3 %collective-permute-start.13 = (bf16[48,4096]{1,0:T(8,128)(2,1)S(1)}, bf16[48,4096]{1,0:T(8,128)(2,1)S(1)}, u32[]{:S(2)}, u32[]{:S(2)}) collective-permute-start(bf16[48,4096]{1,0:T(8,128)(2,1)S(1)} %pad_maximum_fusion.x0), channel_id=1, source_target_pairs={{0,4},{4,0},{8,12},{12,8},{1,5},{5,1},{9,13},{13,9},{2,6},{6,2},{1... | collective-permute-start | bytes 1179656 | tf_op jit(solution)/shard_map/ppermute | solution.py:29
  159.8 8.2 %collective-permute-start.15 = (bf16[48,2048]{1,0:T(8,128)(2,1)S(1)}, bf16[48,2048]{1,0:T(8,128)(2,1)S(1)}, u32[]{:S(2)}, u32[]{:S(2)}) collective-permute-start(bf16[48,2048]{1,0:T(8,128)(2,1)S(1)} %slice.274), channel_id=1, source_target_pairs={{0,4},{4,0},{8,12},{12,8},{1,5},{5,1},{9,13},{13,9},{2,6},{6,2},{1... | collective-permute-start | bytes 589832 | tf_op jit(solution)/shard_map/ppermute | solution.py:29
  165.9 5.7 %collective-permute-start.16 = (bf16[48,2048]{1,0:T(8,128)(2,1)S(1)}, bf16[48,2048]{1,0:T(8,128)(2,1)S(1)}, u32[]{:S(2)}, u32[]{:S(2)}) collective-permute-start(bf16[48,2048]{1,0:T(8,128)(2,1)S(1)} %slice.275), channel_id=1, source_target_pairs={{0,8},{4,12},{8,0},{12,4},{1,9},{5,13},{9,1},{13,5},{2,10},{6,14},... | collective-permute-start | bytes 589832 | tf_op jit(solution)/shard_map/ppermute | solution.py:29
  180.4 29.5 %all-to-all-start.2 = ((bf16[4,48,2048]{2,1,0:T(8,128)(2,1)}), bf16[4,48,2048]{2,1,0:T(8,128)(2,1)S(1)}, u32[]{:S(2)}, u32[]{:S(2)}) async-start(bf16[4,48,2048]{2,1,0:T(8,128)(2,1)} %down.4), calls=%async_computation.2 | async-start | bytes 1572864 | tf_op jit(solution)/shard_map/all_to_all | solution.py:37
  184.4 9.9 %collective-permute-start.43 = (bf16[48,4096]{1,0:T(8,128)(2,1)S(1)}, bf16[48,4096]{1,0:T(8,128)(2,1)S(1)}, u32[]{:S(2)}, u32[]{:S(2)}) collective-permute-start(bf16[48,4096]{1,0:T(8,128)(2,1)S(1)} %pad_maximum_fusion.2.x0), channel_id=1, source_target_pairs={{0,8},{4,12},{8,0},{12,4},{1,9},{5,13},{9,1},{13,5},{2,10},{6,14},... | collective-permute-start | bytes 1179656 | tf_op jit(solution)/shard_map/ppermute | solution.py:29
  186.2 9.2 %collective-permute-start.42 = (bf16[48,4096]{1,0:T(8,128)(2,1)S(1)}, bf16[48,4096]{1,0:T(8,128)(2,1)S(1)}, u32[]{:S(2)}, u32[]{:S(2)}) collective-permute-start(bf16[48,4096]{1,0:T(8,128)(2,1)S(1)} %pad_maximum_fusion.2.x0), channel_id=1, source_target_pairs={{0,4},{4,0},{8,12},{12,8},{1,5},{5,1},{9,13},{13,9},{2,6},{6,2},{1... | collective-permute-start | bytes 1179656 | tf_op jit(solution)/shard_map/ppermute | solution.py:29
  194.4 5.7 %collective-permute-start.44 = (bf16[48,2048]{1,0:T(8,128)(2,1)S(1)}, bf16[48,2048]{1,0:T(8,128)(2,1)S(1)}, u32[]{:S(2)}, u32[]{:S(2)}) collective-permute-start(bf16[48,2048]{1,0:T(8,128)(2,1)S(1)} %slice.294), channel_id=1, source_target_pairs={{0,4},{4,0},{8,12},{12,8},{1,5},{5,1},{9,13},{13,9},{2,6},{6,2},{1... | collective-permute-start | bytes 589832 | tf_op jit(solution)/shard_map/ppermute | solution.py:29
  195.4 5.7 %collective-permute-start.45 = (bf16[48,2048]{1,0:T(8,128)(2,1)S(1)}, bf16[48,2048]{1,0:T(8,128)(2,1)S(1)}, u32[]{:S(2)}, u32[]{:S(2)}) collective-permute-start(bf16[48,2048]{1,0:T(8,128)(2,1)S(1)} %slice.295), channel_id=1, source_target_pairs={{0,8},{4,12},{8,0},{12,4},{1,9},{5,13},{9,1},{13,5},{2,10},{6,14},... | collective-permute-start | bytes 589832 | tf_op jit(solution)/shard_map/ppermute | solution.py:29
  209.9 34.8 %all-to-all-start.4 = ((bf16[4,48,2048]{2,1,0:T(8,128)(2,1)}), bf16[4,48,2048]{2,1,0:T(8,128)(2,1)S(1)}, u32[]{:S(2)}, u32[]{:S(2)}) async-start(bf16[4,48,2048]{2,1,0:T(8,128)(2,1)} %down.6), calls=%async_computation.4 | async-start | bytes 1572864 | tf_op jit(solution)/shard_map/all_to_all | solution.py:37
  215.0 31.1 %collective-permute-start.18 = (bf16[48,2048]{1,0:T(8,128)(2,1)S(1)}, bf16[48,2048]{1,0:T(8,128)(2,1)S(1)}, u32[]{:S(2)}, u32[]{:S(2)}) collective-permute-start(bf16[48,2048]{1,0:T(8,128)(2,1)S(1)} %get-tuple-element.52.x0), channel_id=1, source_target_pairs={{0,1},{1,0},{2,3},{3,2},{4,5},{5,4},{6,7},{7,6},{8,9},{9,8},{10,11... | collective-permute-start | bytes 589832 | tf_op jit(solution)/shard_map/ppermute | solution.py:33
  217.1 32.4 %collective-permute-start.19 = (bf16[48,2048]{1,0:T(8,128)(2,1)S(1)}, bf16[48,2048]{1,0:T(8,128)(2,1)S(1)}, u32[]{:S(2)}, u32[]{:S(2)}) collective-permute-start(bf16[48,2048]{1,0:T(8,128)(2,1)S(1)} %get-tuple-element.52.x0), channel_id=1, source_target_pairs={{0,2},{1,3},{2,0},{3,1},{4,6},{5,7},{6,4},{7,5},{8,10},{9,11},{10,... | collective-permute-start | bytes 589832 | tf_op jit(solution)/shard_map/ppermute | solution.py:33
  219.4 30.1 %collective-permute-start.20 = (bf16[48,2048]{1,0:T(8,128)(2,1)S(1)}, bf16[48,2048]{1,0:T(8,128)(2,1)S(1)}, u32[]{:S(2)}, u32[]{:S(2)}) collective-permute-start(bf16[48,2048]{1,0:T(8,128)(2,1)S(1)} %get-tuple-element.52.x0), channel_id=1, source_target_pairs={{0,3},{1,2},{2,1},{3,0},{4,7},{5,6},{6,5},{7,4},{8,11},{9,10},{10,... | collective-permute-start | bytes 589832 | tf_op jit(solution)/shard_map/ppermute | solution.py:33
  245.0 22.1 %collective-permute-start.46 = (bf16[48,2048]{1,0:T(8,128)(2,1)S(1)}, bf16[48,2048]{1,0:T(8,128)(2,1)S(1)}, u32[]{:S(2)}, u32[]{:S(2)}) collective-permute-start(bf16[48,2048]{1,0:T(8,128)(2,1)S(1)} %get-tuple-element.54.x0), channel_id=1, source_target_pairs={{0,1},{1,0},{2,3},{3,2},{4,5},{5,4},{6,7},{7,6},{8,9},{9,8},{10,11... | collective-permute-start | bytes 589832 | tf_op jit(solution)/shard_map/ppermute | solution.py:33
  245.1 22.1 %collective-permute-start.47 = (bf16[48,2048]{1,0:T(8,128)(2,1)S(1)}, bf16[48,2048]{1,0:T(8,128)(2,1)S(1)}, u32[]{:S(2)}, u32[]{:S(2)}) collective-permute-start(bf16[48,2048]{1,0:T(8,128)(2,1)S(1)} %get-tuple-element.54.x0), channel_id=1, source_target_pairs={{0,2},{1,3},{2,0},{3,1},{4,6},{5,7},{6,4},{7,5},{8,10},{9,11},{10,... | collective-permute-start | bytes 589832 | tf_op jit(solution)/shard_map/ppermute | solution.py:33
  246.1 21.1 %collective-permute-start.48 = (bf16[48,2048]{1,0:T(8,128)(2,1)S(1)}, bf16[48,2048]{1,0:T(8,128)(2,1)S(1)}, u32[]{:S(2)}, u32[]{:S(2)}) collective-permute-start(bf16[48,2048]{1,0:T(8,128)(2,1)S(1)} %get-tuple-element.54.x0), channel_id=1, source_target_pairs={{0,3},{1,2},{2,1},{3,0},{4,7},{5,6},{6,5},{7,4},{8,11},{9,10},{10,... | collective-permute-start | bytes 589832 | tf_op jit(solution)/shard_map/ppermute | solution.py:33
  257.0 41.9 %collective-permute-start.25 = (bf16[2,96,2048]{2,1,0:T(8,128)(2,1)S(1)}, bf16[2,96,2048]{2,1,0:T(8,128)(2,1)S(1)}, u32[]{:S(2)}, u32[]{:S(2)}) collective-permute-start(bf16[2,96,2048]{2,1,0:T(8,128)(2,1)S(1)} %get-tuple-element.36), channel_id=1, source_target_pairs={{0,8},{4,12},{8,0},{12,4},{1,9},{5,13},{9,1},{13,5},{2,10},{6,14},... | collective-permute-start | bytes 2359304 | tf_op jit(solution)/shard_map/ppermute | solution.py:29
  257.5 27.3 %collective-permute-start.23 = (f32[2,48]{1,0:T(2,128)S(1)}, f32[2,48]{1,0:T(2,128)S(1)}, u32[]{:S(2)}, u32[]{:S(2)}) collective-permute-start(f32[2,48]{1,0:T(2,128)S(1)} %pad_maximum_fusion.10), channel_id=1, source_target_pairs={{0,4},{4,0},{8,12},{12,8},{1,5},{5,1},{9,13},{13,9},{2,6},{6,2},{1... | collective-permute-start | bytes 1160 | tf_op jit(solution)/shard_map/ppermute | solution.py:29
  267.1 33.9 %collective-permute-start.21 = (bf16[2,96,2048]{2,1,0:T(8,128)(2,1)S(1)}, bf16[2,96,2048]{2,1,0:T(8,128)(2,1)S(1)}, u32[]{:S(2)}, u32[]{:S(2)}) collective-permute-start(bf16[2,96,2048]{2,1,0:T(8,128)(2,1)S(1)} %get-tuple-element.34), channel_id=1, source_target_pairs={{0,4},{4,0},{8,12},{12,8},{1,5},{5,1},{9,13},{13,9},{2,6},{6,2},{1... | collective-permute-start | bytes 2359304 | tf_op jit(solution)/shard_map/ppermute | solution.py:29
  274.7 26.5 %collective-permute-start.53 = (bf16[2,96,2048]{2,1,0:T(8,128)(2,1)S(1)}, bf16[2,96,2048]{2,1,0:T(8,128)(2,1)S(1)}, u32[]{:S(2)}, u32[]{:S(2)}) collective-permute-start(bf16[2,96,2048]{2,1,0:T(8,128)(2,1)S(1)} %get-tuple-element.44), channel_id=1, source_target_pairs={{0,8},{4,12},{8,0},{12,4},{1,9},{5,13},{9,1},{13,5},{2,10},{6,14},... | collective-permute-start | bytes 2359304 | tf_op jit(solution)/shard_map/ppermute | solution.py:29
  277.2 10.5 %collective-permute-start.51 = (f32[2,48]{1,0:T(2,128)S(1)}, f32[2,48]{1,0:T(2,128)S(1)}, u32[]{:S(2)}, u32[]{:S(2)}) collective-permute-start(f32[2,48]{1,0:T(2,128)S(1)} %pad_maximum_fusion.12), channel_id=1, source_target_pairs={{0,4},{4,0},{8,12},{12,8},{1,5},{5,1},{9,13},{13,9},{2,6},{6,2},{1... | collective-permute-start | bytes 1160 | tf_op jit(solution)/shard_map/ppermute | solution.py:29
  284.8 20.5 %collective-permute-start.49 = (bf16[2,96,2048]{2,1,0:T(8,128)(2,1)S(1)}, bf16[2,96,2048]{2,1,0:T(8,128)(2,1)S(1)}, u32[]{:S(2)}, u32[]{:S(2)}) collective-permute-start(bf16[2,96,2048]{2,1,0:T(8,128)(2,1)S(1)} %get-tuple-element.42), channel_id=1, source_target_pairs={{0,4},{4,0},{8,12},{12,8},{1,5},{5,1},{9,13},{13,9},{2,6},{6,2},{1... | collective-permute-start | bytes 2359304 | tf_op jit(solution)/shard_map/ppermute | solution.py:29
  287.7 7.6 %collective-permute-start.24 = (f32[48]{0:T(128)S(1)}, f32[48]{0:T(128)S(1)}, u32[]{:S(2)}, u32[]{:S(2)}) collective-permute-start(f32[48]{0:T(128)S(1)} %slice_bitcast_fusion.20), channel_id=1, source_target_pairs={{0,8},{4,12},{8,0},{12,4},{1,9},{5,13},{9,1},{13,5},{2,10},{6,14},... | collective-permute-start | bytes 584 | tf_op jit(solution)/shard_map/ppermute | solution.py:29
  299.0 11.9 %collective-permute-start.26 = (bf16[2,48,2048]{2,1,0:T(8,128)(2,1)S(1)}, bf16[2,48,2048]{2,1,0:T(8,128)(2,1)S(1)}, u32[]{:S(2)}, u32[]{:S(2)}) collective-permute-start(bf16[2,48,2048]{2,1,0:T(8,128)(2,1)S(1)} %add_convert_fusion.4), channel_id=1, source_target_pairs={{0,4},{4,0},{8,12},{12,8},{1,5},{5,1},{9,13},{13,9},{2,6},{6,2},{1... | collective-permute-start | bytes 1179656 | tf_op jit(solution)/shard_map/ppermute | solution.py:29
  301.1 9.9 %collective-permute-start.22 = (bf16[2,48,2048]{2,1,0:T(8,128)(2,1)S(1)}, bf16[2,48,2048]{2,1,0:T(8,128)(2,1)S(1)}, u32[]{:S(2)}, u32[]{:S(2)}) collective-permute-start(bf16[2,48,2048]{2,1,0:T(8,128)(2,1)S(1)} %add_convert_fusion.5), channel_id=1, source_target_pairs={{0,8},{4,12},{8,0},{12,4},{1,9},{5,13},{9,1},{13,5},{2,10},{6,14},... | collective-permute-start | bytes 1179656 | tf_op jit(solution)/shard_map/ppermute | solution.py:29
  301.3 13.8 %collective-permute-start.54 = (bf16[2,48,2048]{2,1,0:T(8,128)(2,1)S(1)}, bf16[2,48,2048]{2,1,0:T(8,128)(2,1)S(1)}, u32[]{:S(2)}, u32[]{:S(2)}) collective-permute-start(bf16[2,48,2048]{2,1,0:T(8,128)(2,1)S(1)} %add_convert_fusion), channel_id=1, source_target_pairs={{0,4},{4,0},{8,12},{12,8},{1,5},{5,1},{9,13},{13,9},{2,6},{6,2},{1... | collective-permute-start | bytes 1179656 | tf_op jit(solution)/shard_map/ppermute | solution.py:29
  305.5 9.8 %collective-permute-start.50 = (bf16[2,48,2048]{2,1,0:T(8,128)(2,1)S(1)}, bf16[2,48,2048]{2,1,0:T(8,128)(2,1)S(1)}, u32[]{:S(2)}, u32[]{:S(2)}) collective-permute-start(bf16[2,48,2048]{2,1,0:T(8,128)(2,1)S(1)} %add_convert_fusion.1), channel_id=1, source_target_pairs={{0,8},{4,12},{8,0},{12,4},{1,9},{5,13},{9,1},{13,5},{2,10},{6,14},... | collective-permute-start | bytes 1179656 | tf_op jit(solution)/shard_map/ppermute | solution.py:29
  311.5 8.0 %collective-permute-start.28 = (bf16[48,4096]{1,0:T(8,128)(2,1)S(1)}, bf16[48,4096]{1,0:T(8,128)(2,1)S(1)}, u32[]{:S(2)}, u32[]{:S(2)}) collective-permute-start(bf16[48,4096]{1,0:T(8,128)(2,1)S(1)} %pad_maximum_fusion.1.x0), channel_id=1, source_target_pairs={{0,8},{4,12},{8,0},{12,4},{1,9},{5,13},{9,1},{13,5},{2,10},{6,14},... | collective-permute-start | bytes 1179656 | tf_op jit(solution)/shard_map/ppermute | solution.py:29
  311.9 7.8 %collective-permute-start.27 = (bf16[48,4096]{1,0:T(8,128)(2,1)S(1)}, bf16[48,4096]{1,0:T(8,128)(2,1)S(1)}, u32[]{:S(2)}, u32[]{:S(2)}) collective-permute-start(bf16[48,4096]{1,0:T(8,128)(2,1)S(1)} %pad_maximum_fusion.1.x0), channel_id=1, source_target_pairs={{0,4},{4,0},{8,12},{12,8},{1,5},{5,1},{9,13},{13,9},{2,6},{6,2},{1... | collective-permute-start | bytes 1179656 | tf_op jit(solution)/shard_map/ppermute | solution.py:29
  319.5 5.7 %collective-permute-start.29 = (bf16[48,2048]{1,0:T(8,128)(2,1)S(1)}, bf16[48,2048]{1,0:T(8,128)(2,1)S(1)}, u32[]{:S(2)}, u32[]{:S(2)}) collective-permute-start(bf16[48,2048]{1,0:T(8,128)(2,1)S(1)} %slice.284), channel_id=1, source_target_pairs={{0,4},{4,0},{8,12},{12,8},{1,5},{5,1},{9,13},{13,9},{2,6},{6,2},{1... | collective-permute-start | bytes 589832 | tf_op jit(solution)/shard_map/ppermute | solution.py:29
  319.8 5.7 %collective-permute-start.30 = (bf16[48,2048]{1,0:T(8,128)(2,1)S(1)}, bf16[48,2048]{1,0:T(8,128)(2,1)S(1)}, u32[]{:S(2)}, u32[]{:S(2)}) collective-permute-start(bf16[48,2048]{1,0:T(8,128)(2,1)S(1)} %slice.285), channel_id=1, source_target_pairs={{0,8},{4,12},{8,0},{12,4},{1,9},{5,13},{9,1},{13,5},{2,10},{6,14},... | collective-permute-start | bytes 589832 | tf_op jit(solution)/shard_map/ppermute | solution.py:29
  334.2 35.8 %all-to-all-start.3 = ((bf16[4,48,2048]{2,1,0:T(8,128)(2,1)}), bf16[4,48,2048]{2,1,0:T(8,128)(2,1)S(1)}, u32[]{:S(2)}, u32[]{:S(2)}) async-start(bf16[4,48,2048]{2,1,0:T(8,128)(2,1)} %down.5), calls=%async_computation.3 | async-start | bytes 1572864 | tf_op jit(solution)/shard_map/all_to_all | solution.py:37
  346.8 7.8 %collective-permute-start.56 = (bf16[48,4096]{1,0:T(8,128)(2,1)S(1)}, bf16[48,4096]{1,0:T(8,128)(2,1)S(1)}, u32[]{:S(2)}, u32[]{:S(2)}) collective-permute-start(bf16[48,4096]{1,0:T(8,128)(2,1)S(1)} %pad_maximum_fusion.3.x0), channel_id=1, source_target_pairs={{0,8},{4,12},{8,0},{12,4},{1,9},{5,13},{9,1},{13,5},{2,10},{6,14},... | collective-permute-start | bytes 1179656 | tf_op jit(solution)/shard_map/ppermute | solution.py:29
  347.6 7.9 %collective-permute-start.55 = (bf16[48,4096]{1,0:T(8,128)(2,1)S(1)}, bf16[48,4096]{1,0:T(8,128)(2,1)S(1)}, u32[]{:S(2)}, u32[]{:S(2)}) collective-permute-start(bf16[48,4096]{1,0:T(8,128)(2,1)S(1)} %pad_maximum_fusion.3.x0), channel_id=1, source_target_pairs={{0,4},{4,0},{8,12},{12,8},{1,5},{5,1},{9,13},{13,9},{2,6},{6,2},{1... | collective-permute-start | bytes 1179656 | tf_op jit(solution)/shard_map/ppermute | solution.py:29
  354.6 5.7 %collective-permute-start.57 = (bf16[48,2048]{1,0:T(8,128)(2,1)S(1)}, bf16[48,2048]{1,0:T(8,128)(2,1)S(1)}, u32[]{:S(2)}, u32[]{:S(2)}) collective-permute-start(bf16[48,2048]{1,0:T(8,128)(2,1)S(1)} %slice.304), channel_id=1, source_target_pairs={{0,4},{4,0},{8,12},{12,8},{1,5},{5,1},{9,13},{13,9},{2,6},{6,2},{1... | collective-permute-start | bytes 589832 | tf_op jit(solution)/shard_map/ppermute | solution.py:29
  355.5 5.7 %collective-permute-start.58 = (bf16[48,2048]{1,0:T(8,128)(2,1)S(1)}, bf16[48,2048]{1,0:T(8,128)(2,1)S(1)}, u32[]{:S(2)}, u32[]{:S(2)}) collective-permute-start(bf16[48,2048]{1,0:T(8,128)(2,1)S(1)} %slice.305), channel_id=1, source_target_pairs={{0,8},{4,12},{8,0},{12,4},{1,9},{5,13},{9,1},{13,5},{2,10},{6,14},... | collective-permute-start | bytes 589832 | tf_op jit(solution)/shard_map/ppermute | solution.py:29
  370.1 21.8 %all-to-all-start.5 = ((bf16[4,48,2048]{2,1,0:T(8,128)(2,1)}), bf16[4,48,2048]{2,1,0:T(8,128)(2,1)S(1)}, u32[]{:S(2)}, u32[]{:S(2)}) async-start(bf16[4,48,2048]{2,1,0:T(8,128)(2,1)} %down.7), calls=%async_computation.5 | async-start | bytes 1572864 | tf_op jit(solution)/shard_map/all_to_all | solution.py:37
  375.5 25.2 %collective-permute-start.31 = (bf16[48,2048]{1,0:T(8,128)(2,1)S(1)}, bf16[48,2048]{1,0:T(8,128)(2,1)S(1)}, u32[]{:S(2)}, u32[]{:S(2)}) collective-permute-start(bf16[48,2048]{1,0:T(8,128)(2,1)S(1)} %fusion.17), channel_id=1, source_target_pairs={{0,0},{1,4},{2,8},{3,12},{4,1},{5,5},{6,9},{7,13},{8,2},{9,6},{10,... | collective-permute-start | bytes 589832 | tf_op jit(solution)/shard_map/ppermute | solution.py:25
  392.1 10.7 %collective-permute-start.59 = (bf16[48,2048]{1,0:T(8,128)(2,1)S(1)}, bf16[48,2048]{1,0:T(8,128)(2,1)S(1)}, u32[]{:S(2)}, u32[]{:S(2)}) collective-permute-start(bf16[48,2048]{1,0:T(8,128)(2,1)S(1)} %fusion.21), channel_id=1, source_target_pairs={{0,0},{1,4},{2,8},{3,12},{4,1},{5,5},{6,9},{7,13},{8,2},{9,6},{10,... | collective-permute-start | bytes 589832 | tf_op jit(solution)/shard_map/ppermute | solution.py:25
  (7 other events, 140.3 us)

commit v2 on v1

--- a/solution.py
+++ b/solution.py
@@ -12,7 +12,7 @@
 EPSILON = 1e-05
 AXES = ("section", "dp", "mp")
 TILE = 512
-HALVES = 2
+COST = 1
 VMEM_LIMIT = 40 * 1024 * 1024
 
 
@@ -42,11 +42,13 @@
     pl.when(jnp.logical_not(is_own))(start_other)
 
 
-def gate_up_kernel(number, first, swapped, x0, x1, x2, x3, gain_ref, gate0, up0, gate1, up1, keep_ref, send_ref, rows_ref, held, sems):
+def gate_up_kernel(number, first, swapped, relative, x0, x1, x2, x3, gain_ref, gate0, up0, gate1, up1, keep_ref, send_ref, rows_ref, held, sems):
     step = pl.program_id(0)
     steps = pl.num_programs(0)
     is_own = lax.axis_index("section") == number
-    own_place = lax.axis_index("dp") ^ lax.axis_index("mp")
+    own_place = lax.axis_index("dp")
+    if relative:
+        own_place = own_place ^ lax.axis_index("mp")
     count = x0.shape[0]
 
     def fetch(j, tile):
@@ -84,12 +86,18 @@
 
 def gate_up(number, first, width, swapped, rows, gain_row, own, received):
     groups = 4
+    relative = isinstance(rows, list)
     count, depth = rows[0].shape
     whole = lambda shape: pl.BlockSpec(shape, lambda t: (0,) * len(shape))
+    if relative:
+        piece_specs = [whole((count, depth))] * 4
+    else:
+        piece_specs = [pl.BlockSpec((None, count, depth), lambda t, k=k: (k, 0, 0)) for k in range(4)]
+        rows = [rows] * 4
     return pl.pallas_call(
-        functools.partial(gate_up_kernel, number, first, swapped),
+        functools.partial(gate_up_kernel, number, first, swapped, relative),
         grid=(width // TILE,),
-        in_specs=[whole((count, depth))] * 4 + [whole((1, depth))] + [pl.BlockSpec(memory_space=pl.ANY)] * 4,
+        in_specs=piece_specs + [whole((1, depth))] + [pl.BlockSpec(memory_space=pl.ANY)] * 4,
         out_specs=[pl.BlockSpec((2, 2 * count, TILE), lambda t: (0, 0, t))] * 2,
         out_shape=[
             jax.ShapeDtypeStruct((2, 2 * count, width), jnp.float32),
@@ -102,7 +110,9 @@
         ],
         compiler_params=pltpu.CompilerParams(vmem_limit_bytes=VMEM_LIMIT),
         cost_estimate=pl.CostEstimate(
-            flops=4 * groups * count * depth * width, bytes_accessed=4 * depth * width, transcendentals=0
+            flops=4 * groups * count * depth * width // COST,
+            bytes_accessed=4 * depth * width // COST,
+            transcendentals=0,
         ),
         name="gate_up",
     )(*rows, gain_row, *own, *received)
@@ -163,66 +173,109 @@
         ],
         compiler_params=pltpu.CompilerParams(vmem_limit_bytes=VMEM_LIMIT),
         cost_estimate=pl.CostEstimate(
-            flops=2 * groups * count * depth * features, bytes_accessed=2 * depth * features, transcendentals=0
+            flops=2 * groups * count * depth * features // COST,
+            bytes_accessed=2 * depth * features // COST,
+            transcendentals=0,
         ),
         name="down",
     )(*pieces, own, received)
 
 
-def sum_squares(rows):
-    squares = jnp.stack([jnp.sum(jnp.square(piece.astype(jnp.float32)), axis=-1) for piece in rows])
-    own_place = lax.axis_index("dp") ^ lax.axis_index("mp")
-    keep, send = [jnp.stack([squares[i ^ own_place] for i in pair]) for pair in ((0, 2), (1, 3))]
-    keep = keep + swap_dp(send, 1)
+def squares_by_place(rows):
+    squares = jnp.stack([jnp.sum(jnp.square(rows[k].astype(jnp.float32)), axis=-1) for k in range(4)])
+    own_place = lax.axis_index("dp")
+    if isinstance(rows, list):
+        own_place = own_place ^ lax.axis_index("mp")
+    return [squares[i ^ own_place] for i in range(4)]
+
+
+def tie(value, *earlier):
+    return lax.optimization_barrier((value, earlier))[0]
+
+
+def sum_squares(chunks, late):
+    places = [jnp.stack(pieces) for pieces in zip(*[squares_by_place(rows) for rows in chunks])]
+    keep, send = jnp.stack(places[0::2]), jnp.stack(places[1::2])
+    got = swap_dp(send, 1)
+    keep = keep + tie(got, late)
     return keep[0] + swap_dp(keep[1], 2)
 
 
-def stream(number, first, width, steps, rows, gain_row, own, received):
-    keep, send = gate_up(number, first, width, steps[0] == 1, rows, gain_row, own, received)
-    count = rows[0].shape[0]
-    got = swap_dp(send, steps[0])
+def sum_first(partial, step):
+    keep, send = partial
+    count = keep.shape[1] // 2
+    got = swap_dp(send, step)
     onward = (keep[:, count:] + got[:, count:].astype(jnp.float32)).astype(jnp.bfloat16)
-    last = swap_dp(onward, steps[1])
-    return keep[:, :count] + got[:, :count].astype(jnp.float32) + last.astype(jnp.float32)
+    return keep[:, :count], got[:, :count], onward
+
+
+def sum_second(state, step):
+    keep, got, onward = state
+    return keep + got.astype(jnp.float32) + swap_dp(onward, step).astype(jnp.float32)
 
 
 def enter(own):
     return [own] + [swap_mp(own, k) for k in (1, 2, 3)]
 
 
-def layer(number, own, rows, gain_row, weights, received):
-    half = weights[0].shape[1] // 2
-    scale = lax.rsqrt(sum_squares(rows) / D + EPSILON)[:, None]
-    args = (rows, gain_row, weights[:2], received[:2])
+def add_terms(own, terms):
+    return (own.astype(jnp.float32) + jnp.sum(terms.astype(jnp.float32), axis=0)).astype(jnp.bfloat16)
+
+
+def activate(states, squares):
+    scale = lax.rsqrt(squares / D + EPSILON)[:, None]
     inner = []
-    for total in (stream(number, 0, half, (1, 2), *args), stream(number, half, half, (2, 1), *args)):
-        inner.append((jax.nn.silu(total[0] * scale) * (total[1] * scale)).astype(jnp.bfloat16))
-    inner = jnp.concatenate(inner, axis=1)
-    along_x = swap_dp(inner, 1)
-    along_y = swap_dp(inner, 2)
-    corner = (swap_dp(along_y[:, :half], 1), swap_dp(along_x[:, half:], 2))
-    terms = down_terms(number, (inner, along_x, along_y) + corner, weights[2], received[2])
-    terms = exchange(terms, "mp")
-    return (own.astype(jnp.float32) + jnp.sum(terms.astype(jnp.float32), axis=0)).astype(jnp.bfloat16)
-
-
-def fast_final(hidden_in, layer_gain, gate, up, down, targets):
+    for state, step in zip(states, (2, 1)):
+        total = sum_second(state, step) * scale
+        inner.append((jax.nn.silu(total[0]) * total[1]).astype(jnp.bfloat16))
+    return jnp.concatenate(inner, axis=1)
+
+
+def fast_final(hidden_in, layer_gain, gate, up, down, teacher, counts):
     tokens, features = hidden_in.shape[1:]
-    count = tokens // HALVES
+    half = gate.shape[1] // 2
+    count = tokens // 2
     is_first = lax.axis_index("section") == 0
     gain = lax.dynamic_slice_in_dim(layer_gain[0, 0], lax.axis_index("dp") * features, features, 0)
     other_gain = swap_section(gain)
-    owns = [transpose_mesh(hidden_in[0, i * count : (i + 1) * count]) for i in range(HALVES)]
-    other_gate, other_up = swap_section(gate), swap_section(up)
-    rows = [enter(owns[0])]
-    rows[0], targets, later_down = lax.optimization_barrier((rows[0], targets, down))
-    received = (other_gate, other_up, swap_section(later_down))
-    rows += [enter(own) for own in owns[1:]]
+    early_gate, early_up = tie((gate, up), other_gain)
+    received = [swap_section(early_gate), swap_section(early_up)]
+    owns = [transpose_mesh(hidden_in[0, i * count : (i + 1) * count]) for i in range(2)]
+    targets = fast_targets(*tie((teacher, counts), owns[0]), tokens)
     for number in range(2):
         gain_row = jnp.where(is_first == (number == 0), gain, other_gain)[None, :]
-        if number:
-            rows = [enter(own) for own in owns]
-        owns = [layer(number, own, piece, gain_row, (gate, up, down), received) for own, piece in zip(owns, rows)]
+
+        def products(which, pieces):
+            return gate_up(
+                number, which * half, half, which == 0, pieces, gain_row, (gate, up), received[:2]
+            )
+
+        if not number:
+            rows = enter(owns[0])
+            rows, owns[1], targets, later_down = lax.optimization_barrier((rows, owns[1], targets, down))
+            received.append(swap_section(later_down))
+            later_rows = enter(owns[1])
+        first, second = products(0, rows), products(1, rows)
+        later_rows = tie(later_rows, second[0])
+        states = [sum_first(first, 1), sum_first(second, 2)]
+        later_first = products(0, later_rows)
+        later_second = products(1, tie(later_rows, states[0][2]))
+        later_states = [sum_first(later_first, 1), sum_first(later_second, 2)]
+        squares, later_squares = sum_squares([rows, later_rows], later_second[0])
+        inner, later_inner = activate(states, squares), activate(later_states, later_squares)
+        along = [swap_dp(inner, 1), swap_dp(inner, 2)]
+        later_along = [swap_dp(later_inner, 1), swap_dp(later_inner, 2)]
+        corner = [swap_dp(along[1][:, :half], 1), swap_dp(along[0][:, half:], 2)]
+        terms = exchange(down_terms(number, [inner] + along + corner, down, received[2]), "mp")
+        corner = [swap_dp(later_along[1][:, :half], 1), swap_dp(later_along[0][:, half:], 2)]
+        owns[0] = add_terms(owns[0], terms)
+        if not number:
+            rows = enter(owns[0])
+        terms = down_terms(number, [later_inner] + later_along + corner, down, received[2])
+        rows = tie(rows, terms)
+        owns[1] = add_terms(owns[1], exchange(tie(terms, owns[0]), "mp"))
+        if not number:
+            later_rows = enter(owns[1])
     return jnp.concatenate([transpose_mesh(own) for own in owns], axis=0), targets
 
 
@@ -298,9 +351,14 @@
 def fast_body(
     hidden_in, layer_gain, gate_proj, up_proj, down_proj, final_gain, teacher_rows, send_counts, doc_ids
 ):
-    targets = fast_targets(teacher_rows[0, 0], send_counts[0, 0], hidden_in.shape[1])
     final, targets = fast_final(
-        hidden_in, layer_gain, gate_proj[0, 0], up_proj[0, 0], down_proj[0, 0], targets
+        hidden_in,
+        layer_gain,
+        gate_proj[0, 0],
+        up_proj[0, 0],
+        down_proj[0, 0],
+        teacher_rows[0, 0],
+        send_counts[0, 0],
     )
     return distil_once(final, targets, weights_of_rows(doc_ids[0, 0]), final_gain)
 

time: 420 us -> 392 us (0.933)
  waiting for transfers between devices: 189 us -> 154 us
  other arithmetic: 10.6 us -> 22.8 us
  starting transfers between devices: 107 us -> 99.3 us
    ppermute x12, waiting for transfers between devices: 26.2 us -> 7.54 us  [swap_mp(): return lax.ppermute(value, 'mp', [(m, m ^ k) for m in range(4)])]
    all_to_all x4, waiting for transfers between devices: 36.9 us -> 20.3 us  [exchange(): return lax.all_to_all(value, axis, split_axis=0, concat_axis=0, tiled=True)]
    ppermute x40 -> x36, starting transfers between devices: 41.3 us -> 33.3 us  [swap_dp(): return lax.ppermute(value, 'dp', [(d, d ^ e) for d in range(4)])]
    ppermute x12, starting transfers between devices: 14.4 us -> 22.2 us  [swap_mp(): return lax.ppermute(value, 'mp', [(m, m ^ k) for m in range(4)])]
    mul x0 -> x4, other arithmetic: none -> 5.5 us  [activate(): total = sum_second(state, step) * scale]
    convert_element_type x15 -> x20, other arithmetic: 2.57 us -> 7.31 us  [the longest x8 6.23 us: sum_first(): (keep[:, count:] + got[:, count:].astype(jnp.float32)).astype(jnp.bfloat16)]
    all_to_all x1, waiting for transfers between devices: 0.01 us -> 4.33 us  [fast_targets(): lax.all_to_all(teacher.reshape(4, capacity, features), 'dp', split_axis=0...]
    ppermute x40 -> x36, waiting for transfers between devices: 93.5 us -> 91.3 us  [swap_dp(): return lax.ppermute(value, 'dp', [(d, d ^ e) for d in range(4)])]
  transfers between devices with their start and end apart: 66 -> 62, of which waited for: 37 -> 25; matrix products, arithmetic and copies ran while one was open for 3% -> 6% of each run, Pallas kernels for 18% -> 24%
where the time goes in v2:
time: 392 us; the launch traced here: 391 us
  waiting for transfers between devices  154 us (39%)
  starting transfers between devices  99.3 us (25%)
  Pallas kernels  95.5 us (24%)
  other arithmetic  22.8 us (6%)
  blocking collectives  11.9 us (3%)
  local copies, waits for them, and re-layouts  4.67 us (1%)
    ppermute x36, waiting for transfers between devices, swap_dp(): return lax.ppermute(value, 'dp', [(d, d ^ e) for d in range(4)])  91.3 us
    pallas_call x8, Pallas kernels, gate_up(): pl.pallas_call(functools.partial(gate_up_kernel, number, first, swapped,...  60.4 us
    pallas_call x4, Pallas kernels, down_terms(): pl.pallas_call(functools.partial(down_kernel, number), grid=(features //...  35.1 us
    ppermute x36, starting transfers between devices, swap_dp(): return lax.ppermute(value, 'dp', [(d, d ^ e) for d in range(4)])  33.3 us
    ppermute x4, waiting for transfers between devices, transpose_mesh(): return lax.ppermute(value, ('dp', 'mp'), pairs)  29.3 us
    all_to_all x4, starting transfers between devices, exchange(): return lax.all_to_all(value, axis, split_axis=0, concat_axis=0, tiled=True)  22.6 us
    ppermute x12, starting transfers between devices, swap_mp(): return lax.ppermute(value, 'mp', [(m, m ^ k) for m in range(4)])  22.2 us
    all_to_all x4, waiting for transfers between devices, exchange(): return lax.all_to_all(value, axis, split_axis=0, concat_axis=0, tiled=True)  20.3 us
  transfers between devices with their start and end apart: 62, of which 25 were waited for; matrix products, arithmetic and copies ran while one was open for 6% of the time, Pallas kernels for 24%

profile of v2, /device:TPU:2, one launch (start us, length us, event | category | flops | bytes accessed | tf_op | source)
XLA Modules:
  0.0 391.3 jit_solution(17494234953887523560)
XLA Ops:
  4.1 3.5 collective-permute-start
  7.6 3.3 collective-permute-start.4
  10.9 20.6 %collective-permute-done.x0 = bf16[48,2048]{1,0:T(8,128)(2,1)S(1)} collective-permute-done((bf16[48,2048]{1,0:T(8,128)(2,1)S(1)}, bf16[48,2048]{1,0:T(8,128)(2,1)S(1)}, u32[]{:S(2)}, u32[]{:S(2)}) %collective-permute-start) | collective-permute-done | bytes 196640 | tf_op jit(solution)/shard_map/ppermute | solution.py:25
  32.9 3.3 all-to-all-start.1
  36.2 4.2 %collective-permute-start.2 = (bf16[48,2048]{1,0:T(8,128)(2,1)S(1)}, bf16[48,2048]{1,0:T(8,128)(2,1)S(1)}, u32[]{:S(2)}, u32[]{:S(2)}) collective-permute-start(bf16[48,2048]{1,0:T(8,128)(2,1)S(1)} %collective-permute-done.x0), channel_id=1, source_target_pairs={{0,2},{1,3},{2,0},{3,1},{4,6},{5,7},{6,4},{7,5},{8,10},{9,11},{10,... | collective-permute-start | bytes 589832 | tf_op jit(solution)/shard_map/ppermute | solution.py:33
  40.4 4.2 %all-to-all-start = ((bf16[4,48,2048]{2,1,0:T(8,128)(2,1)}), bf16[4,48,2048]{2,1,0:T(8,128)(2,1)S(1)}, u32[]{:S(2)}, u32[]{:S(2)}) async-start(bf16[4,48,2048]{2,1,0:T(8,128)(2,1)} %bitcast.222), calls=%async_computation | async-start | bytes 1572864 | tf_op jit(solution)/shard_map/all_to_all | solution.py:285
  45.1 3.3 collective-permute-start.3
  48.4 4.3 %all-to-all-done = bf16[4,48,2048]{2,1,0:T(8,128)(2,1)S(1)} async-done(((bf16[4,48,2048]{2,1,0:T(8,128)(2,1)}), bf16[4,48,2048]{2,1,0:T(8,128)(2,1)S(1)}, u32[]{:S(2)}, u32[]{:S(2)}) %all-to-all-start) | async-done | bytes 786464 | tf_op jit(solution)/shard_map/all_to_all | solution.py:285
  54.7 1.8 collective-permute-start.10
  56.5 1.8 collective-permute-start.11
  59.7 7.5 %gate_up.9 = (f32[2,96,2048]{2,1,0:T(8,128)S(1)}, bf16[2,96,2048]{2,1,0:T(8,128)(2,1)S(1)}) custom-call(bf16[48,2048]{1,0:T(8,128)(2,1)S(1)} %collective-permute-done.x0, bf16[48,2048]{1,0:T(8,128)(2,1)S(1)} %collective-permute-done.1.x1, bf16[48,2048]{1,0:T(8,128)(2,1)S(1)} %collective-permute-done.2.x2, bf16[48,2048]{1,0:T(8,128)(2,1)S(1)} %collective-permute-done.3.x3, ...), custom_call_target="tpu_custom_call" | custom-call | flops 3221225472 | bytes 16777216 | tf_op jit(solution)/shard_map/gate_up/pallas_call | solution.py:97
  68.4 5.2 %collective-permute-done.11.x2 = bf16[48,2048]{1,0:T(8,128)(2,1)S(1)} collective-permute-done((bf16[48,2048]{1,0:T(8,128)(2,1)S(1)}, bf16[48,2048]{1,0:T(8,128)(2,1)S(1)}, u32[]{:S(2)}, u32[]{:S(2)}) %collective-permute-start.11) | collective-permute-done | bytes 196640 | tf_op jit(solution)/shard_map/ppermute | solution.py:33
  73.6 7.5 %gate_up.8 = (f32[2,96,2048]{2,1,0:T(8,128)S(1)}, bf16[2,96,2048]{2,1,0:T(8,128)(2,1)S(1)}) custom-call(bf16[48,2048]{1,0:T(8,128)(2,1)S(1)} %collective-permute-done.x0, bf16[48,2048]{1,0:T(8,128)(2,1)S(1)} %collective-permute-done.1.x1, bf16[48,2048]{1,0:T(8,128)(2,1)S(1)} %collective-permute-done.2.x2, bf16[48,2048]{1,0:T(8,128)(2,1)S(1)} %collective-permute-done.3.x3, ...), custom_call_target="tpu_custom_call" | custom-call | flops 3221225472 | bytes 16777216 | tf_op jit(solution)/shard_map/gate_up/pallas_call | solution.py:97
  81.8 1.9 collective-permute-start.13
  83.7 7.5 %gate_up.11 = (f32[2,96,2048]{2,1,0:T(8,128)S(1)}, bf16[2,96,2048]{2,1,0:T(8,128)(2,1)S(1)}) custom-call(bf16[48,2048]{1,0:T(8,128)(2,1)S(1)} %collective-permute-done.4.x0, bf16[48,2048]{1,0:T(8,128)(2,1)S(1)} %collective-permute-done.10.x1, bf16[48,2048]{1,0:T(8,128)(2,1)S(1)} %collective-permute-done.11.x2, ...), custom_call_target="tpu_custom_call" | custom-call | flops 3221225472 | bytes 16777216 | tf_op jit(solution)/shard_map/gate_up/pallas_call | solution.py:97
  91.4 10.1 %collective-permute-done.8 = bf16[2,96,2048]{2,1,0:T(8,128)(2,1)S(1)} collective-permute-done((bf16[2,96,2048]{2,1,0:T(8,128)(2,1)S(1)}, bf16[2,96,2048]{2,1,0:T(8,128)(2,1)S(1)}, u32[]{:S(2)}, u32[]{:S(2)}) %collective-permute-start.8) | collective-permute-done | bytes 786464 | tf_op jit(solution)/shard_map/ppermute | solution.py:29
  103.2 7.5 %gate_up.10 = (f32[2,96,2048]{2,1,0:T(8,128)S(1)}, bf16[2,96,2048]{2,1,0:T(8,128)(2,1)S(1)}) custom-call(bf16[48,2048]{1,0:T(8,128)(2,1)S(1)} %collective-permute-done.4.x0, bf16[48,2048]{1,0:T(8,128)(2,1)S(1)} %collective-permute-done.10.x1, bf16[48,2048]{1,0:T(8,128)(2,1)S(1)} %collective-permute-done.11.x2, ...), custom_call_target="tpu_custom_call" | custom-call | flops 3221225472 | bytes 16777216 | tf_op jit(solution)/shard_map/gate_up/pallas_call | solution.py:97
  112.0 2.3 collective-permute-done.14
  115.0 9.5 %collective-permute-done.16 = bf16[2,48,2048]{2,1,0:T(8,128)(2,1)S(1)} collective-permute-done((bf16[2,48,2048]{2,1,0:T(8,128)(2,1)S(1)}, bf16[2,48,2048]{2,1,0:T(8,128)(2,1)S(1)}, u32[]{:S(2)}, u32[]{:S(2)}) %collective-permute-start.16) | collective-permute-done | bytes 393248 | tf_op jit(solution)/shard_map/ppermute | solution.py:29
  125.1 1.5 collective-permute-start.18
  128.9 10.0 %collective-permute-done.18.x2 = bf16[48,4096]{1,0:T(8,128)(2,1)S(1)} collective-permute-done((bf16[48,4096]{1,0:T(8,128)(2,1)S(1)}, bf16[48,4096]{1,0:T(8,128)(2,1)S(1)}, u32[]{:S(2)}, u32[]{:S(2)}) %collective-permute-start.18) | collective-permute-done | bytes 393248 | tf_op jit(solution)/shard_map/ppermute | solution.py:29
  139.0 1.6 collective-permute-start.19
  142.2 3.9 collective-permute-done.19.x3a
  146.0 3.1 collective-permute-done.20.x3b
  149.1 8.8 %down.4 = bf16[4,48,2048]{2,1,0:T(8,128)(2,1)} custom-call(bf16[48,4096]{1,0:T(8,128)(2,1)S(1)} %pad_maximum_fusion.x0, bf16[48,4096]{1,0:T(8,128)(2,1)S(1)} %collective-permute-done.17.x1, bf16[48,4096]{1,0:T(8,128)(2,1)S(1)} %collective-permute-done.18.x2, bf16[48,2048]{1,0:T(8,128)(2,1)S(1)} %collective-permute-done.19.x3a, ...), custom_call_target="tpu_custom_call" | custom-call | flops 3221225472 | bytes 16777216 | tf_op jit(solution)/shard_map/down/pallas_call | solution.py:162
  157.9 7.5 %all-to-all-start.2 = ((bf16[4,48,2048]{2,1,0:T(8,128)(2,1)}), bf16[4,48,2048]{2,1,0:T(8,128)(2,1)}, u32[]{:S(2)}, u32[]{:S(2)}) async-start(bf16[4,48,2048]{2,1,0:T(8,128)(2,1)} %down.4), calls=%async_computation.2 | async-start | bytes 1572864 | tf_op jit(solution)/shard_map/all_to_all | solution.py:37
  165.4 1.8 add_multiply_fusion.5
  169.1 7.0 %collective-permute-done.30.x2 = bf16[48,4096]{1,0:T(8,128)(2,1)S(1)} collective-permute-done((bf16[48,4096]{1,0:T(8,128)(2,1)S(1)}, bf16[48,4096]{1,0:T(8,128)(2,1)S(1)}, u32[]{:S(2)}, u32[]{:S(2)}) %collective-permute-start.30) | collective-permute-done | bytes 393248 | tf_op jit(solution)/shard_map/ppermute | solution.py:29
  177.1 1.9 collective-permute-done.29.x1
  179.1 5.1 %all-to-all-done.2 = bf16[4,48,2048]{2,1,0:T(8,128)(2,1)} async-done(((bf16[4,48,2048]{2,1,0:T(8,128)(2,1)}), bf16[4,48,2048]{2,1,0:T(8,128)(2,1)}, u32[]{:S(2)}, u32[]{:S(2)}) %all-to-all-start.2) | async-done | bytes 786464 | tf_op jit(solution)/shard_map/all_to_all | solution.py:37
  185.6 2.0 collective-permute-start.23
  187.6 2.4 collective-permute-start.24
  190.0 8.8 %down.5 = bf16[4,48,2048]{2,1,0:T(8,128)(2,1)} custom-call(bf16[48,4096]{1,0:T(8,128)(2,1)S(1)} %pad_maximum_fusion.1.x0, bf16[48,4096]{1,0:T(8,128)(2,1)S(1)} %collective-permute-done.29.x1, bf16[48,4096]{1,0:T(8,128)(2,1)S(1)} %collective-permute-done.30.x2, bf16[48,2048]{1,0:T(8,128)(2,1)S(1)} %collective-permute-done.31.x3a, ...), custom_call_target="tpu_custom_call" | custom-call | flops 3221225472 | bytes 16777216 | tf_op jit(solution)/shard_map/down/pallas_call | solution.py:162
  198.8 4.4 %all-to-all-start.3 = ((bf16[4,48,2048]{2,1,0:T(8,128)(2,1)}), bf16[4,48,2048]{2,1,0:T(8,128)(2,1)}, u32[]{:S(2)}, u32[]{:S(2)}) async-start(bf16[4,48,2048]{2,1,0:T(8,128)(2,1)} %down.5), calls=%async_computation.3 | async-start | bytes 1572864 | tf_op jit(solution)/shard_map/all_to_all | solution.py:37
  203.2 7.5 %gate_up.13 = (f32[2,96,2048]{2,1,0:T(8,128)S(1)}, bf16[2,96,2048]{2,1,0:T(8,128)(2,1)S(1)}) custom-call(bf16[48,2048]{1,0:T(8,128)(2,1)S(1)} %add_convert_fusion.11.x0, bf16[48,2048]{1,0:T(8,128)(2,1)S(1)} %collective-permute-done.22.x1, bf16[48,2048]{1,0:T(8,128)(2,1)S(1)} %collective-permute-done.23.x2, bf16[48,2048]{1,0:T(8,128)(2,1)S(1)} %collective-permute-done.24.x3, ...), custom_call_target="tpu_custom_call" | custom-call | flops 3221225472 | bytes 16777216 | tf_op jit(solution)/shard_map/gate_up/pallas_call | solution.py:97
  210.7 1.5 collective-permute-start.40
  212.2 8.2 %gate_up.12 = (f32[2,96,2048]{2,1,0:T(8,128)S(1)}, bf16[2,96,2048]{2,1,0:T(8,128)(2,1)}) custom-call(bf16[48,2048]{1,0:T(8,128)(2,1)S(1)} %add_convert_fusion.11.x0, bf16[48,2048]{1,0:T(8,128)(2,1)S(1)} %collective-permute-done.22.x1, bf16[48,2048]{1,0:T(8,128)(2,1)S(1)} %collective-permute-done.23.x2, bf16[48,2048]{1,0:T(8,128)(2,1)S(1)} %collective-permute-done.24.x3, ...), custom_call_target="tpu_custom_call" | custom-call | flops 3221225472 | bytes 16777216 | tf_op jit(solution)/shard_map/gate_up/pallas_call | solution.py:97
  224.8 3.3 collective-permute-start.35
  229.0 1.5 collective-permute-start.37
  230.5 9.2 %collective-permute-done.33 = bf16[2,96,2048]{2,1,0:T(8,128)(2,1)} collective-permute-done((bf16[2,96,2048]{2,1,0:T(8,128)(2,1)}, bf16[2,96,2048]{2,1,0:T(8,128)(2,1)}, u32[]{:S(2)}, u32[]{:S(2)}) %collective-permute-start.33) | collective-permute-done | bytes 786464 | tf_op jit(solution)/shard_map/ppermute | solution.py:29
  241.3 2.3 collective-permute-done.36.x2
  245.1 7.5 %gate_up.14 = (f32[2,96,2048]{2,1,0:T(8,128)S(1)}, bf16[2,96,2048]{2,1,0:T(8,128)(2,1)S(1)}) custom-call(bf16[48,2048]{1,0:T(8,128)(2,1)S(1)} %add_convert_fusion.10.x0, bf16[48,2048]{1,0:T(8,128)(2,1)S(1)} %collective-permute-done.35.x1, bf16[48,2048]{1,0:T(8,128)(2,1)S(1)} %collective-permute-done.36.x2, bf16[48,2048]{1,0:T(8,128)(2,1)S(1)} %collective-permute-done.37.x3, ...), custom_call_target="tpu_custom_call" | custom-call | flops 3221225472 | bytes 16777216 | tf_op jit(solution)/shard_map/gate_up/pallas_call | solution.py:97
  255.5 1.6 collective-permute-start.49
  257.2 5.1 %collective-permute-done.41 = bf16[2,48,2048]{2,1,0:T(8,128)(2,1)S(1)} collective-permute-done((bf16[2,48,2048]{2,1,0:T(8,128)(2,1)S(1)}, bf16[2,48,2048]{2,1,0:T(8,128)(2,1)S(1)}, u32[]{:S(2)}, u32[]{:S(2)}) %collective-permute-start.41) | collective-permute-done | bytes 393248 | tf_op jit(solution)/shard_map/ppermute | solution.py:29
  264.1 1.9 collective-permute-start.43
  266.0 1.6 collective-permute-start.42
  267.6 7.5 %gate_up.15 = (f32[2,96,2048]{2,1,0:T(8,128)S(1)}, bf16[2,96,2048]{2,1,0:T(8,128)(2,1)S(1)}) custom-call(bf16[48,2048]{1,0:T(8,128)(2,1)S(1)} %add_convert_fusion.10.x0, bf16[48,2048]{1,0:T(8,128)(2,1)S(1)} %collective-permute-done.35.x1, bf16[48,2048]{1,0:T(8,128)(2,1)S(1)} %collective-permute-done.36.x2, bf16[48,2048]{1,0:T(8,128)(2,1)S(1)} %collective-permute-done.37.x3, ...), custom_call_target="tpu_custom_call" | custom-call | flops 3221225472 | bytes 16777216 | tf_op jit(solution)/shard_map/gate_up/pallas_call | solution.py:97
  275.6 4.7 %collective-permute-done.43.x2 = bf16[48,4096]{1,0:T(8,128)(2,1)S(1)} collective-permute-done((bf16[48,4096]{1,0:T(8,128)(2,1)S(1)}, bf16[48,4096]{1,0:T(8,128)(2,1)S(1)}, u32[]{:S(2)}, u32[]{:S(2)}) %collective-permute-start.43) | collective-permute-done | bytes 393248 | tf_op jit(solution)/shard_map/ppermute | solution.py:29
  280.3 1.9 collective-permute-start.44
  284.4 11.2 %collective-permute-done.47 = bf16[2,96,2048]{2,1,0:T(8,128)(2,1)S(1)} collective-permute-done((bf16[2,96,2048]{2,1,0:T(8,128)(2,1)S(1)}, bf16[2,96,2048]{2,1,0:T(8,128)(2,1)S(1)}, u32[]{:S(2)}, u32[]{:S(2)}) %collective-permute-start.47) | collective-permute-done | bytes 786464 | tf_op jit(solution)/shard_map/ppermute | solution.py:29
  296.8 2.3 collective-permute-done.44.x3a
  299.1 8.8 %down.6 = bf16[4,48,2048]{2,1,0:T(8,128)(2,1)} custom-call(bf16[48,4096]{1,0:T(8,128)(2,1)S(1)} %pad_maximum_fusion.2.x0, bf16[48,4096]{1,0:T(8,128)(2,1)S(1)} %collective-permute-done.42.x1, bf16[48,4096]{1,0:T(8,128)(2,1)S(1)} %collective-permute-done.43.x2, bf16[48,2048]{1,0:T(8,128)(2,1)S(1)} %collective-permute-done.44.x3a, ...), custom_call_target="tpu_custom_call" | custom-call | flops 3221225472 | bytes 16777216 | tf_op jit(solution)/shard_map/down/pallas_call | solution.py:162
  307.9 5.6 %all-to-all-start.4 = ((bf16[4,48,2048]{2,1,0:T(8,128)(2,1)}), bf16[4,48,2048]{2,1,0:T(8,128)(2,1)S(1)}, u32[]{:S(2)}, u32[]{:S(2)}) async-start(bf16[4,48,2048]{2,1,0:T(8,128)(2,1)} %down.6), calls=%async_computation.4 | async-start | bytes 1572864 | tf_op jit(solution)/shard_map/all_to_all | solution.py:37
  313.5 1.9 add_multiply_fusion.1
  317.5 6.2 %collective-permute-done.52.x2 = bf16[48,4096]{1,0:T(8,128)(2,1)S(1)} collective-permute-done((bf16[48,4096]{1,0:T(8,128)(2,1)S(1)}, bf16[48,4096]{1,0:T(8,128)(2,1)S(1)}, u32[]{:S(2)}, u32[]{:S(2)}) %collective-permute-start.52) | collective-permute-done | bytes 393248 | tf_op jit(solution)/shard_map/ppermute | solution.py:29
  325.8 3.6 collective-permute-done.53.x3a
  330.4 8.8 %down.7 = bf16[4,48,2048]{2,1,0:T(8,128)(2,1)} custom-call(bf16[48,4096]{1,0:T(8,128)(2,1)S(1)} %pad_maximum_fusion.3.x0, bf16[48,4096]{1,0:T(8,128)(2,1)S(1)} %collective-permute-done.51.x1, bf16[48,4096]{1,0:T(8,128)(2,1)S(1)} %collective-permute-done.52.x2, bf16[48,2048]{1,0:T(8,128)(2,1)S(1)} %collective-permute-done.53.x3a, ...), custom_call_target="tpu_custom_call" | custom-call | flops 3221225472 | bytes 16777216 | tf_op jit(solution)/shard_map/down/pallas_call | solution.py:162
  339.4 5.1 %all-to-all-start.5 = ((bf16[4,48,2048]{2,1,0:T(8,128)(2,1)}), bf16[4,48,2048]{2,1,0:T(8,128)(2,1)S(1)}, u32[]{:S(2)}, u32[]{:S(2)}) async-start(bf16[4,48,2048]{2,1,0:T(8,128)(2,1)} %down.7), calls=%async_computation.5 | async-start | bytes 1572864 | tf_op jit(solution)/shard_map/all_to_all | solution.py:37
  344.6 4.4 %collective-permute-start.46 = (bf16[48,2048]{1,0:T(8,128)(2,1)S(1)}, bf16[48,2048]{1,0:T(8,128)(2,1)S(1)}, u32[]{:S(2)}, u32[]{:S(2)}) collective-permute-start(bf16[48,2048]{1,0:T(8,128)(2,1)S(1)} %add_convert_fusion.9), channel_id=1, source_target_pairs={{0,0},{1,4},{2,8},{3,12},{4,1},{5,5},{6,9},{7,13},{8,2},{9,6},{10,... | collective-permute-start | bytes 589832 | tf_op jit(solution)/shard_map/ppermute | solution.py:25
  349.0 15.1 %all-to-all-done.5 = bf16[4,48,2048]{2,1,0:T(8,128)(2,1)S(1)} async-done(((bf16[4,48,2048]{2,1,0:T(8,128)(2,1)}), bf16[4,48,2048]{2,1,0:T(8,128)(2,1)S(1)}, u32[]{:S(2)}, u32[]{:S(2)}) %all-to-all-start.5) | async-done | bytes 786464 | tf_op jit(solution)/shard_map/all_to_all | solution.py:37
  364.3 1.9 collective-permute-start.55
  366.4 6.6 %collective-permute-done.46 = bf16[48,2048]{1,0:T(8,128)(2,1)S(1)} collective-permute-done((bf16[48,2048]{1,0:T(8,128)(2,1)S(1)}, bf16[48,2048]{1,0:T(8,128)(2,1)S(1)}, u32[]{:S(2)}, u32[]{:S(2)}) %collective-permute-start.46) | collective-permute-done | bytes 196640 | tf_op jit(solution)/shard_map/ppermute | solution.py:25
  373.0 2.1 collective-permute-done.55
  375.7 11.9 %all-gather.1 = f32[4,4,96]{2,1,0:T(4,128)S(1)} all-gather(f32[1,4,96]{2,1,0:T(4,128)S(1)} %maximum_bitcast_fusion), channel_id=2, replica_groups=mesh['section'=2,'dp'=4,'mp'=4] {'mp'}, dimensions={0}, use_global_device_ids=true | all-gather | bytes 7680 | tf_op jit(solution)/shard_map/all_gather | solution.py:338
  (206 shorter events, 48.6 us)
Async XLA Ops:
  1.4 1.2 collective-permute-start.5
  2.6 56.1 %collective-permute-start.6 = (bf16[2048,4096]{1,0:T(8,128)(2,1)}, bf16[2048,4096]{1,0:T(8,128)(2,1)}, u32[]{:S(2)}, u32[]{:S(2)}) collective-permute-start(bf16[2048,4096]{1,0:T(8,128)(2,1)} %bitcast.198), channel_id=1, source_target_pairs={{0,16},{16,0},{1,17},{17,1},{2,18},{18,2},{3,19},{19,3},{4,20},{20... | collective-permute-start | bytes 50331656 | tf_op jit(solution)/shard_map/ppermute | solution.py:20
  2.7 56.9 %collective-permute-start.7 = (bf16[2048,4096]{1,0:T(8,128)(2,1)}, bf16[2048,4096]{1,0:T(8,128)(2,1)}, u32[]{:S(2)}, u32[]{:S(2)}) collective-permute-start(bf16[2048,4096]{1,0:T(8,128)(2,1)} %bitcast.207), channel_id=1, source_target_pairs={{0,16},{16,0},{1,17},{17,1},{2,18},{18,2},{3,19},{19,3},{4,20},{20... | collective-permute-start | bytes 50331656 | tf_op jit(solution)/shard_map/ppermute | solution.py:20
  4.1 27.4 %collective-permute-start = (bf16[48,2048]{1,0:T(8,128)(2,1)S(1)}, bf16[48,2048]{1,0:T(8,128)(2,1)S(1)}, u32[]{:S(2)}, u32[]{:S(2)}) collective-permute-start(bf16[48,2048]{1,0:T(8,128)(2,1)S(1)} %get-tuple-element.110), channel_id=1, source_target_pairs={{0,0},{1,4},{2,8},{3,12},{4,1},{5,5},{6,9},{7,13},{8,2},{9,6},{10,... | collective-permute-start | bytes 589832 | tf_op jit(solution)/shard_map/ppermute | solution.py:25
  7.6 37.5 %collective-permute-start.4 = (bf16[48,2048]{1,0:T(8,128)(2,1)S(1)}, bf16[48,2048]{1,0:T(8,128)(2,1)S(1)}, u32[]{:S(2)}, u32[]{:S(2)}) collective-permute-start(bf16[48,2048]{1,0:T(8,128)(2,1)S(1)} %get-tuple-element.109), channel_id=1, source_target_pairs={{0,0},{1,4},{2,8},{3,12},{4,1},{5,5},{6,9},{7,13},{8,2},{9,6},{10,... | collective-permute-start | bytes 589832 | tf_op jit(solution)/shard_map/ppermute | solution.py:25
  32.9 7.5 %all-to-all-start.1 = ((bf16[4,1,1]{2,1,0:T(2,128)(2,1)}), bf16[4,1,1]{2,1,0:T(2,128)(2,1)S(1)}, u32[]{:S(2)}, u32[]{:S(2)}) async-start(bf16[4,1,1]{2,1,0:T(2,128)(2,1)} %copy.22), calls=%async_computation.1 | async-start | bytes 4096 | tf_op jit(solution)/shard_map/all_to_all | solution.py:288
  36.2 18.4 %collective-permute-start.1 = (bf16[48,2048]{1,0:T(8,128)(2,1)S(1)}, bf16[48,2048]{1,0:T(8,128)(2,1)S(1)}, u32[]{:S(2)}, u32[]{:S(2)}) collective-permute-start(bf16[48,2048]{1,0:T(8,128)(2,1)S(1)} %collective-permute-done.x0), channel_id=1, source_target_pairs={{0,1},{1,0},{2,3},{3,2},{4,5},{5,4},{6,7},{7,6},{8,9},{9,8},{10,11... | collective-permute-start | bytes 589832 | tf_op jit(solution)/shard_map/ppermute | solution.py:33
  36.2 18.4 %collective-permute-start.2 = (bf16[48,2048]{1,0:T(8,128)(2,1)S(1)}, bf16[48,2048]{1,0:T(8,128)(2,1)S(1)}, u32[]{:S(2)}, u32[]{:S(2)}) collective-permute-start(bf16[48,2048]{1,0:T(8,128)(2,1)S(1)} %collective-permute-done.x0), channel_id=1, source_target_pairs={{0,2},{1,3},{2,0},{3,1},{4,6},{5,7},{6,4},{7,5},{8,10},{9,11},{10,... | collective-permute-start | bytes 589832 | tf_op jit(solution)/shard_map/ppermute | solution.py:33
  40.4 12.4 %all-to-all-start = ((bf16[4,48,2048]{2,1,0:T(8,128)(2,1)}), bf16[4,48,2048]{2,1,0:T(8,128)(2,1)S(1)}, u32[]{:S(2)}, u32[]{:S(2)}) async-start(bf16[4,48,2048]{2,1,0:T(8,128)(2,1)} %bitcast.222), calls=%async_computation | async-start | bytes 1572864 | tf_op jit(solution)/shard_map/all_to_all | solution.py:285
  45.1 9.5 %collective-permute-start.3 = (bf16[48,2048]{1,0:T(8,128)(2,1)S(1)}, bf16[48,2048]{1,0:T(8,128)(2,1)S(1)}, u32[]{:S(2)}, u32[]{:S(2)}) collective-permute-start(bf16[48,2048]{1,0:T(8,128)(2,1)S(1)} %collective-permute-done.x0), channel_id=1, source_target_pairs={{0,3},{1,2},{2,1},{3,0},{4,7},{5,6},{6,5},{7,4},{8,11},{9,10},{10,... | collective-permute-start | bytes 589832 | tf_op jit(solution)/shard_map/ppermute | solution.py:33
  54.6 87.6 %collective-permute-start.21 = (bf16[4096,2048]{1,0:T(8,128)(2,1)}, bf16[4096,2048]{1,0:T(8,128)(2,1)}, u32[]{:S(2)}, u32[]{:S(2)}) collective-permute-start(bf16[4096,2048]{1,0:T(8,128)(2,1)} %bitcast.216), channel_id=1, source_target_pairs={{0,16},{16,0},{1,17},{17,1},{2,18},{18,2},{3,19},{19,3},{4,20},{20... | collective-permute-start | bytes 50331656 | tf_op jit(solution)/shard_map/ppermute | solution.py:20
  54.7 13.7 %collective-permute-start.10 = (bf16[48,2048]{1,0:T(8,128)(2,1)S(1)}, bf16[48,2048]{1,0:T(8,128)(2,1)S(1)}, u32[]{:S(2)}, u32[]{:S(2)}) collective-permute-start(bf16[48,2048]{1,0:T(8,128)(2,1)S(1)} %collective-permute-done.4.x0), channel_id=1, source_target_pairs={{0,1},{1,0},{2,3},{3,2},{4,5},{5,4},{6,7},{7,6},{8,9},{9,8},{10,11... | collective-permute-start | bytes 589832 | tf_op jit(solution)/shard_map/ppermute | solution.py:33
  56.5 17.1 %collective-permute-start.11 = (bf16[48,2048]{1,0:T(8,128)(2,1)S(1)}, bf16[48,2048]{1,0:T(8,128)(2,1)S(1)}, u32[]{:S(2)}, u32[]{:S(2)}) collective-permute-start(bf16[48,2048]{1,0:T(8,128)(2,1)S(1)} %collective-permute-done.4.x0), channel_id=1, source_target_pairs={{0,2},{1,3},{2,0},{3,1},{4,6},{5,7},{6,4},{7,5},{8,10},{9,11},{10,... | collective-permute-start | bytes 589832 | tf_op jit(solution)/shard_map/ppermute | solution.py:33
  58.6 15.0 %collective-permute-start.12 = (bf16[48,2048]{1,0:T(8,128)(2,1)S(1)}, bf16[48,2048]{1,0:T(8,128)(2,1)S(1)}, u32[]{:S(2)}, u32[]{:S(2)}) collective-permute-start(bf16[48,2048]{1,0:T(8,128)(2,1)S(1)} %collective-permute-done.4.x0), channel_id=1, source_target_pairs={{0,3},{1,2},{2,1},{3,0},{4,7},{5,6},{6,5},{7,4},{8,11},{9,10},{10,... | collective-permute-start | bytes 589832 | tf_op jit(solution)/shard_map/ppermute | solution.py:33
  67.1 44.2 %collective-permute-start.15 = (bf16[2,96,2048]{2,1,0:T(8,128)(2,1)S(1)}, bf16[2,96,2048]{2,1,0:T(8,128)(2,1)S(1)}, u32[]{:S(2)}, u32[]{:S(2)}) collective-permute-start(bf16[2,96,2048]{2,1,0:T(8,128)(2,1)S(1)} %get-tuple-element.75), channel_id=1, source_target_pairs={{0,8},{4,12},{8,0},{12,4},{1,9},{5,13},{9,1},{13,5},{2,10},{6,14},... | collective-permute-start | bytes 2359304 | tf_op jit(solution)/shard_map/ppermute | solution.py:29
  81.0 20.5 %collective-permute-start.8 = (bf16[2,96,2048]{2,1,0:T(8,128)(2,1)S(1)}, bf16[2,96,2048]{2,1,0:T(8,128)(2,1)S(1)}, u32[]{:S(2)}, u32[]{:S(2)}) collective-permute-start(bf16[2,96,2048]{2,1,0:T(8,128)(2,1)S(1)} %get-tuple-element.62), channel_id=1, source_target_pairs={{0,4},{4,0},{8,12},{12,8},{1,5},{5,1},{9,13},{13,9},{2,6},{6,2},{1... | collective-permute-start | bytes 2359304 | tf_op jit(solution)/shard_map/ppermute | solution.py:29
  81.8 28.8 %collective-permute-start.13 = (f32[2,2,48]{2,1,0:T(2,128)S(1)}, f32[2,2,48]{2,1,0:T(2,128)S(1)}, u32[]{:S(2)}, u32[]{:S(2)}) collective-permute-start(f32[2,2,48]{2,1,0:T(2,128)S(1)} %pad_maximum_fusion.7), channel_id=1, source_target_pairs={{0,4},{4,0},{8,12},{12,8},{1,5},{5,1},{9,13},{13,9},{2,6},{6,2},{1... | collective-permute-start | bytes 2312 | tf_op jit(solution)/shard_map/ppermute | solution.py:29
  91.1 36.8 %collective-permute-start.25 = (bf16[2,96,2048]{2,1,0:T(8,128)(2,1)S(1)}, bf16[2,96,2048]{2,1,0:T(8,128)(2,1)S(1)}, u32[]{:S(2)}, u32[]{:S(2)}) collective-permute-start(bf16[2,96,2048]{2,1,0:T(8,128)(2,1)S(1)} %get-tuple-element.78), channel_id=1, source_target_pairs={{0,4},{4,0},{8,12},{12,8},{1,5},{5,1},{9,13},{13,9},{2,6},{6,2},{1... | collective-permute-start | bytes 2359304 | tf_op jit(solution)/shard_map/ppermute | solution.py:29
  101.7 22.8 %collective-permute-start.9 = (bf16[2,48,2048]{2,1,0:T(8,128)(2,1)S(1)}, bf16[2,48,2048]{2,1,0:T(8,128)(2,1)S(1)}, u32[]{:S(2)}, u32[]{:S(2)}) collective-permute-start(bf16[2,48,2048]{2,1,0:T(8,128)(2,1)S(1)} %add_convert_fusion.7), channel_id=1, source_target_pairs={{0,8},{4,12},{8,0},{12,4},{1,9},{5,13},{9,1},{13,5},{2,10},{6,14},... | collective-permute-start | bytes 1179656 | tf_op jit(solution)/shard_map/ppermute | solution.py:29
  110.7 3.7 collective-permute-start.14
  111.4 13.1 %collective-permute-start.16 = (bf16[2,48,2048]{2,1,0:T(8,128)(2,1)S(1)}, bf16[2,48,2048]{2,1,0:T(8,128)(2,1)S(1)}, u32[]{:S(2)}, u32[]{:S(2)}) collective-permute-start(bf16[2,48,2048]{2,1,0:T(8,128)(2,1)S(1)} %add_convert_fusion.6), channel_id=1, source_target_pairs={{0,4},{4,0},{8,12},{12,8},{1,5},{5,1},{9,13},{13,9},{2,6},{6,2},{1... | collective-permute-start | bytes 1179656 | tf_op jit(solution)/shard_map/ppermute | solution.py:29
  114.4 26.3 %collective-permute-start.27 = (bf16[2,96,2048]{2,1,0:T(8,128)(2,1)S(1)}, bf16[2,96,2048]{2,1,0:T(8,128)(2,1)S(1)}, u32[]{:S(2)}, u32[]{:S(2)}) collective-permute-start(bf16[2,96,2048]{2,1,0:T(8,128)(2,1)S(1)} %get-tuple-element.79), channel_id=1, source_target_pairs={{0,8},{4,12},{8,0},{12,4},{1,9},{5,13},{9,1},{13,5},{2,10},{6,14},... | collective-permute-start | bytes 2359304 | tf_op jit(solution)/shard_map/ppermute | solution.py:29
  125.1 13.8 %collective-permute-start.18 = (bf16[48,4096]{1,0:T(8,128)(2,1)S(1)}, bf16[48,4096]{1,0:T(8,128)(2,1)S(1)}, u32[]{:S(2)}, u32[]{:S(2)}) collective-permute-start(bf16[48,4096]{1,0:T(8,128)(2,1)S(1)} %pad_maximum_fusion.x0), channel_id=1, source_target_pairs={{0,8},{4,12},{8,0},{12,4},{1,9},{5,13},{9,1},{13,5},{2,10},{6,14},... | collective-permute-start | bytes 1179656 | tf_op jit(solution)/shard_map/ppermute | solution.py:29
  126.7 13.8 %collective-permute-start.17 = (bf16[48,4096]{1,0:T(8,128)(2,1)S(1)}, bf16[48,4096]{1,0:T(8,128)(2,1)S(1)}, u32[]{:S(2)}, u32[]{:S(2)}) collective-permute-start(bf16[48,4096]{1,0:T(8,128)(2,1)S(1)} %pad_maximum_fusion.x0), channel_id=1, source_target_pairs={{0,4},{4,0},{8,12},{12,8},{1,5},{5,1},{9,13},{13,9},{2,6},{6,2},{1... | collective-permute-start | bytes 1179656 | tf_op jit(solution)/shard_map/ppermute | solution.py:29
  128.8 36.6 %collective-permute-start.26 = (bf16[2,48,2048]{2,1,0:T(8,128)(2,1)}, bf16[2,48,2048]{2,1,0:T(8,128)(2,1)}, u32[]{:S(2)}, u32[]{:S(2)}) collective-permute-start(bf16[2,48,2048]{2,1,0:T(8,128)(2,1)} %add_convert_fusion.5), channel_id=1, source_target_pairs={{0,8},{4,12},{8,0},{12,4},{1,9},{5,13},{9,1},{13,5},{2,10},{6,14},... | collective-permute-start | bytes 1179656 | tf_op jit(solution)/shard_map/ppermute | solution.py:29
  139.0 7.1 %collective-permute-start.19 = (bf16[48,2048]{1,0:T(8,128)(2,1)S(1)}, bf16[48,2048]{1,0:T(8,128)(2,1)S(1)}, u32[]{:S(2)}, u32[]{:S(2)}) collective-permute-start(bf16[48,2048]{1,0:T(8,128)(2,1)S(1)} %slice.260), channel_id=1, source_target_pairs={{0,4},{4,0},{8,12},{12,8},{1,5},{5,1},{9,13},{13,9},{2,6},{6,2},{1... | collective-permute-start | bytes 589832 | tf_op jit(solution)/shard_map/ppermute | solution.py:29
  140.5 8.6 %collective-permute-start.20 = (bf16[48,2048]{1,0:T(8,128)(2,1)S(1)}, bf16[48,2048]{1,0:T(8,128)(2,1)S(1)}, u32[]{:S(2)}, u32[]{:S(2)}) collective-permute-start(bf16[48,2048]{1,0:T(8,128)(2,1)S(1)} %slice.261), channel_id=1, source_target_pairs={{0,8},{4,12},{8,0},{12,4},{1,9},{5,13},{9,1},{13,5},{2,10},{6,14},... | collective-permute-start | bytes 589832 | tf_op jit(solution)/shard_map/ppermute | solution.py:29
  141.6 23.8 %collective-permute-start.28 = (bf16[2,48,2048]{2,1,0:T(8,128)(2,1)}, bf16[2,48,2048]{2,1,0:T(8,128)(2,1)}, u32[]{:S(2)}, u32[]{:S(2)}) collective-permute-start(bf16[2,48,2048]{2,1,0:T(8,128)(2,1)} %add_convert_fusion.4), channel_id=1, source_target_pairs={{0,4},{4,0},{8,12},{12,8},{1,5},{5,1},{9,13},{13,9},{2,6},{6,2},{1... | collective-permute-start | bytes 1179656 | tf_op jit(solution)/shard_map/ppermute | solution.py:29
  157.9 26.3 %all-to-all-start.2 = ((bf16[4,48,2048]{2,1,0:T(8,128)(2,1)}), bf16[4,48,2048]{2,1,0:T(8,128)(2,1)}, u32[]{:S(2)}, u32[]{:S(2)}) async-start(bf16[4,48,2048]{2,1,0:T(8,128)(2,1)} %down.4), calls=%async_computation.2 | async-start | bytes 1572864 | tf_op jit(solution)/shard_map/all_to_all | solution.py:37
  167.5 8.7 %collective-permute-start.30 = (bf16[48,4096]{1,0:T(8,128)(2,1)S(1)}, bf16[48,4096]{1,0:T(8,128)(2,1)S(1)}, u32[]{:S(2)}, u32[]{:S(2)}) collective-permute-start(bf16[48,4096]{1,0:T(8,128)(2,1)S(1)} %pad_maximum_fusion.1.x0), channel_id=1, source_target_pairs={{0,8},{4,12},{8,0},{12,4},{1,9},{5,13},{9,1},{13,5},{2,10},{6,14},... | collective-permute-start | bytes 1179656 | tf_op jit(solution)/shard_map/ppermute | solution.py:29
  168.2 10.8 %collective-permute-start.29 = (bf16[48,4096]{1,0:T(8,128)(2,1)S(1)}, bf16[48,4096]{1,0:T(8,128)(2,1)S(1)}, u32[]{:S(2)}, u32[]{:S(2)}) collective-permute-start(bf16[48,4096]{1,0:T(8,128)(2,1)S(1)} %pad_maximum_fusion.1.x0), channel_id=1, source_target_pairs={{0,4},{4,0},{8,12},{12,8},{1,5},{5,1},{9,13},{13,9},{2,6},{6,2},{1... | collective-permute-start | bytes 1179656 | tf_op jit(solution)/shard_map/ppermute | solution.py:29
  176.2 13.8 %collective-permute-start.31 = (bf16[48,2048]{1,0:T(8,128)(2,1)S(1)}, bf16[48,2048]{1,0:T(8,128)(2,1)S(1)}, u32[]{:S(2)}, u32[]{:S(2)}) collective-permute-start(bf16[48,2048]{1,0:T(8,128)(2,1)S(1)} %slice.270), channel_id=1, source_target_pairs={{0,4},{4,0},{8,12},{12,8},{1,5},{5,1},{9,13},{13,9},{2,6},{6,2},{1... | collective-permute-start | bytes 589832 | tf_op jit(solution)/shard_map/ppermute | solution.py:29
  179.0 11.0 %collective-permute-start.32 = (bf16[48,2048]{1,0:T(8,128)(2,1)S(1)}, bf16[48,2048]{1,0:T(8,128)(2,1)S(1)}, u32[]{:S(2)}, u32[]{:S(2)}) collective-permute-start(bf16[48,2048]{1,0:T(8,128)(2,1)S(1)} %slice.271), channel_id=1, source_target_pairs={{0,8},{4,12},{8,0},{12,4},{1,9},{5,13},{9,1},{13,5},{2,10},{6,14},... | collective-permute-start | bytes 589832 | tf_op jit(solution)/shard_map/ppermute | solution.py:29
  185.6 17.6 %collective-permute-start.22 = (bf16[48,2048]{1,0:T(8,128)(2,1)S(1)}, bf16[48,2048]{1,0:T(8,128)(2,1)S(1)}, u32[]{:S(2)}, u32[]{:S(2)}) collective-permute-start(bf16[48,2048]{1,0:T(8,128)(2,1)S(1)} %add_convert_fusion.11.x0), channel_id=1, source_target_pairs={{0,1},{1,0},{2,3},{3,2},{4,5},{5,4},{6,7},{7,6},{8,9},{9,8},{10,11... | collective-permute-start | bytes 589832 | tf_op jit(solution)/shard_map/ppermute | solution.py:33
  185.6 17.5 %collective-permute-start.23 = (bf16[48,2048]{1,0:T(8,128)(2,1)S(1)}, bf16[48,2048]{1,0:T(8,128)(2,1)S(1)}, u32[]{:S(2)}, u32[]{:S(2)}) collective-permute-start(bf16[48,2048]{1,0:T(8,128)(2,1)S(1)} %add_convert_fusion.11.x0), channel_id=1, source_target_pairs={{0,2},{1,3},{2,0},{3,1},{4,6},{5,7},{6,4},{7,5},{8,10},{9,11},{10,... | collective-permute-start | bytes 589832 | tf_op jit(solution)/shard_map/ppermute | solution.py:33
  187.6 15.6 %collective-permute-start.24 = (bf16[48,2048]{1,0:T(8,128)(2,1)S(1)}, bf16[48,2048]{1,0:T(8,128)(2,1)S(1)}, u32[]{:S(2)}, u32[]{:S(2)}) collective-permute-start(bf16[48,2048]{1,0:T(8,128)(2,1)S(1)} %add_convert_fusion.11.x0), channel_id=1, source_target_pairs={{0,3},{1,2},{2,1},{3,0},{4,7},{5,6},{6,5},{7,4},{8,11},{9,10},{10,... | collective-permute-start | bytes 589832 | tf_op jit(solution)/shard_map/ppermute | solution.py:33
  198.8 24.6 %all-to-all-start.3 = ((bf16[4,48,2048]{2,1,0:T(8,128)(2,1)}), bf16[4,48,2048]{2,1,0:T(8,128)(2,1)}, u32[]{:S(2)}, u32[]{:S(2)}) async-start(bf16[4,48,2048]{2,1,0:T(8,128)(2,1)} %down.5), calls=%async_computation.3 | async-start | bytes 1572864 | tf_op jit(solution)/shard_map/all_to_all | solution.py:37
  210.7 42.4 %collective-permute-start.40 = (bf16[2,96,2048]{2,1,0:T(8,128)(2,1)S(1)}, bf16[2,96,2048]{2,1,0:T(8,128)(2,1)}, u32[]{:S(2)}, u32[]{:S(2)}) collective-permute-start(bf16[2,96,2048]{2,1,0:T(8,128)(2,1)S(1)} %get-tuple-element.98), channel_id=1, source_target_pairs={{0,8},{4,12},{8,0},{12,4},{1,9},{5,13},{9,1},{13,5},{2,10},{6,14},... | collective-permute-start | bytes 2359304 | tf_op jit(solution)/shard_map/ppermute | solution.py:29
  221.5 18.3 %collective-permute-start.33 = (bf16[2,96,2048]{2,1,0:T(8,128)(2,1)}, bf16[2,96,2048]{2,1,0:T(8,128)(2,1)}, u32[]{:S(2)}, u32[]{:S(2)}) collective-permute-start(bf16[2,96,2048]{2,1,0:T(8,128)(2,1)} %get-tuple-element.85), channel_id=1, source_target_pairs={{0,4},{4,0},{8,12},{12,8},{1,5},{5,1},{9,13},{13,9},{2,6},{6,2},{1... | collective-permute-start | bytes 2359304 | tf_op jit(solution)/shard_map/ppermute | solution.py:29
  224.8 16.5 %collective-permute-start.35 = (bf16[48,2048]{1,0:T(8,128)(2,1)S(1)}, bf16[48,2048]{1,0:T(8,128)(2,1)S(1)}, u32[]{:S(2)}, u32[]{:S(2)}) collective-permute-start(bf16[48,2048]{1,0:T(8,128)(2,1)S(1)} %add_convert_fusion.10.x0), channel_id=1, source_target_pairs={{0,1},{1,0},{2,3},{3,2},{4,5},{5,4},{6,7},{7,6},{8,9},{9,8},{10,11... | collective-permute-start | bytes 589832 | tf_op jit(solution)/shard_map/ppermute | solution.py:33
  228.1 15.5 %collective-permute-start.36 = (bf16[48,2048]{1,0:T(8,128)(2,1)S(1)}, bf16[48,2048]{1,0:T(8,128)(2,1)S(1)}, u32[]{:S(2)}, u32[]{:S(2)}) collective-permute-start(bf16[48,2048]{1,0:T(8,128)(2,1)S(1)} %add_convert_fusion.10.x0), channel_id=1, source_target_pairs={{0,2},{1,3},{2,0},{3,1},{4,6},{5,7},{6,4},{7,5},{8,10},{9,11},{10,... | collective-permute-start | bytes 589832 | tf_op jit(solution)/shard_map/ppermute | solution.py:33
  229.0 14.5 %collective-permute-start.37 = (bf16[48,2048]{1,0:T(8,128)(2,1)S(1)}, bf16[48,2048]{1,0:T(8,128)(2,1)S(1)}, u32[]{:S(2)}, u32[]{:S(2)}) collective-permute-start(bf16[48,2048]{1,0:T(8,128)(2,1)S(1)} %add_convert_fusion.10.x0), channel_id=1, source_target_pairs={{0,3},{1,2},{2,1},{3,0},{4,7},{5,6},{6,5},{7,4},{8,11},{9,10},{10,... | collective-permute-start | bytes 589832 | tf_op jit(solution)/shard_map/ppermute | solution.py:33
  240.9 21.4 %collective-permute-start.34 = (bf16[2,48,2048]{2,1,0:T(8,128)(2,1)S(1)}, bf16[2,48,2048]{2,1,0:T(8,128)(2,1)S(1)}, u32[]{:S(2)}, u32[]{:S(2)}) collective-permute-start(bf16[2,48,2048]{2,1,0:T(8,128)(2,1)S(1)} %add_convert_fusion.3), channel_id=1, source_target_pairs={{0,8},{4,12},{8,0},{12,4},{1,9},{5,13},{9,1},{13,5},{2,10},{6,14},... | collective-permute-start | bytes 1179656 | tf_op jit(solution)/shard_map/ppermute | solution.py:29
  244.2 8.4 %collective-permute-start.38 = (f32[2,2,48]{2,1,0:T(2,128)S(1)}, f32[2,2,48]{2,1,0:T(2,128)S(1)}, u32[]{:S(2)}, u32[]{:S(2)}) collective-permute-start(f32[2,2,48]{2,1,0:T(2,128)S(1)} %pad_maximum_fusion.10), channel_id=1, source_target_pairs={{0,4},{4,0},{8,12},{12,8},{1,5},{5,1},{9,13},{13,9},{2,6},{6,2},{1... | collective-permute-start | bytes 2312 | tf_op jit(solution)/shard_map/ppermute | solution.py:29
  252.7 4.5 %collective-permute-start.39 = (f32[2,48]{1,0:T(2,128)S(1)}, f32[2,48]{1,0:T(2,128)S(1)}, u32[]{:S(2)}, u32[]{:S(2)}) collective-permute-start(f32[2,48]{1,0:T(2,128)S(1)} %slice_bitcast_fusion.18), channel_id=1, source_target_pairs={{0,8},{4,12},{8,0},{12,4},{1,9},{5,13},{9,1},{13,5},{2,10},{6,14},... | collective-permute-start | bytes 1160 | tf_op jit(solution)/shard_map/ppermute | solution.py:29
  254.3 8.0 %collective-permute-start.41 = (bf16[2,48,2048]{2,1,0:T(8,128)(2,1)S(1)}, bf16[2,48,2048]{2,1,0:T(8,128)(2,1)S(1)}, u32[]{:S(2)}, u32[]{:S(2)}) collective-permute-start(bf16[2,48,2048]{2,1,0:T(8,128)(2,1)S(1)} %add_convert_fusion.2), channel_id=1, source_target_pairs={{0,4},{4,0},{8,12},{12,8},{1,5},{5,1},{9,13},{13,9},{2,6},{6,2},{1... | collective-permute-start | bytes 1179656 | tf_op jit(solution)/shard_map/ppermute | solution.py:29
  255.5 27.4 %collective-permute-start.49 = (bf16[2,96,2048]{2,1,0:T(8,128)(2,1)S(1)}, bf16[2,96,2048]{2,1,0:T(8,128)(2,1)S(1)}, u32[]{:S(2)}, u32[]{:S(2)}) collective-permute-start(bf16[2,96,2048]{2,1,0:T(8,128)(2,1)S(1)} %get-tuple-element.101), channel_id=1, source_target_pairs={{0,8},{4,12},{8,0},{12,4},{1,9},{5,13},{9,1},{13,5},{2,10},{6,14},... | collective-permute-start | bytes 2359304 | tf_op jit(solution)/shard_map/ppermute | solution.py:29
  264.1 16.2 %collective-permute-start.43 = (bf16[48,4096]{1,0:T(8,128)(2,1)S(1)}, bf16[48,4096]{1,0:T(8,128)(2,1)S(1)}, u32[]{:S(2)}, u32[]{:S(2)}) collective-permute-start(bf16[48,4096]{1,0:T(8,128)(2,1)S(1)} %pad_maximum_fusion.2.x0), channel_id=1, source_target_pairs={{0,8},{4,12},{8,0},{12,4},{1,9},{5,13},{9,1},{13,5},{2,10},{6,14},... | collective-permute-start | bytes 1179656 | tf_op jit(solution)/shard_map/ppermute | solution.py:29
  266.0 16.2 %collective-permute-start.42 = (bf16[48,4096]{1,0:T(8,128)(2,1)S(1)}, bf16[48,4096]{1,0:T(8,128)(2,1)S(1)}, u32[]{:S(2)}, u32[]{:S(2)}) collective-permute-start(bf16[48,4096]{1,0:T(8,128)(2,1)S(1)} %pad_maximum_fusion.2.x0), channel_id=1, source_target_pairs={{0,4},{4,0},{8,12},{12,8},{1,5},{5,1},{9,13},{13,9},{2,6},{6,2},{1... | collective-permute-start | bytes 1179656 | tf_op jit(solution)/shard_map/ppermute | solution.py:29
  275.0 20.5 %collective-permute-start.47 = (bf16[2,96,2048]{2,1,0:T(8,128)(2,1)S(1)}, bf16[2,96,2048]{2,1,0:T(8,128)(2,1)S(1)}, u32[]{:S(2)}, u32[]{:S(2)}) collective-permute-start(bf16[2,96,2048]{2,1,0:T(8,128)(2,1)S(1)} %get-tuple-element.100), channel_id=1, source_target_pairs={{0,4},{4,0},{8,12},{12,8},{1,5},{5,1},{9,13},{13,9},{2,6},{6,2},{1... | collective-permute-start | bytes 2359304 | tf_op jit(solution)/shard_map/ppermute | solution.py:29
  280.3 18.8 %collective-permute-start.44 = (bf16[48,2048]{1,0:T(8,128)(2,1)S(1)}, bf16[48,2048]{1,0:T(8,128)(2,1)S(1)}, u32[]{:S(2)}, u32[]{:S(2)}) collective-permute-start(bf16[48,2048]{1,0:T(8,128)(2,1)S(1)} %slice.282), channel_id=1, source_target_pairs={{0,4},{4,0},{8,12},{12,8},{1,5},{5,1},{9,13},{13,9},{2,6},{6,2},{1... | collective-permute-start | bytes 589832 | tf_op jit(solution)/shard_map/ppermute | solution.py:29
  282.2 16.9 %collective-permute-start.45 = (bf16[48,2048]{1,0:T(8,128)(2,1)S(1)}, bf16[48,2048]{1,0:T(8,128)(2,1)S(1)}, u32[]{:S(2)}, u32[]{:S(2)}) collective-permute-start(bf16[48,2048]{1,0:T(8,128)(2,1)S(1)} %slice.283), channel_id=1, source_target_pairs={{0,8},{4,12},{8,0},{12,4},{1,9},{5,13},{9,1},{13,5},{2,10},{6,14},... | collective-permute-start | bytes 589832 | tf_op jit(solution)/shard_map/ppermute | solution.py:29
  283.9 29.5 %collective-permute-start.50 = (bf16[2,48,2048]{2,1,0:T(8,128)(2,1)}, bf16[2,48,2048]{2,1,0:T(8,128)(2,1)S(1)}, u32[]{:S(2)}, u32[]{:S(2)}) collective-permute-start(bf16[2,48,2048]{2,1,0:T(8,128)(2,1)} %add_convert_fusion), channel_id=1, source_target_pairs={{0,4},{4,0},{8,12},{12,8},{1,5},{5,1},{9,13},{13,9},{2,6},{6,2},{1... | collective-permute-start | bytes 1179656 | tf_op jit(solution)/shard_map/ppermute | solution.py:29
  296.5 16.9 %collective-permute-start.48 = (bf16[2,48,2048]{2,1,0:T(8,128)(2,1)}, bf16[2,48,2048]{2,1,0:T(8,128)(2,1)}, u32[]{:S(2)}, u32[]{:S(2)}) collective-permute-start(bf16[2,48,2048]{2,1,0:T(8,128)(2,1)} %add_convert_fusion.1), channel_id=1, source_target_pairs={{0,8},{4,12},{8,0},{12,4},{1,9},{5,13},{9,1},{13,5},{2,10},{6,14},... | collective-permute-start | bytes 1179656 | tf_op jit(solution)/shard_map/ppermute | solution.py:29
  307.9 31.4 %all-to-all-start.4 = ((bf16[4,48,2048]{2,1,0:T(8,128)(2,1)}), bf16[4,48,2048]{2,1,0:T(8,128)(2,1)S(1)}, u32[]{:S(2)}, u32[]{:S(2)}) async-start(bf16[4,48,2048]{2,1,0:T(8,128)(2,1)} %down.6), calls=%async_computation.4 | async-start | bytes 1572864 | tf_op jit(solution)/shard_map/all_to_all | solution.py:37
  315.6 8.1 %collective-permute-start.52 = (bf16[48,4096]{1,0:T(8,128)(2,1)S(1)}, bf16[48,4096]{1,0:T(8,128)(2,1)S(1)}, u32[]{:S(2)}, u32[]{:S(2)}) collective-permute-start(bf16[48,4096]{1,0:T(8,128)(2,1)S(1)} %pad_maximum_fusion.3.x0), channel_id=1, source_target_pairs={{0,8},{4,12},{8,0},{12,4},{1,9},{5,13},{9,1},{13,5},{2,10},{6,14},... | collective-permute-start | bytes 1179656 | tf_op jit(solution)/shard_map/ppermute | solution.py:29
  316.6 8.1 %collective-permute-start.51 = (bf16[48,4096]{1,0:T(8,128)(2,1)S(1)}, bf16[48,4096]{1,0:T(8,128)(2,1)S(1)}, u32[]{:S(2)}, u32[]{:S(2)}) collective-permute-start(bf16[48,4096]{1,0:T(8,128)(2,1)S(1)} %pad_maximum_fusion.3.x0), channel_id=1, source_target_pairs={{0,4},{4,0},{8,12},{12,8},{1,5},{5,1},{9,13},{13,9},{2,6},{6,2},{1... | collective-permute-start | bytes 1179656 | tf_op jit(solution)/shard_map/ppermute | solution.py:29
  323.7 5.7 %collective-permute-start.53 = (bf16[48,2048]{1,0:T(8,128)(2,1)S(1)}, bf16[48,2048]{1,0:T(8,128)(2,1)S(1)}, u32[]{:S(2)}, u32[]{:S(2)}) collective-permute-start(bf16[48,2048]{1,0:T(8,128)(2,1)S(1)} %slice.292), channel_id=1, source_target_pairs={{0,4},{4,0},{8,12},{12,8},{1,5},{5,1},{9,13},{13,9},{2,6},{6,2},{1... | collective-permute-start | bytes 589832 | tf_op jit(solution)/shard_map/ppermute | solution.py:29
  324.7 5.7 %collective-permute-start.54 = (bf16[48,2048]{1,0:T(8,128)(2,1)S(1)}, bf16[48,2048]{1,0:T(8,128)(2,1)S(1)}, u32[]{:S(2)}, u32[]{:S(2)}) collective-permute-start(bf16[48,2048]{1,0:T(8,128)(2,1)S(1)} %slice.293), channel_id=1, source_target_pairs={{0,8},{4,12},{8,0},{12,4},{1,9},{5,13},{9,1},{13,5},{2,10},{6,14},... | collective-permute-start | bytes 589832 | tf_op jit(solution)/shard_map/ppermute | solution.py:29
  339.4 24.7 %all-to-all-start.5 = ((bf16[4,48,2048]{2,1,0:T(8,128)(2,1)}), bf16[4,48,2048]{2,1,0:T(8,128)(2,1)S(1)}, u32[]{:S(2)}, u32[]{:S(2)}) async-start(bf16[4,48,2048]{2,1,0:T(8,128)(2,1)} %down.7), calls=%async_computation.5 | async-start | bytes 1572864 | tf_op jit(solution)/shard_map/all_to_all | solution.py:37
  344.5 30.7 %copy-start.7 = (f32[96,2048]{1,0:T(8,128)S(1)}, f32[96,2048]{1,0:T(8,128)}, u32[]{:S(2)}) copy-start(f32[96,2048]{1,0:T(8,128)} %convert_element_type.249) | copy-start | bytes 2359300
  344.5 30.7 %copy-start.12 = (f32[2048]{0:T(1024)S(1)}, f32[2048]{0:T(1024)}, u32[]{:S(2)}) copy-start(f32[2048]{0:T(1024)} %param.14) | copy-start | bytes 24580
  344.6 28.3 %collective-permute-start.46 = (bf16[48,2048]{1,0:T(8,128)(2,1)S(1)}, bf16[48,2048]{1,0:T(8,128)(2,1)S(1)}, u32[]{:S(2)}, u32[]{:S(2)}) collective-permute-start(bf16[48,2048]{1,0:T(8,128)(2,1)S(1)} %add_convert_fusion.9), channel_id=1, source_target_pairs={{0,0},{1,4},{2,8},{3,12},{4,1},{5,5},{6,9},{7,13},{8,2},{9,6},{10,... | collective-permute-start | bytes 589832 | tf_op jit(solution)/shard_map/ppermute | solution.py:25
  364.3 10.7 %collective-permute-start.55 = (bf16[48,2048]{1,0:T(8,128)(2,1)S(1)}, bf16[48,2048]{1,0:T(8,128)(2,1)S(1)}, u32[]{:S(2)}, u32[]{:S(2)}) collective-permute-start(bf16[48,2048]{1,0:T(8,128)(2,1)S(1)} %add_convert_fusion.8), channel_id=1, source_target_pairs={{0,0},{1,4},{2,8},{3,12},{4,1},{5,5},{6,9},{7,13},{8,2},{9,6},{10,... | collective-permute-start | bytes 589832 | tf_op jit(solution)/shard_map/ppermute | solution.py:25
  (12 other events, 135.3 us)

commit v3 on v2

--- a/solution.py
+++ b/solution.py
@@ -42,7 +42,7 @@
     pl.when(jnp.logical_not(is_own))(start_other)
 
 
-def gate_up_kernel(number, first, swapped, relative, x0, x1, x2, x3, gain_ref, gate0, up0, gate1, up1, keep_ref, send_ref, rows_ref, held, sems):
+def wide_product_kernel(number, swapped, relative, x0, x1, x2, x3, gain_ref, own, received, keep_ref, send_ref, rows_ref, held, sems):
     step = pl.program_id(0)
     steps = pl.num_programs(0)
     is_own = lax.axis_index("section") == number
@@ -51,14 +51,14 @@
         own_place = own_place ^ lax.axis_index("mp")
     count = x0.shape[0]
 
-    def fetch(j, tile):
-        slot = 2 * lax.rem(tile, 2) + j
-        columns = pl.ds(pl.multiple_of(first + tile * TILE, TILE), TILE)
+    def fetch(j, step):
+        slot = 2 * lax.rem(step, 2) + j
+        columns = pl.ds(pl.multiple_of((2 * step + j) * TILE, TILE), TILE)
 
         def copy(source):
             return lambda: pltpu.make_async_copy(source.at[:, columns], held.at[slot], sems.at[slot]).start()
 
-        either(is_own, copy((gate0, up0)[j]), copy((gate1, up1)[j]))
+        either(is_own, copy(own), copy(received))
 
     @pl.when(step == 0)
     def _():
@@ -78,16 +78,17 @@
             fetch(j, step + 1)
 
         slot = 2 * lax.rem(step, 2) + j
-        pltpu.make_async_copy(gate0.at[:, pl.ds(0, TILE)], held.at[slot], sems.at[slot]).wait()
+        pltpu.make_async_copy(own.at[:, pl.ds(0, TILE)], held.at[slot], sems.at[slot]).wait()
         product = jnp.dot(rows_ref[...], held[slot], preferred_element_type=jnp.float32)
-        keep_ref[j] = product[: 2 * count]
-        send_ref[j] = product[2 * count :].astype(jnp.bfloat16)
-
-
-def gate_up(number, first, width, swapped, rows, gain_row, own, received):
+        keep_ref[:, j * TILE : (j + 1) * TILE] = product[: 2 * count]
+        send_ref[:, j * TILE : (j + 1) * TILE] = product[2 * count :].astype(jnp.bfloat16)
+
+
+def wide_product(number, swapped, rows, gain_row, own, received):
     groups = 4
     relative = isinstance(rows, list)
     count, depth = rows[0].shape
+    width = own.shape[1]
     whole = lambda shape: pl.BlockSpec(shape, lambda t: (0,) * len(shape))
     if relative:
         piece_specs = [whole((count, depth))] * 4
@@ -95,13 +96,13 @@
         piece_specs = [pl.BlockSpec((None, count, depth), lambda t, k=k: (k, 0, 0)) for k in range(4)]
         rows = [rows] * 4
     return pl.pallas_call(
-        functools.partial(gate_up_kernel, number, first, swapped, relative),
-        grid=(width // TILE,),
-        in_specs=piece_specs + [whole((1, depth))] + [pl.BlockSpec(memory_space=pl.ANY)] * 4,
-        out_specs=[pl.BlockSpec((2, 2 * count, TILE), lambda t: (0, 0, t))] * 2,
+        functools.partial(wide_product_kernel, number, swapped, relative),
+        grid=(width // (2 * TILE),),
+        in_specs=piece_specs + [whole((1, depth))] + [pl.BlockSpec(memory_space=pl.ANY)] * 2,
+        out_specs=[pl.BlockSpec((2 * count, 2 * TILE), lambda t: (0, t))] * 2,
         out_shape=[
-            jax.ShapeDtypeStruct((2, 2 * count, width), jnp.float32),
-            jax.ShapeDtypeStruct((2, 2 * count, width), jnp.bfloat16),
+            jax.ShapeDtypeStruct((2 * count, width), jnp.float32),
+            jax.ShapeDtypeStruct((2 * count, width), jnp.bfloat16),
         ],
         scratch_shapes=[
             pltpu.VMEM((groups * count, depth), jnp.bfloat16),
@@ -110,12 +111,10 @@
         ],
         compiler_params=pltpu.CompilerParams(vmem_limit_bytes=VMEM_LIMIT),
         cost_estimate=pl.CostEstimate(
-            flops=4 * groups * count * depth * width // COST,
-            bytes_accessed=4 * depth * width // COST,
-            transcendentals=0,
+            flops=2 * groups * count * depth * width, bytes_accessed=2 * depth * width, transcendentals=0
         ),
-        name="gate_up",
-    )(*rows, gain_row, *own, *received)
+        name="wide_product",
+    )(*rows, gain_row, own, received)
 
 
 def down_kernel(number, x0, x1, x2, x3a, x3b, own, received, out_ref, rows_ref, held, sems):
@@ -203,10 +202,10 @@
 
 def sum_first(partial, step):
     keep, send = partial
-    count = keep.shape[1] // 2
+    count = keep.shape[0] // 2
     got = swap_dp(send, step)
-    onward = (keep[:, count:] + got[:, count:].astype(jnp.float32)).astype(jnp.bfloat16)
-    return keep[:, :count], got[:, :count], onward
+    onward = (keep[count:] + got[count:].astype(jnp.float32)).astype(jnp.bfloat16)
+    return keep[:count], got[:count], onward
 
 
 def sum_second(state, step):
@@ -224,11 +223,8 @@
 
 def activate(states, squares):
     scale = lax.rsqrt(squares / D + EPSILON)[:, None]
-    inner = []
-    for state, step in zip(states, (2, 1)):
-        total = sum_second(state, step) * scale
-        inner.append((jax.nn.silu(total[0]) * total[1]).astype(jnp.bfloat16))
-    return jnp.concatenate(inner, axis=1)
+    gate_rows, up_rows = sum_second(states[0], 2) * scale, sum_second(states[1], 1) * scale
+    return (jax.nn.silu(gate_rows) * up_rows).astype(jnp.bfloat16)
 
 
 def fast_final(hidden_in, layer_gain, gate, up, down, teacher, counts):
@@ -238,16 +234,16 @@
     is_first = lax.axis_index("section") == 0
     gain = lax.dynamic_slice_in_dim(layer_gain[0, 0], lax.axis_index("dp") * features, features, 0)
     other_gain = swap_section(gain)
-    early_gate, early_up = tie((gate, up), other_gain)
-    received = [swap_section(early_gate), swap_section(early_up)]
+    received = [swap_section(tie(gate, other_gain))]
     owns = [transpose_mesh(hidden_in[0, i * count : (i + 1) * count]) for i in range(2)]
+    received.append(swap_section(tie(up, owns[0])))
     targets = fast_targets(*tie((teacher, counts), owns[0]), tokens)
     for number in range(2):
         gain_row = jnp.where(is_first == (number == 0), gain, other_gain)[None, :]
 
         def products(which, pieces):
-            return gate_up(
-                number, which * half, half, which == 0, pieces, gain_row, (gate, up), received[:2]
+            return wide_product(
+                number, which == 0, pieces, gain_row, (gate, up)[which], received[which]
             )
 
         if not number:
@@ -255,7 +251,8 @@
             rows, owns[1], targets, later_down = lax.optimization_barrier((rows, owns[1], targets, down))
             received.append(swap_section(later_down))
             later_rows = enter(owns[1])
-        first, second = products(0, rows), products(1, rows)
+        first = products(0, rows)
+        second = products(1, rows if number else tie(rows, first[0]))
         later_rows = tie(later_rows, second[0])
         states = [sum_first(first, 1), sum_first(second, 2)]
         later_first = products(0, later_rows)

time: 392 us -> 388 us (0.990)
  other arithmetic: 22.8 us -> 18.6 us
    ppermute x36, starting transfers between devices: 33.3 us -> 41.5 us  [swap_dp(): return lax.ppermute(value, 'dp', [(d, d ^ e) for d in range(4)])]
    mul x4 -> x0, other arithmetic: 5.5 us -> none  [activate(): total = sum_second(state, step) * scale]
    convert_element_type x16 -> x12, other arithmetic: 7.16 us -> 8.65 us  [the longest x4 6 us: activate(): return (jax.nn.silu(gate_rows) * up_rows).astype(jnp.bfloat16)]
  transfers between devices with their start and end apart: 62 -> 62, of which waited for: 25 -> 26; matrix products, arithmetic and copies ran while one was open for 6% -> 5% of each run, Pallas kernels for 24% -> 24%
where the time goes in v3:
time: 388 us; the launch traced here: 387 us
  waiting for transfers between devices  153 us (39%)
  starting transfers between devices  100 us (26%)
  Pallas kernels  94.7 us (24%)
  other arithmetic  18.6 us (5%)
  blocking collectives  11.9 us (3%)
  local copies, waits for them, and re-layouts  5.57 us (1%)
    ppermute x36, waiting for transfers between devices, swap_dp(): return lax.ppermute(value, 'dp', [(d, d ^ e) for d in range(4)])  88.8 us
    pallas_call x8, Pallas kernels, wide_product(): pl.pallas_call(functools.partial(wide_product_kernel, number, swapped, re...  59.6 us
    ppermute x36, starting transfers between devices, swap_dp(): return lax.ppermute(value, 'dp', [(d, d ^ e) for d in range(4)])  41.5 us
    pallas_call x4, Pallas kernels, down_terms(): pl.pallas_call(functools.partial(down_kernel, number), grid=(features //...  35.1 us
    ppermute x4, waiting for transfers between devices, transpose_mesh(): return lax.ppermute(value, ('dp', 'mp'), pairs)  30.8 us
    all_to_all x4, waiting for transfers between devices, exchange(): return lax.all_to_all(value, axis, split_axis=0, concat_axis=0, tiled=True)  20.4 us
    all_to_all x4, starting transfers between devices, exchange(): return lax.all_to_all(value, axis, split_axis=0, concat_axis=0, tiled=True)  19.9 us
    ppermute x12, starting transfers between devices, swap_mp(): return lax.ppermute(value, 'mp', [(m, m ^ k) for m in range(4)])  19.4 us
  transfers between devices with their start and end apart: 62, of which 26 were waited for; matrix products, arithmetic and copies ran while one was open for 5% of the time, Pallas kernels for 24%

profile of v3, /device:TPU:2, one launch (start us, length us, event | category | flops | bytes accessed | tf_op | source)
XLA Modules:
  0.0 387.1 jit_solution(7971901708951763827)
XLA Ops:
  3.8 3.5 collective-permute-start
  7.3 14.9 %collective-permute-done.x0 = bf16[48,2048]{1,0:T(8,128)(2,1)S(1)} collective-permute-done((bf16[48,2048]{1,0:T(8,128)(2,1)S(1)}, bf16[48,2048]{1,0:T(8,128)(2,1)S(1)}, u32[]{:S(2)}, u32[]{:S(2)}) %collective-permute-start) | collective-permute-done | bytes 196640 | tf_op jit(solution)/shard_map/ppermute | solution.py:25
  22.2 1.9 collective-permute-start.4
  25.4 3.3 all-to-all-start.1
  28.7 3.4 collective-permute-start.1
  32.1 1.7 collective-permute-start.2
  33.8 4.2 %all-to-all-start = ((bf16[4,48,2048]{2,1,0:T(8,128)(2,1)}), bf16[4,48,2048]{2,1,0:T(8,128)(2,1)S(1)}, u32[]{:S(2)}, u32[]{:S(2)}) async-start(bf16[4,48,2048]{2,1,0:T(8,128)(2,1)} %bitcast.134), calls=%async_computation | async-start | bytes 1572864 | tf_op jit(solution)/shard_map/all_to_all | solution.py:282
  38.5 3.7 collective-permute-done.4.x0
  42.2 5.6 %all-to-all-done = bf16[4,48,2048]{2,1,0:T(8,128)(2,1)S(1)} async-done(((bf16[4,48,2048]{2,1,0:T(8,128)(2,1)}), bf16[4,48,2048]{2,1,0:T(8,128)(2,1)S(1)}, u32[]{:S(2)}, u32[]{:S(2)}) %all-to-all-start) | async-done | bytes 786464 | tf_op jit(solution)/shard_map/all_to_all | solution.py:282
  50.9 3.3 collective-permute-start.10
  55.8 7.5 %wide_product.8 = (f32[96,4096]{1,0:T(8,128)S(1)}, bf16[96,4096]{1,0:T(8,128)(2,1)S(1)}) custom-call(bf16[48,2048]{1,0:T(8,128)(2,1)S(1)} %collective-permute-done.x0, bf16[48,2048]{1,0:T(8,128)(2,1)S(1)} %collective-permute-done.1.x1, bf16[48,2048]{1,0:T(8,128)(2,1)S(1)} %collective-permute-done.2.x2, bf16[48,2048]{1,0:T(8,128)(2,1)S(1)} %collective-permute-done.3.x3, ...), custom_call_target="tpu_custom_call" | custom-call | flops 3221225472 | bytes 16777216 | tf_op jit(solution)/shard_map/wide_product/pallas_call | solution.py:98
  63.7 7.4 %wide_product.9 = (f32[96,4096]{1,0:T(8,128)S(1)}, bf16[96,4096]{1,0:T(8,128)(2,1)S(1)}) custom-call(bf16[48,2048]{1,0:T(8,128)(2,1)S(1)} %collective-permute-done.x0, bf16[48,2048]{1,0:T(8,128)(2,1)S(1)} %collective-permute-done.1.x1, bf16[48,2048]{1,0:T(8,128)(2,1)S(1)} %collective-permute-done.2.x2, bf16[48,2048]{1,0:T(8,128)(2,1)S(1)} %collective-permute-done.3.x3, ...), custom_call_target="tpu_custom_call" | custom-call | flops 3221225472 | bytes 16777216 | tf_op jit(solution)/shard_map/wide_product/pallas_call | solution.py:98
  71.1 2.6 collective-permute-start.15
  74.9 7.4 %wide_product.11 = (f32[96,4096]{1,0:T(8,128)S(1)}, bf16[96,4096]{1,0:T(8,128)(2,1)S(1)}) custom-call(bf16[48,2048]{1,0:T(8,128)(2,1)S(1)} %collective-permute-done.4.x0, bf16[48,2048]{1,0:T(8,128)(2,1)S(1)} %collective-permute-done.9.x1, bf16[48,2048]{1,0:T(8,128)(2,1)S(1)} %collective-permute-done.10.x2, bf16[48,2048]{1,0:T(8,128)(2,1)S(1)} %collective-permute-done.11.x3, ...), custom_call_target="tpu_custom_call" | custom-call | flops 3221225472 | bytes 16777216 | tf_op jit(solution)/shard_map/wide_product/pallas_call | solution.py:98
  82.4 1.4 collective-permute-start.25
  84.4 7.4 %wide_product.10 = (f32[96,4096]{1,0:T(8,128)S(1)}, bf16[96,4096]{1,0:T(8,128)(2,1)S(1)}) custom-call(bf16[48,2048]{1,0:T(8,128)(2,1)S(1)} %collective-permute-done.4.x0, bf16[48,2048]{1,0:T(8,128)(2,1)S(1)} %collective-permute-done.9.x1, bf16[48,2048]{1,0:T(8,128)(2,1)S(1)} %collective-permute-done.10.x2, bf16[48,2048]{1,0:T(8,128)(2,1)S(1)} %collective-permute-done.11.x3, ...), custom_call_target="tpu_custom_call" | custom-call | flops 3221225472 | bytes 16777216 | tf_op jit(solution)/shard_map/wide_product/pallas_call | solution.py:98
  91.9 1.7 collective-permute-start.14
  94.3 6.4 %collective-permute-done.14 = f32[2,48]{1,0:T(2,128)S(1)} collective-permute-done((f32[2,48]{1,0:T(2,128)S(1)}, f32[2,48]{1,0:T(2,128)S(1)}, u32[]{:S(2)}, u32[]{:S(2)}) %collective-permute-start.14) | collective-permute-done | bytes 416 | tf_op jit(solution)/shard_map/ppermute | solution.py:29
  101.9 7.7 %collective-permute-done.16 = bf16[48,4096]{1,0:T(8,128)(2,1)S(1)} collective-permute-done((bf16[48,4096]{1,0:T(8,128)(2,1)S(1)}, bf16[48,4096]{1,0:T(8,128)(2,1)S(1)}, u32[]{:S(2)}, u32[]{:S(2)}) %collective-permute-start.16) | collective-permute-done | bytes 393248 | tf_op jit(solution)/shard_map/ppermute | solution.py:29
  110.0 1.5 collective-permute-start.18
  113.4 12.4 %collective-permute-done.18.x2 = bf16[48,4096]{1,0:T(8,128)(2,1)S(1)} collective-permute-done((bf16[48,4096]{1,0:T(8,128)(2,1)S(1)}, bf16[48,4096]{1,0:T(8,128)(2,1)S(1)}, u32[]{:S(2)}, u32[]{:S(2)}) %collective-permute-start.18) | collective-permute-done | bytes 393248 | tf_op jit(solution)/shard_map/ppermute | solution.py:29
  127.2 1.5 collective-permute-start.20
  130.3 3.5 collective-permute-done.19.x3a
  133.8 3.6 collective-permute-done.20.x3b
  137.4 8.8 %down.4 = bf16[4,48,2048]{2,1,0:T(8,128)(2,1)} custom-call(bf16[48,4096]{1,0:T(8,128)(2,1)S(1)} %multiply_convert_fusion.3.x0, bf16[48,4096]{1,0:T(8,128)(2,1)S(1)} %collective-permute-done.17.x1, bf16[48,4096]{1,0:T(8,128)(2,1)S(1)} %collective-permute-done.18.x2, bf16[48,2048]{1,0:T(8,128)(2,1)S(1)} %collective-permute-done.19.x3a, ...), custom_call_target="tpu_custom_call" | custom-call | flops 3221225472 | bytes 16777216 | tf_op jit(solution)/shard_map/down/pallas_call | solution.py:161
  146.2 4.2 %all-to-all-start.2 = ((bf16[4,48,2048]{2,1,0:T(8,128)(2,1)}), bf16[4,48,2048]{2,1,0:T(8,128)(2,1)}, u32[]{:S(2)}, u32[]{:S(2)}) async-start(bf16[4,48,2048]{2,1,0:T(8,128)(2,1)} %down.4), calls=%async_computation.2 | async-start | bytes 1572864 | tf_op jit(solution)/shard_map/all_to_all | solution.py:37
  150.4 1.9 multiply_convert_fusion.2.x0
  152.4 1.8 collective-permute-start.30
  154.9 7.7 %collective-permute-done.30.x2 = bf16[48,4096]{1,0:T(8,128)(2,1)S(1)} collective-permute-done((bf16[48,4096]{1,0:T(8,128)(2,1)S(1)}, bf16[48,4096]{1,0:T(8,128)(2,1)S(1)}, u32[]{:S(2)}, u32[]{:S(2)}) %collective-permute-start.30) | collective-permute-done | bytes 393248 | tf_op jit(solution)/shard_map/ppermute | solution.py:29
  164.9 5.3 %all-to-all-done.2 = bf16[4,48,2048]{2,1,0:T(8,128)(2,1)} async-done(((bf16[4,48,2048]{2,1,0:T(8,128)(2,1)}), bf16[4,48,2048]{2,1,0:T(8,128)(2,1)}, u32[]{:S(2)}, u32[]{:S(2)}) %all-to-all-start.2) | async-done | bytes 786464 | tf_op jit(solution)/shard_map/all_to_all | solution.py:37
  171.6 2.0 collective-permute-start.23
  173.6 2.4 collective-permute-start.24
  176.0 8.8 %down.5 = bf16[4,48,2048]{2,1,0:T(8,128)(2,1)} custom-call(bf16[48,4096]{1,0:T(8,128)(2,1)S(1)} %multiply_convert_fusion.2.x0, bf16[48,4096]{1,0:T(8,128)(2,1)S(1)} %collective-permute-done.29.x1, bf16[48,4096]{1,0:T(8,128)(2,1)S(1)} %collective-permute-done.30.x2, bf16[48,2048]{1,0:T(8,128)(2,1)S(1)} %collective-permute-done.31.x3a, ...), custom_call_target="tpu_custom_call" | custom-call | flops 3221225472 | bytes 16777216 | tf_op jit(solution)/shard_map/down/pallas_call | solution.py:161
  184.7 4.4 %all-to-all-start.3 = ((bf16[4,48,2048]{2,1,0:T(8,128)(2,1)}), bf16[4,48,2048]{2,1,0:T(8,128)(2,1)}, u32[]{:S(2)}, u32[]{:S(2)}) async-start(bf16[4,48,2048]{2,1,0:T(8,128)(2,1)} %down.5), calls=%async_computation.3 | async-start | bytes 1572864 | tf_op jit(solution)/shard_map/all_to_all | solution.py:37
  189.3 7.5 %wide_product.13 = (f32[96,4096]{1,0:T(8,128)S(1)}, bf16[96,4096]{1,0:T(8,128)(2,1)S(1)}) custom-call(bf16[48,2048]{1,0:T(8,128)(2,1)S(1)} %add_convert_fusion.11.x0, bf16[48,2048]{1,0:T(8,128)(2,1)S(1)} %collective-permute-done.22.x1, bf16[48,2048]{1,0:T(8,128)(2,1)S(1)} %collective-permute-done.23.x2, bf16[48,2048]{1,0:T(8,128)(2,1)S(1)} %collective-permute-done.24.x3, ...), custom_call_target="tpu_custom_call" | custom-call | flops 3221225472 | bytes 16777216 | tf_op jit(solution)/shard_map/wide_product/pallas_call | solution.py:98
  196.8 1.5 collective-permute-start.40
  198.6 7.5 %wide_product.12 = (f32[96,4096]{1,0:T(8,128)S(1)}, bf16[96,4096]{1,0:T(8,128)(2,1)S(1)}) custom-call(bf16[48,2048]{1,0:T(8,128)(2,1)S(1)} %add_convert_fusion.11.x0, bf16[48,2048]{1,0:T(8,128)(2,1)S(1)} %collective-permute-done.22.x1, bf16[48,2048]{1,0:T(8,128)(2,1)S(1)} %collective-permute-done.23.x2, bf16[48,2048]{1,0:T(8,128)(2,1)S(1)} %collective-permute-done.24.x3, ...), custom_call_target="tpu_custom_call" | custom-call | flops 3221225472 | bytes 16777216 | tf_op jit(solution)/shard_map/wide_product/pallas_call | solution.py:98
  208.1 6.4 %collective-permute-done.40 = bf16[96,4096]{1,0:T(8,128)(2,1)S(1)} collective-permute-done((bf16[96,4096]{1,0:T(8,128)(2,1)S(1)}, bf16[96,4096]{1,0:T(8,128)(2,1)S(1)}, u32[]{:S(2)}, u32[]{:S(2)}) %collective-permute-start.40) | collective-permute-done | bytes 786464 | tf_op jit(solution)/shard_map/ppermute | solution.py:29
  217.5 2.9 collective-permute-start.35
  221.5 1.5 collective-permute-start.37
  222.9 5.1 %collective-permute-done.33 = bf16[96,4096]{1,0:T(8,128)(2,1)} collective-permute-done((bf16[96,4096]{1,0:T(8,128)(2,1)S(1)}, bf16[96,4096]{1,0:T(8,128)(2,1)}, u32[]{:S(2)}, u32[]{:S(2)}) %collective-permute-start.33) | collective-permute-done | bytes 786464 | tf_op jit(solution)/shard_map/ppermute | solution.py:29
  229.9 4.7 %collective-permute-done.36.x2 = bf16[48,2048]{1,0:T(8,128)(2,1)S(1)} collective-permute-done((bf16[48,2048]{1,0:T(8,128)(2,1)S(1)}, bf16[48,2048]{1,0:T(8,128)(2,1)S(1)}, u32[]{:S(2)}, u32[]{:S(2)}) %collective-permute-start.36) | collective-permute-done | bytes 196640 | tf_op jit(solution)/shard_map/ppermute | solution.py:33
  235.3 1.5 collective-permute-start.38
  236.8 7.4 %wide_product.14 = (f32[96,4096]{1,0:T(8,128)S(1)}, bf16[96,4096]{1,0:T(8,128)(2,1)S(1)}) custom-call(bf16[48,2048]{1,0:T(8,128)(2,1)S(1)} %add_convert_fusion.10.x0, bf16[48,2048]{1,0:T(8,128)(2,1)S(1)} %collective-permute-done.35.x1, bf16[48,2048]{1,0:T(8,128)(2,1)S(1)} %collective-permute-done.36.x2, bf16[48,2048]{1,0:T(8,128)(2,1)S(1)} %collective-permute-done.37.x3, ...), custom_call_target="tpu_custom_call" | custom-call | flops 3221225472 | bytes 16777216 | tf_op jit(solution)/shard_map/wide_product/pallas_call | solution.py:98
  244.4 1.5 collective-permute-start.39
  245.8 7.4 %wide_product.15 = (f32[96,4096]{1,0:T(8,128)S(1)}, bf16[96,4096]{1,0:T(8,128)(2,1)S(1)}) custom-call(bf16[48,2048]{1,0:T(8,128)(2,1)S(1)} %add_convert_fusion.10.x0, bf16[48,2048]{1,0:T(8,128)(2,1)S(1)} %collective-permute-done.35.x1, bf16[48,2048]{1,0:T(8,128)(2,1)S(1)} %collective-permute-done.36.x2, bf16[48,2048]{1,0:T(8,128)(2,1)S(1)} %collective-permute-done.37.x3, ...), custom_call_target="tpu_custom_call" | custom-call | flops 3221225472 | bytes 16777216 | tf_op jit(solution)/shard_map/wide_product/pallas_call | solution.py:98
  254.3 1.6 multiply_convert_fusion.1.x0
  259.1 8.8 %collective-permute-done.43.x2 = bf16[48,4096]{1,0:T(8,128)(2,1)S(1)} collective-permute-done((bf16[48,4096]{1,0:T(8,128)(2,1)S(1)}, bf16[48,4096]{1,0:T(8,128)(2,1)S(1)}, u32[]{:S(2)}, u32[]{:S(2)}) %collective-permute-start.43) | collective-permute-done | bytes 393248 | tf_op jit(solution)/shard_map/ppermute | solution.py:29
  269.2 11.7 %collective-permute-done.42.x1 = bf16[48,4096]{1,0:T(8,128)(2,1)S(1)} collective-permute-done((bf16[48,4096]{1,0:T(8,128)(2,1)S(1)}, bf16[48,4096]{1,0:T(8,128)(2,1)S(1)}, u32[]{:S(2)}, u32[]{:S(2)}) %collective-permute-start.42) | collective-permute-done | bytes 393248 | tf_op jit(solution)/shard_map/ppermute | solution.py:29
  284.7 1.8 collective-permute-start.50
  286.5 2.3 collective-permute-done.45.x3b
  288.8 8.8 %down.6 = bf16[4,48,2048]{2,1,0:T(8,128)(2,1)} custom-call(bf16[48,4096]{1,0:T(8,128)(2,1)S(1)} %multiply_convert_fusion.1.x0, bf16[48,4096]{1,0:T(8,128)(2,1)S(1)} %collective-permute-done.42.x1, bf16[48,4096]{1,0:T(8,128)(2,1)S(1)} %collective-permute-done.43.x2, bf16[48,2048]{1,0:T(8,128)(2,1)S(1)} %collective-permute-done.44.x3a, ...), custom_call_target="tpu_custom_call" | custom-call | flops 3221225472 | bytes 16777216 | tf_op jit(solution)/shard_map/down/pallas_call | solution.py:161
  297.6 6.2 %all-to-all-start.4 = ((bf16[4,48,2048]{2,1,0:T(8,128)(2,1)}), bf16[4,48,2048]{2,1,0:T(8,128)(2,1)S(1)}, u32[]{:S(2)}, u32[]{:S(2)}) async-start(bf16[4,48,2048]{2,1,0:T(8,128)(2,1)} %down.6), calls=%async_computation.4 | async-start | bytes 1572864 | tf_op jit(solution)/shard_map/all_to_all | solution.py:37
  303.8 2.0 multiply_convert_fusion.x0
  308.0 7.7 %collective-permute-done.52.x2 = bf16[48,4096]{1,0:T(8,128)(2,1)S(1)} collective-permute-done((bf16[48,4096]{1,0:T(8,128)(2,1)S(1)}, bf16[48,4096]{1,0:T(8,128)(2,1)S(1)}, u32[]{:S(2)}, u32[]{:S(2)}) %collective-permute-start.52) | collective-permute-done | bytes 393248 | tf_op jit(solution)/shard_map/ppermute | solution.py:29
  318.1 3.5 collective-permute-done.53.x3a
  322.4 8.8 %down.7 = bf16[4,48,2048]{2,1,0:T(8,128)(2,1)} custom-call(bf16[48,4096]{1,0:T(8,128)(2,1)S(1)} %multiply_convert_fusion.x0, bf16[48,4096]{1,0:T(8,128)(2,1)S(1)} %collective-permute-done.51.x1, bf16[48,4096]{1,0:T(8,128)(2,1)S(1)} %collective-permute-done.52.x2, bf16[48,2048]{1,0:T(8,128)(2,1)S(1)} %collective-permute-done.53.x3a, ...), custom_call_target="tpu_custom_call" | custom-call | flops 3221225472 | bytes 16777216 | tf_op jit(solution)/shard_map/down/pallas_call | solution.py:161
  331.4 5.1 %all-to-all-start.5 = ((bf16[4,48,2048]{2,1,0:T(8,128)(2,1)}), bf16[4,48,2048]{2,1,0:T(8,128)(2,1)S(1)}, u32[]{:S(2)}, u32[]{:S(2)}) async-start(bf16[4,48,2048]{2,1,0:T(8,128)(2,1)} %down.7), calls=%async_computation.5 | async-start | bytes 1572864 | tf_op jit(solution)/shard_map/all_to_all | solution.py:37
  336.6 4.7 %collective-permute-start.46 = (bf16[48,2048]{1,0:T(8,128)(2,1)S(1)}, bf16[48,2048]{1,0:T(8,128)(2,1)S(1)}, u32[]{:S(2)}, u32[]{:S(2)}) collective-permute-start(bf16[48,2048]{1,0:T(8,128)(2,1)S(1)} %add_convert_fusion.9), channel_id=1, source_target_pairs={{0,0},{1,4},{2,8},{3,12},{4,1},{5,5},{6,9},{7,13},{8,2},{9,6},{10,... | collective-permute-start | bytes 589832 | tf_op jit(solution)/shard_map/ppermute | solution.py:25
  341.4 15.1 %all-to-all-done.5 = bf16[4,48,2048]{2,1,0:T(8,128)(2,1)S(1)} async-done(((bf16[4,48,2048]{2,1,0:T(8,128)(2,1)}), bf16[4,48,2048]{2,1,0:T(8,128)(2,1)S(1)}, u32[]{:S(2)}, u32[]{:S(2)}) %all-to-all-start.5) | async-done | bytes 786464 | tf_op jit(solution)/shard_map/all_to_all | solution.py:37
  356.7 1.9 collective-permute-start.55
  358.7 8.7 %collective-permute-done.46 = bf16[48,2048]{1,0:T(8,128)(2,1)S(1)} collective-permute-done((bf16[48,2048]{1,0:T(8,128)(2,1)S(1)}, bf16[48,2048]{1,0:T(8,128)(2,1)S(1)}, u32[]{:S(2)}, u32[]{:S(2)}) %collective-permute-start.46) | collective-permute-done | bytes 196640 | tf_op jit(solution)/shard_map/ppermute | solution.py:25
  367.4 3.5 collective-permute-done.55
  371.5 11.9 %all-gather.1 = f32[4,4,96]{2,1,0:T(4,128)S(1)} all-gather(f32[1,4,96]{2,1,0:T(4,128)S(1)} %maximum_bitcast_fusion), channel_id=2, replica_groups=mesh['section'=2,'dp'=4,'mp'=4] {'mp'}, dimensions={0}, use_global_device_ids=true | all-gather | bytes 7680 | tf_op jit(solution)/shard_map/all_gather | solution.py:335
  (198 shorter events, 50.3 us)
Async XLA Ops:
  1.4 1.2 collective-permute-start.5
  2.6 53.2 %collective-permute-start.6 = (bf16[2048,4096]{1,0:T(8,128)(2,1)}, bf16[2048,4096]{1,0:T(8,128)(2,1)}, u32[]{:S(2)}, u32[]{:S(2)}) collective-permute-start(bf16[2048,4096]{1,0:T(8,128)(2,1)} %bitcast.123), channel_id=1, source_target_pairs={{0,16},{16,0},{1,17},{17,1},{2,18},{18,2},{3,19},{19,3},{4,20},{20... | collective-permute-start | bytes 50331656 | tf_op jit(solution)/shard_map/ppermute | solution.py:20
  3.8 18.4 %collective-permute-start = (bf16[48,2048]{1,0:T(8,128)(2,1)S(1)}, bf16[48,2048]{1,0:T(8,128)(2,1)S(1)}, u32[]{:S(2)}, u32[]{:S(2)}) collective-permute-start(bf16[48,2048]{1,0:T(8,128)(2,1)S(1)} %get-tuple-element.118), channel_id=1, source_target_pairs={{0,0},{1,4},{2,8},{3,12},{4,1},{5,5},{6,9},{7,13},{8,2},{9,6},{10,... | collective-permute-start | bytes 589832 | tf_op jit(solution)/shard_map/ppermute | solution.py:25
  22.2 41.2 %collective-permute-start.12 = (bf16[2048,4096]{1,0:T(8,128)(2,1)}, bf16[2048,4096]{1,0:T(8,128)(2,1)}, u32[]{:S(2)}, u32[]{:S(2)}) collective-permute-start(bf16[2048,4096]{1,0:T(8,128)(2,1)} %bitcast.118), channel_id=1, source_target_pairs={{0,16},{16,0},{1,17},{17,1},{2,18},{18,2},{3,19},{19,3},{4,20},{20... | collective-permute-start | bytes 50331656 | tf_op jit(solution)/shard_map/ppermute | solution.py:20
  22.2 20.0 %collective-permute-start.4 = (bf16[48,2048]{1,0:T(8,128)(2,1)S(1)}, bf16[48,2048]{1,0:T(8,128)(2,1)S(1)}, u32[]{:S(2)}, u32[]{:S(2)}) collective-permute-start(bf16[48,2048]{1,0:T(8,128)(2,1)S(1)} %get-tuple-element.117), channel_id=1, source_target_pairs={{0,0},{1,4},{2,8},{3,12},{4,1},{5,5},{6,9},{7,13},{8,2},{9,6},{10,... | collective-permute-start | bytes 589832 | tf_op jit(solution)/shard_map/ppermute | solution.py:25
  25.4 8.4 %all-to-all-start.1 = ((bf16[4,1,1]{2,1,0:T(2,128)(2,1)}), bf16[4,1,1]{2,1,0:T(2,128)(2,1)S(1)}, u32[]{:S(2)}, u32[]{:S(2)}) async-start(bf16[4,1,1]{2,1,0:T(2,128)(2,1)} %copy.22), calls=%async_computation.1 | async-start | bytes 4096 | tf_op jit(solution)/shard_map/all_to_all | solution.py:285
  28.7 20.8 %collective-permute-start.1 = (bf16[48,2048]{1,0:T(8,128)(2,1)S(1)}, bf16[48,2048]{1,0:T(8,128)(2,1)S(1)}, u32[]{:S(2)}, u32[]{:S(2)}) collective-permute-start(bf16[48,2048]{1,0:T(8,128)(2,1)S(1)} %collective-permute-done.x0), channel_id=1, source_target_pairs={{0,1},{1,0},{2,3},{3,2},{4,5},{5,4},{6,7},{7,6},{8,9},{9,8},{10,11... | collective-permute-start | bytes 589832 | tf_op jit(solution)/shard_map/ppermute | solution.py:33
  32.1 17.5 %collective-permute-start.2 = (bf16[48,2048]{1,0:T(8,128)(2,1)S(1)}, bf16[48,2048]{1,0:T(8,128)(2,1)S(1)}, u32[]{:S(2)}, u32[]{:S(2)}) collective-permute-start(bf16[48,2048]{1,0:T(8,128)(2,1)S(1)} %collective-permute-done.x0), channel_id=1, source_target_pairs={{0,2},{1,3},{2,0},{3,1},{4,6},{5,7},{6,4},{7,5},{8,10},{9,11},{10,... | collective-permute-start | bytes 589832 | tf_op jit(solution)/shard_map/ppermute | solution.py:33
  33.8 14.0 %all-to-all-start = ((bf16[4,48,2048]{2,1,0:T(8,128)(2,1)}), bf16[4,48,2048]{2,1,0:T(8,128)(2,1)S(1)}, u32[]{:S(2)}, u32[]{:S(2)}) async-start(bf16[4,48,2048]{2,1,0:T(8,128)(2,1)} %bitcast.134), calls=%async_computation | async-start | bytes 1572864 | tf_op jit(solution)/shard_map/all_to_all | solution.py:282
  42.2 8.7 %collective-permute-start.3 = (bf16[48,2048]{1,0:T(8,128)(2,1)S(1)}, bf16[48,2048]{1,0:T(8,128)(2,1)S(1)}, u32[]{:S(2)}, u32[]{:S(2)}) collective-permute-start(bf16[48,2048]{1,0:T(8,128)(2,1)S(1)} %collective-permute-done.x0), channel_id=1, source_target_pairs={{0,3},{1,2},{2,1},{3,0},{4,7},{5,6},{6,5},{7,4},{8,11},{9,10},{10,... | collective-permute-start | bytes 589832 | tf_op jit(solution)/shard_map/ppermute | solution.py:33
  50.9 79.4 %collective-permute-start.21 = (bf16[4096,2048]{1,0:T(8,128)(2,1)}, bf16[4096,2048]{1,0:T(8,128)(2,1)}, u32[]{:S(2)}, u32[]{:S(2)}) collective-permute-start(bf16[4096,2048]{1,0:T(8,128)(2,1)} %bitcast.128), channel_id=1, source_target_pairs={{0,16},{16,0},{1,17},{17,1},{2,18},{18,2},{3,19},{19,3},{4,20},{20... | collective-permute-start | bytes 50331656 | tf_op jit(solution)/shard_map/ppermute | solution.py:20
  50.9 20.2 %collective-permute-start.10 = (bf16[48,2048]{1,0:T(8,128)(2,1)S(1)}, bf16[48,2048]{1,0:T(8,128)(2,1)S(1)}, u32[]{:S(2)}, u32[]{:S(2)}) collective-permute-start(bf16[48,2048]{1,0:T(8,128)(2,1)S(1)} %collective-permute-done.4.x0), channel_id=1, source_target_pairs={{0,2},{1,3},{2,0},{3,1},{4,6},{5,7},{6,4},{7,5},{8,10},{9,11},{10,... | collective-permute-start | bytes 589832 | tf_op jit(solution)/shard_map/ppermute | solution.py:33
  54.2 19.5 %collective-permute-start.11 = (bf16[48,2048]{1,0:T(8,128)(2,1)S(1)}, bf16[48,2048]{1,0:T(8,128)(2,1)S(1)}, u32[]{:S(2)}, u32[]{:S(2)}) collective-permute-start(bf16[48,2048]{1,0:T(8,128)(2,1)S(1)} %collective-permute-done.4.x0), channel_id=1, source_target_pairs={{0,3},{1,2},{2,1},{3,0},{4,7},{5,6},{6,5},{7,4},{8,11},{9,10},{10,... | collective-permute-start | bytes 589832 | tf_op jit(solution)/shard_map/ppermute | solution.py:33
  55.8 18.0 %collective-permute-start.9 = (bf16[48,2048]{1,0:T(8,128)(2,1)S(1)}, bf16[48,2048]{1,0:T(8,128)(2,1)S(1)}, u32[]{:S(2)}, u32[]{:S(2)}) collective-permute-start(bf16[48,2048]{1,0:T(8,128)(2,1)S(1)} %collective-permute-done.4.x0), channel_id=1, source_target_pairs={{0,1},{1,0},{2,3},{3,2},{4,5},{5,4},{6,7},{7,6},{8,9},{9,8},{10,11... | collective-permute-start | bytes 589832 | tf_op jit(solution)/shard_map/ppermute | solution.py:33
  63.3 20.5 %collective-permute-start.7 = (bf16[96,4096]{1,0:T(8,128)(2,1)S(1)}, bf16[96,4096]{1,0:T(8,128)(2,1)S(1)}, u32[]{:S(2)}, u32[]{:S(2)}) collective-permute-start(bf16[96,4096]{1,0:T(8,128)(2,1)S(1)} %get-tuple-element.65), channel_id=1, source_target_pairs={{0,4},{4,0},{8,12},{12,8},{1,5},{5,1},{9,13},{13,9},{2,6},{6,2},{1... | collective-permute-start | bytes 2359304 | tf_op jit(solution)/shard_map/ppermute | solution.py:29
  71.1 22.4 %collective-permute-start.15 = (bf16[96,4096]{1,0:T(8,128)(2,1)S(1)}, bf16[96,4096]{1,0:T(8,128)(2,1)S(1)}, u32[]{:S(2)}, u32[]{:S(2)}) collective-permute-start(bf16[96,4096]{1,0:T(8,128)(2,1)S(1)} %get-tuple-element.83), channel_id=1, source_target_pairs={{0,8},{4,12},{8,0},{12,4},{1,9},{5,13},{9,1},{13,5},{2,10},{6,14},... | collective-permute-start | bytes 2359304 | tf_op jit(solution)/shard_map/ppermute | solution.py:29
  74.2 17.6 %collective-permute-start.13 = (f32[2,2,48]{2,1,0:T(2,128)S(1)}, f32[2,2,48]{2,1,0:T(2,128)S(1)}, u32[]{:S(2)}, u32[]{:S(2)}) collective-permute-start(f32[2,2,48]{2,1,0:T(2,128)S(1)} %pad_maximum_fusion.3), channel_id=1, source_target_pairs={{0,4},{4,0},{8,12},{12,8},{1,5},{5,1},{9,13},{13,9},{2,6},{6,2},{1... | collective-permute-start | bytes 2312 | tf_op jit(solution)/shard_map/ppermute | solution.py:29
  82.4 29.8 %collective-permute-start.25 = (bf16[96,4096]{1,0:T(8,128)(2,1)S(1)}, bf16[96,4096]{1,0:T(8,128)(2,1)S(1)}, u32[]{:S(2)}, u32[]{:S(2)}) collective-permute-start(bf16[96,4096]{1,0:T(8,128)(2,1)S(1)} %get-tuple-element.86), channel_id=1, source_target_pairs={{0,4},{4,0},{8,12},{12,8},{1,5},{5,1},{9,13},{13,9},{2,6},{6,2},{1... | collective-permute-start | bytes 2359304 | tf_op jit(solution)/shard_map/ppermute | solution.py:29
  83.9 18.0 %collective-permute-start.8 = (bf16[48,4096]{1,0:T(8,128)(2,1)S(1)}, bf16[48,4096]{1,0:T(8,128)(2,1)S(1)}, u32[]{:S(2)}, u32[]{:S(2)}) collective-permute-start(bf16[48,4096]{1,0:T(8,128)(2,1)S(1)} %add_convert_fusion.7), channel_id=1, source_target_pairs={{0,8},{4,12},{8,0},{12,4},{1,9},{5,13},{9,1},{13,5},{2,10},{6,14},... | collective-permute-start | bytes 1179656 | tf_op jit(solution)/shard_map/ppermute | solution.py:29
  91.8 36.9 %copy-start.4 = (f32[96,4096]{1,0:T(8,128)}, f32[96,4096]{1,0:T(8,128)S(1)}, u32[]{:S(2)}) copy-start(f32[96,4096]{1,0:T(8,128)S(1)} %get-tuple-element.81) | copy-start | bytes 4718596
  91.9 8.8 %collective-permute-start.14 = (f32[2,48]{1,0:T(2,128)S(1)}, f32[2,48]{1,0:T(2,128)S(1)}, u32[]{:S(2)}, u32[]{:S(2)}) collective-permute-start(f32[2,48]{1,0:T(2,128)S(1)} %slice_bitcast_fusion.4), channel_id=1, source_target_pairs={{0,8},{4,12},{8,0},{12,4},{1,9},{5,13},{9,1},{13,5},{2,10},{6,14},... | collective-permute-start | bytes 1160 | tf_op jit(solution)/shard_map/ppermute | solution.py:29
  93.6 35.2 %collective-permute-start.27 = (bf16[96,4096]{1,0:T(8,128)(2,1)S(1)}, bf16[96,4096]{1,0:T(8,128)(2,1)S(1)}, u32[]{:S(2)}, u32[]{:S(2)}) collective-permute-start(bf16[96,4096]{1,0:T(8,128)(2,1)S(1)} %get-tuple-element.87), channel_id=1, source_target_pairs={{0,8},{4,12},{8,0},{12,4},{1,9},{5,13},{9,1},{13,5},{2,10},{6,14},... | collective-permute-start | bytes 2359304 | tf_op jit(solution)/shard_map/ppermute | solution.py:29
  100.6 8.9 %collective-permute-start.16 = (bf16[48,4096]{1,0:T(8,128)(2,1)S(1)}, bf16[48,4096]{1,0:T(8,128)(2,1)S(1)}, u32[]{:S(2)}, u32[]{:S(2)}) collective-permute-start(bf16[48,4096]{1,0:T(8,128)(2,1)S(1)} %add_convert_fusion.6), channel_id=1, source_target_pairs={{0,4},{4,0},{8,12},{12,8},{1,5},{5,1},{9,13},{13,9},{2,6},{6,2},{1... | collective-permute-start | bytes 1179656 | tf_op jit(solution)/shard_map/ppermute | solution.py:29
  110.0 15.8 %collective-permute-start.18 = (bf16[48,4096]{1,0:T(8,128)(2,1)S(1)}, bf16[48,4096]{1,0:T(8,128)(2,1)S(1)}, u32[]{:S(2)}, u32[]{:S(2)}) collective-permute-start(bf16[48,4096]{1,0:T(8,128)(2,1)S(1)} %multiply_convert_fusion.3.x0), channel_id=1, source_target_pairs={{0,8},{4,12},{8,0},{12,4},{1,9},{5,13},{9,1},{13,5},{2,10},{6,14},... | collective-permute-start | bytes 1179656 | tf_op jit(solution)/shard_map/ppermute | solution.py:29
  111.5 15.7 %collective-permute-start.17 = (bf16[48,4096]{1,0:T(8,128)(2,1)S(1)}, bf16[48,4096]{1,0:T(8,128)(2,1)S(1)}, u32[]{:S(2)}, u32[]{:S(2)}) collective-permute-start(bf16[48,4096]{1,0:T(8,128)(2,1)S(1)} %multiply_convert_fusion.3.x0), channel_id=1, source_target_pairs={{0,4},{4,0},{8,12},{12,8},{1,5},{5,1},{9,13},{13,9},{2,6},{6,2},{1... | collective-permute-start | bytes 1179656 | tf_op jit(solution)/shard_map/ppermute | solution.py:29
  112.3 38.1 %collective-permute-start.26 = (bf16[48,4096]{1,0:T(8,128)(2,1)S(1)}, bf16[48,4096]{1,0:T(8,128)(2,1)}, u32[]{:S(2)}, u32[]{:S(2)}) collective-permute-start(bf16[48,4096]{1,0:T(8,128)(2,1)S(1)} %add_convert_fusion.5), channel_id=1, source_target_pairs={{0,8},{4,12},{8,0},{12,4},{1,9},{5,13},{9,1},{13,5},{2,10},{6,14},... | collective-permute-start | bytes 1179656 | tf_op jit(solution)/shard_map/ppermute | solution.py:29
  125.9 7.9 %collective-permute-start.19 = (bf16[48,2048]{1,0:T(8,128)(2,1)S(1)}, bf16[48,2048]{1,0:T(8,128)(2,1)S(1)}, u32[]{:S(2)}, u32[]{:S(2)}) collective-permute-start(bf16[48,2048]{1,0:T(8,128)(2,1)S(1)} %slice.192), channel_id=1, source_target_pairs={{0,4},{4,0},{8,12},{12,8},{1,5},{5,1},{9,13},{13,9},{2,6},{6,2},{1... | collective-permute-start | bytes 589832 | tf_op jit(solution)/shard_map/ppermute | solution.py:29
  127.2 10.2 %collective-permute-start.20 = (bf16[48,2048]{1,0:T(8,128)(2,1)S(1)}, bf16[48,2048]{1,0:T(8,128)(2,1)S(1)}, u32[]{:S(2)}, u32[]{:S(2)}) collective-permute-start(bf16[48,2048]{1,0:T(8,128)(2,1)S(1)} %slice.193), channel_id=1, source_target_pairs={{0,8},{4,12},{8,0},{12,4},{1,9},{5,13},{9,1},{13,5},{2,10},{6,14},... | collective-permute-start | bytes 589832 | tf_op jit(solution)/shard_map/ppermute | solution.py:29
  128.8 21.6 %collective-permute-start.28 = (bf16[48,4096]{1,0:T(8,128)(2,1)S(1)}, bf16[48,4096]{1,0:T(8,128)(2,1)}, u32[]{:S(2)}, u32[]{:S(2)}) collective-permute-start(bf16[48,4096]{1,0:T(8,128)(2,1)S(1)} %add_convert_fusion.4), channel_id=1, source_target_pairs={{0,4},{4,0},{8,12},{12,8},{1,5},{5,1},{9,13},{13,9},{2,6},{6,2},{1... | collective-permute-start | bytes 1179656 | tf_op jit(solution)/shard_map/ppermute | solution.py:29
  146.2 24.0 %all-to-all-start.2 = ((bf16[4,48,2048]{2,1,0:T(8,128)(2,1)}), bf16[4,48,2048]{2,1,0:T(8,128)(2,1)}, u32[]{:S(2)}, u32[]{:S(2)}) async-start(bf16[4,48,2048]{2,1,0:T(8,128)(2,1)} %down.4), calls=%async_computation.2 | async-start | bytes 1572864 | tf_op jit(solution)/shard_map/all_to_all | solution.py:37
  152.4 10.3 %collective-permute-start.30 = (bf16[48,4096]{1,0:T(8,128)(2,1)S(1)}, bf16[48,4096]{1,0:T(8,128)(2,1)S(1)}, u32[]{:S(2)}, u32[]{:S(2)}) collective-permute-start(bf16[48,4096]{1,0:T(8,128)(2,1)S(1)} %multiply_convert_fusion.2.x0), channel_id=1, source_target_pairs={{0,8},{4,12},{8,0},{12,4},{1,9},{5,13},{9,1},{13,5},{2,10},{6,14},... | collective-permute-start | bytes 1179656 | tf_op jit(solution)/shard_map/ppermute | solution.py:29
  154.2 9.6 %collective-permute-start.29 = (bf16[48,4096]{1,0:T(8,128)(2,1)S(1)}, bf16[48,4096]{1,0:T(8,128)(2,1)S(1)}, u32[]{:S(2)}, u32[]{:S(2)}) collective-permute-start(bf16[48,4096]{1,0:T(8,128)(2,1)S(1)} %multiply_convert_fusion.2.x0), channel_id=1, source_target_pairs={{0,4},{4,0},{8,12},{12,8},{1,5},{5,1},{9,13},{13,9},{2,6},{6,2},{1... | collective-permute-start | bytes 1179656 | tf_op jit(solution)/shard_map/ppermute | solution.py:29
  162.6 13.4 %collective-permute-start.31 = (bf16[48,2048]{1,0:T(8,128)(2,1)S(1)}, bf16[48,2048]{1,0:T(8,128)(2,1)S(1)}, u32[]{:S(2)}, u32[]{:S(2)}) collective-permute-start(bf16[48,2048]{1,0:T(8,128)(2,1)S(1)} %slice.198), channel_id=1, source_target_pairs={{0,4},{4,0},{8,12},{12,8},{1,5},{5,1},{9,13},{13,9},{2,6},{6,2},{1... | collective-permute-start | bytes 589832 | tf_op jit(solution)/shard_map/ppermute | solution.py:29
  163.8 12.2 %collective-permute-start.32 = (bf16[48,2048]{1,0:T(8,128)(2,1)S(1)}, bf16[48,2048]{1,0:T(8,128)(2,1)S(1)}, u32[]{:S(2)}, u32[]{:S(2)}) collective-permute-start(bf16[48,2048]{1,0:T(8,128)(2,1)S(1)} %slice.199), channel_id=1, source_target_pairs={{0,8},{4,12},{8,0},{12,4},{1,9},{5,13},{9,1},{13,5},{2,10},{6,14},... | collective-permute-start | bytes 589832 | tf_op jit(solution)/shard_map/ppermute | solution.py:29
  171.5 17.6 %collective-permute-start.22 = (bf16[48,2048]{1,0:T(8,128)(2,1)S(1)}, bf16[48,2048]{1,0:T(8,128)(2,1)S(1)}, u32[]{:S(2)}, u32[]{:S(2)}) collective-permute-start(bf16[48,2048]{1,0:T(8,128)(2,1)S(1)} %add_convert_fusion.11.x0), channel_id=1, source_target_pairs={{0,1},{1,0},{2,3},{3,2},{4,5},{5,4},{6,7},{7,6},{8,9},{9,8},{10,11... | collective-permute-start | bytes 589832 | tf_op jit(solution)/shard_map/ppermute | solution.py:33
  171.6 17.5 %collective-permute-start.23 = (bf16[48,2048]{1,0:T(8,128)(2,1)S(1)}, bf16[48,2048]{1,0:T(8,128)(2,1)S(1)}, u32[]{:S(2)}, u32[]{:S(2)}) collective-permute-start(bf16[48,2048]{1,0:T(8,128)(2,1)S(1)} %add_convert_fusion.11.x0), channel_id=1, source_target_pairs={{0,2},{1,3},{2,0},{3,1},{4,6},{5,7},{6,4},{7,5},{8,10},{9,11},{10,... | collective-permute-start | bytes 589832 | tf_op jit(solution)/shard_map/ppermute | solution.py:33
  173.6 15.5 %collective-permute-start.24 = (bf16[48,2048]{1,0:T(8,128)(2,1)S(1)}, bf16[48,2048]{1,0:T(8,128)(2,1)S(1)}, u32[]{:S(2)}, u32[]{:S(2)}) collective-permute-start(bf16[48,2048]{1,0:T(8,128)(2,1)S(1)} %add_convert_fusion.11.x0), channel_id=1, source_target_pairs={{0,3},{1,2},{2,1},{3,0},{4,7},{5,6},{6,5},{7,4},{8,11},{9,10},{10,... | collective-permute-start | bytes 589832 | tf_op jit(solution)/shard_map/ppermute | solution.py:33
  184.7 31.5 %all-to-all-start.3 = ((bf16[4,48,2048]{2,1,0:T(8,128)(2,1)}), bf16[4,48,2048]{2,1,0:T(8,128)(2,1)}, u32[]{:S(2)}, u32[]{:S(2)}) async-start(bf16[4,48,2048]{2,1,0:T(8,128)(2,1)} %down.5), calls=%async_computation.3 | async-start | bytes 1572864 | tf_op jit(solution)/shard_map/all_to_all | solution.py:37
  196.8 17.7 %collective-permute-start.40 = (bf16[96,4096]{1,0:T(8,128)(2,1)S(1)}, bf16[96,4096]{1,0:T(8,128)(2,1)S(1)}, u32[]{:S(2)}, u32[]{:S(2)}) collective-permute-start(bf16[96,4096]{1,0:T(8,128)(2,1)S(1)} %get-tuple-element.106), channel_id=1, source_target_pairs={{0,8},{4,12},{8,0},{12,4},{1,9},{5,13},{9,1},{13,5},{2,10},{6,14},... | collective-permute-start | bytes 2359304 | tf_op jit(solution)/shard_map/ppermute | solution.py:29
  207.3 20.6 %collective-permute-start.33 = (bf16[96,4096]{1,0:T(8,128)(2,1)S(1)}, bf16[96,4096]{1,0:T(8,128)(2,1)}, u32[]{:S(2)}, u32[]{:S(2)}) collective-permute-start(bf16[96,4096]{1,0:T(8,128)(2,1)S(1)} %get-tuple-element.93), channel_id=1, source_target_pairs={{0,4},{4,0},{8,12},{12,8},{1,5},{5,1},{9,13},{13,9},{2,6},{6,2},{1... | collective-permute-start | bytes 2359304 | tf_op jit(solution)/shard_map/ppermute | solution.py:29
  215.5 38.7 %collective-permute-start.41 = (bf16[48,4096]{1,0:T(8,128)(2,1)S(1)}, bf16[48,4096]{1,0:T(8,128)(2,1)}, u32[]{:S(2)}, u32[]{:S(2)}) collective-permute-start(bf16[48,4096]{1,0:T(8,128)(2,1)S(1)} %add_convert_fusion.2), channel_id=1, source_target_pairs={{0,4},{4,0},{8,12},{12,8},{1,5},{5,1},{9,13},{13,9},{2,6},{6,2},{1... | collective-permute-start | bytes 1179656 | tf_op jit(solution)/shard_map/ppermute | solution.py:29
  217.5 12.4 %collective-permute-start.35 = (bf16[48,2048]{1,0:T(8,128)(2,1)S(1)}, bf16[48,2048]{1,0:T(8,128)(2,1)S(1)}, u32[]{:S(2)}, u32[]{:S(2)}) collective-permute-start(bf16[48,2048]{1,0:T(8,128)(2,1)S(1)} %add_convert_fusion.10.x0), channel_id=1, source_target_pairs={{0,1},{1,0},{2,3},{3,2},{4,5},{5,4},{6,7},{7,6},{8,9},{9,8},{10,11... | collective-permute-start | bytes 589832 | tf_op jit(solution)/shard_map/ppermute | solution.py:33
  220.5 14.2 %collective-permute-start.36 = (bf16[48,2048]{1,0:T(8,128)(2,1)S(1)}, bf16[48,2048]{1,0:T(8,128)(2,1)S(1)}, u32[]{:S(2)}, u32[]{:S(2)}) collective-permute-start(bf16[48,2048]{1,0:T(8,128)(2,1)S(1)} %add_convert_fusion.10.x0), channel_id=1, source_target_pairs={{0,2},{1,3},{2,0},{3,1},{4,6},{5,7},{6,4},{7,5},{8,10},{9,11},{10,... | collective-permute-start | bytes 589832 | tf_op jit(solution)/shard_map/ppermute | solution.py:33
  221.5 13.2 %collective-permute-start.37 = (bf16[48,2048]{1,0:T(8,128)(2,1)S(1)}, bf16[48,2048]{1,0:T(8,128)(2,1)S(1)}, u32[]{:S(2)}, u32[]{:S(2)}) collective-permute-start(bf16[48,2048]{1,0:T(8,128)(2,1)S(1)} %add_convert_fusion.10.x0), channel_id=1, source_target_pairs={{0,3},{1,2},{2,1},{3,0},{4,7},{5,6},{6,5},{7,4},{8,11},{9,10},{10,... | collective-permute-start | bytes 589832 | tf_op jit(solution)/shard_map/ppermute | solution.py:33
  229.3 25.0 %collective-permute-start.34 = (bf16[48,4096]{1,0:T(8,128)(2,1)S(1)}, bf16[48,4096]{1,0:T(8,128)(2,1)S(1)}, u32[]{:S(2)}, u32[]{:S(2)}) collective-permute-start(bf16[48,4096]{1,0:T(8,128)(2,1)S(1)} %add_convert_fusion.3), channel_id=1, source_target_pairs={{0,8},{4,12},{8,0},{12,4},{1,9},{5,13},{9,1},{13,5},{2,10},{6,14},... | collective-permute-start | bytes 1179656 | tf_op jit(solution)/shard_map/ppermute | solution.py:29
  235.3 9.0 %collective-permute-start.38 = (f32[2,2,48]{2,1,0:T(2,128)S(1)}, f32[2,2,48]{2,1,0:T(2,128)S(1)}, u32[]{:S(2)}, u32[]{:S(2)}) collective-permute-start(f32[2,2,48]{2,1,0:T(2,128)S(1)} %pad_maximum_fusion.6), channel_id=1, source_target_pairs={{0,4},{4,0},{8,12},{12,8},{1,5},{5,1},{9,13},{13,9},{2,6},{6,2},{1... | collective-permute-start | bytes 2312 | tf_op jit(solution)/shard_map/ppermute | solution.py:29
  244.3 39.5 %copy-start.5 = (f32[96,4096]{1,0:T(8,128)}, f32[96,4096]{1,0:T(8,128)S(1)}, u32[]{:S(2)}) copy-start(f32[96,4096]{1,0:T(8,128)S(1)} %get-tuple-element.104) | copy-start | bytes 4718596
  244.4 9.8 %collective-permute-start.39 = (f32[2,48]{1,0:T(2,128)S(1)}, f32[2,48]{1,0:T(2,128)S(1)}, u32[]{:S(2)}, u32[]{:S(2)}) collective-permute-start(f32[2,48]{1,0:T(2,128)S(1)} %slice_bitcast_fusion.2), channel_id=1, source_target_pairs={{0,8},{4,12},{8,0},{12,4},{1,9},{5,13},{9,1},{13,5},{2,10},{6,14},... | collective-permute-start | bytes 1160 | tf_op jit(solution)/shard_map/ppermute | solution.py:29
  253.3 29.0 %collective-permute-start.47 = (bf16[96,4096]{1,0:T(8,128)(2,1)S(1)}, bf16[96,4096]{1,0:T(8,128)(2,1)S(1)}, u32[]{:S(2)}, u32[]{:S(2)}) collective-permute-start(bf16[96,4096]{1,0:T(8,128)(2,1)S(1)} %get-tuple-element.108), channel_id=1, source_target_pairs={{0,4},{4,0},{8,12},{12,8},{1,5},{5,1},{9,13},{13,9},{2,6},{6,2},{1... | collective-permute-start | bytes 2359304 | tf_op jit(solution)/shard_map/ppermute | solution.py:29
  255.8 12.1 %collective-permute-start.43 = (bf16[48,4096]{1,0:T(8,128)(2,1)S(1)}, bf16[48,4096]{1,0:T(8,128)(2,1)S(1)}, u32[]{:S(2)}, u32[]{:S(2)}) collective-permute-start(bf16[48,4096]{1,0:T(8,128)(2,1)S(1)} %multiply_convert_fusion.1.x0), channel_id=1, source_target_pairs={{0,8},{4,12},{8,0},{12,4},{1,9},{5,13},{9,1},{13,5},{2,10},{6,14},... | collective-permute-start | bytes 1179656 | tf_op jit(solution)/shard_map/ppermute | solution.py:29
  257.0 23.9 %collective-permute-start.42 = (bf16[48,4096]{1,0:T(8,128)(2,1)S(1)}, bf16[48,4096]{1,0:T(8,128)(2,1)S(1)}, u32[]{:S(2)}, u32[]{:S(2)}) collective-permute-start(bf16[48,4096]{1,0:T(8,128)(2,1)S(1)} %multiply_convert_fusion.1.x0), channel_id=1, source_target_pairs={{0,4},{4,0},{8,12},{12,8},{1,5},{5,1},{9,13},{13,9},{2,6},{6,2},{1... | collective-permute-start | bytes 1179656 | tf_op jit(solution)/shard_map/ppermute | solution.py:29
  258.2 25.6 %collective-permute-start.49 = (bf16[96,4096]{1,0:T(8,128)(2,1)S(1)}, bf16[96,4096]{1,0:T(8,128)(2,1)S(1)}, u32[]{:S(2)}, u32[]{:S(2)}) collective-permute-start(bf16[96,4096]{1,0:T(8,128)(2,1)S(1)} %get-tuple-element.109), channel_id=1, source_target_pairs={{0,8},{4,12},{8,0},{12,4},{1,9},{5,13},{9,1},{13,5},{2,10},{6,14},... | collective-permute-start | bytes 2359304 | tf_op jit(solution)/shard_map/ppermute | solution.py:29
  268.0 18.5 %collective-permute-start.44 = (bf16[48,2048]{1,0:T(8,128)(2,1)S(1)}, bf16[48,2048]{1,0:T(8,128)(2,1)S(1)}, u32[]{:S(2)}, u32[]{:S(2)}) collective-permute-start(bf16[48,2048]{1,0:T(8,128)(2,1)S(1)} %slice.206), channel_id=1, source_target_pairs={{0,4},{4,0},{8,12},{12,8},{1,5},{5,1},{9,13},{13,9},{2,6},{6,2},{1... | collective-permute-start | bytes 589832 | tf_op jit(solution)/shard_map/ppermute | solution.py:29
  280.9 7.9 %collective-permute-start.45 = (bf16[48,2048]{1,0:T(8,128)(2,1)S(1)}, bf16[48,2048]{1,0:T(8,128)(2,1)S(1)}, u32[]{:S(2)}, u32[]{:S(2)}) collective-permute-start(bf16[48,2048]{1,0:T(8,128)(2,1)S(1)} %slice.207), channel_id=1, source_target_pairs={{0,8},{4,12},{8,0},{12,4},{1,9},{5,13},{9,1},{13,5},{2,10},{6,14},... | collective-permute-start | bytes 589832 | tf_op jit(solution)/shard_map/ppermute | solution.py:29
  282.4 21.4 %collective-permute-start.48 = (bf16[48,4096]{1,0:T(8,128)(2,1)S(1)}, bf16[48,4096]{1,0:T(8,128)(2,1)}, u32[]{:S(2)}, u32[]{:S(2)}) collective-permute-start(bf16[48,4096]{1,0:T(8,128)(2,1)S(1)} %add_convert_fusion.1), channel_id=1, source_target_pairs={{0,8},{4,12},{8,0},{12,4},{1,9},{5,13},{9,1},{13,5},{2,10},{6,14},... | collective-permute-start | bytes 1179656 | tf_op jit(solution)/shard_map/ppermute | solution.py:29
  284.7 19.1 %collective-permute-start.50 = (bf16[48,4096]{1,0:T(8,128)(2,1)}, bf16[48,4096]{1,0:T(8,128)(2,1)}, u32[]{:S(2)}, u32[]{:S(2)}) collective-permute-start(bf16[48,4096]{1,0:T(8,128)(2,1)} %add_convert_fusion), channel_id=1, source_target_pairs={{0,4},{4,0},{8,12},{12,8},{1,5},{5,1},{9,13},{13,9},{2,6},{6,2},{1... | collective-permute-start | bytes 1179656 | tf_op jit(solution)/shard_map/ppermute | solution.py:29
  297.6 33.6 %all-to-all-start.4 = ((bf16[4,48,2048]{2,1,0:T(8,128)(2,1)}), bf16[4,48,2048]{2,1,0:T(8,128)(2,1)S(1)}, u32[]{:S(2)}, u32[]{:S(2)}) async-start(bf16[4,48,2048]{2,1,0:T(8,128)(2,1)} %down.6), calls=%async_computation.4 | async-start | bytes 1572864 | tf_op jit(solution)/shard_map/all_to_all | solution.py:37
  305.8 9.9 %collective-permute-start.52 = (bf16[48,4096]{1,0:T(8,128)(2,1)S(1)}, bf16[48,4096]{1,0:T(8,128)(2,1)S(1)}, u32[]{:S(2)}, u32[]{:S(2)}) collective-permute-start(bf16[48,4096]{1,0:T(8,128)(2,1)S(1)} %multiply_convert_fusion.x0), channel_id=1, source_target_pairs={{0,8},{4,12},{8,0},{12,4},{1,9},{5,13},{9,1},{13,5},{2,10},{6,14},... | collective-permute-start | bytes 1179656 | tf_op jit(solution)/shard_map/ppermute | solution.py:29
  307.3 9.4 %collective-permute-start.51 = (bf16[48,4096]{1,0:T(8,128)(2,1)S(1)}, bf16[48,4096]{1,0:T(8,128)(2,1)S(1)}, u32[]{:S(2)}, u32[]{:S(2)}) collective-permute-start(bf16[48,4096]{1,0:T(8,128)(2,1)S(1)} %multiply_convert_fusion.x0), channel_id=1, source_target_pairs={{0,4},{4,0},{8,12},{12,8},{1,5},{5,1},{9,13},{13,9},{2,6},{6,2},{1... | collective-permute-start | bytes 1179656 | tf_op jit(solution)/shard_map/ppermute | solution.py:29
  315.8 5.7 %collective-permute-start.53 = (bf16[48,2048]{1,0:T(8,128)(2,1)S(1)}, bf16[48,2048]{1,0:T(8,128)(2,1)S(1)}, u32[]{:S(2)}, u32[]{:S(2)}) collective-permute-start(bf16[48,2048]{1,0:T(8,128)(2,1)S(1)} %slice.212), channel_id=1, source_target_pairs={{0,4},{4,0},{8,12},{12,8},{1,5},{5,1},{9,13},{13,9},{2,6},{6,2},{1... | collective-permute-start | bytes 589832 | tf_op jit(solution)/shard_map/ppermute | solution.py:29
  316.7 5.7 %collective-permute-start.54 = (bf16[48,2048]{1,0:T(8,128)(2,1)S(1)}, bf16[48,2048]{1,0:T(8,128)(2,1)S(1)}, u32[]{:S(2)}, u32[]{:S(2)}) collective-permute-start(bf16[48,2048]{1,0:T(8,128)(2,1)S(1)} %slice.213), channel_id=1, source_target_pairs={{0,8},{4,12},{8,0},{12,4},{1,9},{5,13},{9,1},{13,5},{2,10},{6,14},... | collective-permute-start | bytes 589832 | tf_op jit(solution)/shard_map/ppermute | solution.py:29
  331.4 25.1 %all-to-all-start.5 = ((bf16[4,48,2048]{2,1,0:T(8,128)(2,1)}), bf16[4,48,2048]{2,1,0:T(8,128)(2,1)S(1)}, u32[]{:S(2)}, u32[]{:S(2)}) async-start(bf16[4,48,2048]{2,1,0:T(8,128)(2,1)} %down.7), calls=%async_computation.5 | async-start | bytes 1572864 | tf_op jit(solution)/shard_map/all_to_all | solution.py:37
  336.6 30.7 %collective-permute-start.46 = (bf16[48,2048]{1,0:T(8,128)(2,1)S(1)}, bf16[48,2048]{1,0:T(8,128)(2,1)S(1)}, u32[]{:S(2)}, u32[]{:S(2)}) collective-permute-start(bf16[48,2048]{1,0:T(8,128)(2,1)S(1)} %add_convert_fusion.9), channel_id=1, source_target_pairs={{0,0},{1,4},{2,8},{3,12},{4,1},{5,5},{6,9},{7,13},{8,2},{9,6},{10,... | collective-permute-start | bytes 589832 | tf_op jit(solution)/shard_map/ppermute | solution.py:25
  356.7 14.2 %collective-permute-start.55 = (bf16[48,2048]{1,0:T(8,128)(2,1)S(1)}, bf16[48,2048]{1,0:T(8,128)(2,1)S(1)}, u32[]{:S(2)}, u32[]{:S(2)}) collective-permute-start(bf16[48,2048]{1,0:T(8,128)(2,1)S(1)} %add_convert_fusion.8), channel_id=1, source_target_pairs={{0,0},{1,4},{2,8},{3,12},{4,1},{5,5},{6,9},{7,13},{8,2},{9,6},{10,... | collective-permute-start | bytes 589832 | tf_op jit(solution)/shard_map/ppermute | solution.py:25
  (14 other events, 163.3 us)
